TPU v7x, 32 devices: a whole 2x2x4 slice. The times are simulated.
32 devices in a mesh: groups: 2 (over y), dev: 8 (over z, x), pair: 2 (over core).
Axes of the slice: x: 2, y: 2, z: 4, core: 2. Of those that a mesh axis runs over, the one named last changes fastest.
Arguments:
- query: bfloat16 [512, 64, 128], P(('groups', 'dev', 'pair')), parts along dimension 0, may hold values from -10 to 10
- stored_keys: bfloat16 [512, 256, 4, 128], P(('groups', 'dev', 'pair')), parts along dimension 0, may hold values from -30 to 30
- stored_values: bfloat16 [512, 256, 4, 128], P(('groups', 'dev', 'pair')), parts along dimension 0, may hold values from -6 to 6
- incoming_key: bfloat16 [512, 4, 128], P(('groups', 'dev', 'pair')), parts along dimension 0, may hold values from -6 to 6
- incoming_value: bfloat16 [512, 4, 128], P(('groups', 'dev', 'pair')), parts along dimension 0, may hold values from -6 to 6
- lengths: int32 [512], P(('groups', 'dev', 'pair')), parts along dimension 0, may hold values from 2 to 256, as said below
- out_weight: bfloat16 [8192, 2048], P('dev', 'pair'), may hold values from -0.25 to 0.25
- residual: bfloat16 [512, 2048], P(('groups', 'dev'), 'pair'), parts along dimension 0, may hold values from -6 to 6
- norm_gain: float32 [2048], P('pair'), may hold values from 0.1 to 1.9
- expert_ids: int32 [512, 8], P(('groups', 'dev')), parts along dimension 0, may hold values from 0 to 15, all different within a row; in each aligned block of 32 rows (0 to 31, 32 to 63, ...) at most 24 rows name the same one
- route_weights: float32 [512, 8], P(('groups', 'dev')), parts along dimension 0, may hold values from 0.05 to 1
- w_gate: bfloat16 [16, 2048, 768], P('dev', 'pair'), may hold values from -0.125 to 0.125
- w_up: bfloat16 [16, 2048, 768], P('dev', 'pair'), may hold values from -0.125 to 0.125
- w_down: bfloat16 [16, 768, 2048], P('dev', None, 'pair'), may hold values from -0.4375 to 0.4375
Outputs:
- layer_out: bfloat16 [512, 2048], P(('groups', 'dev'), 'pair'), parts along dimension 0
There are 2 independent parts, one for each index of `groups`. A program takes and returns all parts, laid end to end along the dimension named above; an argument that names none is the same for every part. Nothing has to cross between parts.
Inputs may be any that keep to these rules, and one draw needn't show every extreme that they name: `lengths`: every draw has a row with exactly 256 valid positions. `expert_ids`: each row names 8 different experts; among the rows of one index of dev no expert is named by more than 24 rows.
All inputs are finite; a program needn't handle non-finite values.
Results may differ from a plain program's by a relative error of at most 0.0085.
Values may be sent and summed in bfloat16 or wider, within the bound.
No kernel may reach another device: no remote copies, remote signals or barrier semaphores. Data moves between devices by JAX's collectives and lax.ppermute only.
A program may use at most 128 MiB of HBM per device.

v0:
```python
import jax
import jax.numpy as jnp
from jax import lax
from jax.sharding import PartitionSpec as P


def per_device(
    query,
    stored_keys,
    stored_values,
    incoming_key,
    incoming_value,
    lengths,
    out_weight,
    residual,
    norm_gain,
    expert_ids,
    route_weights,
    w_gate,
    w_up,
    w_down,
):
    high = lax.Precision.HIGHEST
    local_rows, heads, head_size = query.shape
    positions = stored_keys.shape[1]
    kv_heads = stored_keys.shape[2]
    grouped_queries = query.reshape(local_rows, kv_heads, heads // kv_heads, head_size)
    factor = head_size ** (-0.5)
    scores = (
        jnp.einsum(
            "bgjd,btgd->bgjt", grouped_queries, stored_keys, preferred_element_type=jnp.float32
        )
        * factor
    )
    places = jnp.arange(positions, dtype=jnp.int32)
    valid = (places[None, :] < lengths[:, None])[:, None, None, :]
    masked = jnp.where(valid, scores, -1e30)
    own = (
        jnp.einsum(
            "bgjd,bgd->bgj", grouped_queries, incoming_key, preferred_element_type=jnp.float32
        )
        * factor
    )
    peak = jnp.maximum(jnp.max(masked, axis=3), own)
    expo = jnp.where(valid, jnp.exp(masked - peak[..., None]), 0.0)
    fresh = jnp.exp(own - peak)
    total = jnp.sum(expo, axis=3) + fresh
    accum = jnp.einsum("bgjt,btgd->bgjd", expo, stored_values.astype(jnp.float32), precision=high)
    accum = accum + fresh[..., None] * incoming_value.astype(jnp.float32)[:, :, None, :]
    local_attended = (
        (accum / total[..., None]).reshape(local_rows, heads * head_size).astype(jnp.bfloat16)
    )
    attended = lax.all_gather(local_attended, "pair", axis=0, tiled=True)
    rows = attended.shape[0]
    regrouped = lax.all_to_all(attended, "dev", split_axis=1, concat_axis=0, tiled=True)
    projected = lax.psum_scatter(
        jnp.dot(regrouped, out_weight, preferred_element_type=jnp.float32),
        "dev",
        scatter_dimension=0,
        tiled=True,
    )
    mixed = residual.astype(jnp.float32) + projected
    squares = lax.psum(jnp.sum(mixed * mixed, axis=1), "pair")
    full_width = mixed.shape[1] * lax.axis_size("pair")
    normed = (mixed * lax.rsqrt(squares / full_width + 1e-06)[:, None] * norm_gain[None, :]).astype(
        jnp.bfloat16
    )
    local_experts = w_gate.shape[0]
    count_dev = lax.axis_size("dev")
    experts_all = local_experts * count_dev
    picks = expert_ids.shape[1]
    capacity = min(rows, max(2, rows * picks * 3 // (2 * experts_all)))
    slots_all = experts_all * capacity
    flat_ids = expert_ids.reshape(-1)
    onehot = (flat_ids[:, None] == jnp.arange(experts_all, dtype=jnp.int32)[None, :]).astype(
        jnp.int32
    )
    rank = jnp.sum((jnp.cumsum(onehot, axis=0) - onehot) * onehot, axis=1)
    slot = flat_ids * capacity + rank
    placing = (slot[None, :] == jnp.arange(slots_all, dtype=jnp.int32)[:, None]).astype(
        jnp.bfloat16
    )
    placing = jnp.sum(placing.reshape(slots_all, rows, picks), axis=2)
    outgoing = jnp.dot(placing, normed, preferred_element_type=jnp.float32).astype(jnp.bfloat16)
    outgoing = outgoing.reshape(count_dev, local_experts, capacity, normed.shape[1])
    arrived = lax.all_to_all(outgoing, "dev", split_axis=0, concat_axis=0, tiled=True)
    gate = jnp.einsum("sacd,adf->sacf", arrived, w_gate, preferred_element_type=jnp.float32)
    up = jnp.einsum("sacd,adf->sacf", arrived, w_up, preferred_element_type=jnp.float32)
    gate, up = (
        lax.psum(gate.astype(jnp.bfloat16), "pair").astype(jnp.float32),
        lax.psum(up.astype(jnp.bfloat16), "pair").astype(jnp.float32),
    )
    active = (jax.nn.silu(gate) * up).astype(jnp.bfloat16)
    produced = jnp.einsum("sacf,afd->sacd", active, w_down, preferred_element_type=jnp.float32)
    returned = lax.all_to_all(
        produced.astype(jnp.bfloat16), "dev", split_axis=0, concat_axis=0, tiled=True
    )
    flat_back = returned.reshape(slots_all, returned.shape[3])
    picked = flat_back[slot].reshape(rows, picks, flat_back.shape[1]).astype(jnp.float32)
    shares = route_weights / jnp.sum(route_weights, axis=1, keepdims=True)
    result = mixed + jnp.sum(shares[:, :, None] * picked, axis=1)
    return result.astype(jnp.bfloat16)


def solution(mesh):
    in_specs = (
        P(("groups", "dev", "pair"), None, None),
        P(("groups", "dev", "pair"), None, None, None),
        P(("groups", "dev", "pair"), None, None, None),
        P(("groups", "dev", "pair"), None, None),
        P(("groups", "dev", "pair"), None, None),
        P(("groups", "dev", "pair")),
        P("dev", "pair"),
        P(("groups", "dev"), "pair"),
        P("pair"),
        P(("groups", "dev"), None),
        P(("groups", "dev"), None),
        P("dev", "pair", None),
        P("dev", "pair", None),
        P("dev", None, "pair"),
    )
    out_specs = P(("groups", "dev"), "pair")
    return jax.shard_map(
        per_device, mesh=mesh, in_specs=in_specs, out_specs=out_specs, check_vma=False
    )
```

profile of v0, /device:TPU:0, one launch (start us, length us, event | category | flops | bytes accessed | tf_op | source)
XLA Modules:
  0.0 200.0 jit_solution(15346453247266217819)
XLA Ops:
  6.5 0.0 copy-start
  6.5 0.9 iota_compare_fusion.3
  7.4 1.3 fusion.61
  8.7 0.0 copy-start.5
  8.7 0.0 copy-start.9
  8.7 3.7 %fusion.71 = (f32[16,4,16]{2,1,0:T(4,128)S(1)}, f32[16,4,16,256]{3,2,1,0:T(8,128)S(1)}) fusion(bf16[16,4,16,128]{3,2,1,0:T(8,128)(2,1)} %bitcast.86, bf16[16,256,4,128]{3,2,1,0:T(4,128)(2,1)} %param.15, pred[16,256]{1,0:T(8,128)(4,1)S(1)} %iota_compare_fusion.3), kind=kOutput, calls=%fused_computation.74 | convolution fusion | flops 67894272 | bytes 5513216 | tf_op jit(solution)/shard_map/bgjd,btgd->bgjt/dot_general | solution.py:30
  12.4 0.4 fusion.49
  12.9 2.0 %fusion.45 = bf16[16,4,16,128]{3,2,1,0:T(8,128)(2,1)S(1)} fusion(bf16[16,256,4,128]{3,2,1,0:T(4,128)(2,1)S(1)} %copy-done.9, f32[16,4,16,256]{3,2,1,0:T(8,128)S(1)} %get-tuple-element.12, f32[16,4,16]{2,1,0:T(4,128)S(1)} %multiply_maximum_fusion, pred[16,256]{1,0:T(8,128)(4,1)S(1)} %iota_compare_fusion.3, f32[16,4,16]{2,1,0:T(4,128)S(1)} %get-tuple-element.7, ...), kind=kOutput, calls=%fused_computation.29 | convolution fusion | flops 403701760 | bytes 5554176 | tf_op jit(solution)/shard_map/bgjt,btgd->bgjd/dot_general | solution.py:48
  15.0 0.0 copy-start.2
  15.0 0.2 copy.95
  15.2 2.4 %all_gather.3 = bf16[32,8192]{1,0:T(8,128)(2,1)S(1)} all-gather(bf16[16,8192]{1,0:T(8,128)(2,1)S(1)} %bitcast.84), channel_id=1, replica_groups=mesh['groups'=2,'dev'=8,'pair'=2] {'pair'}, dimensions={0}, use_global_device_ids=true | all-gather | bytes 786432 | tf_op jit(solution)/shard_map/all_gather | solution.py:53
  17.6 0.0 copy-start.8
  17.6 0.0 copy-start.4
  17.6 0.0 copy-start.7
  17.6 21.9 %all_to_all.29 = bf16[32,8,1024]{2,0,1:T(8,128)(2,1)S(1)} all-to-all(bf16[32,8,1024]{2,0,1:T(8,128)(2,1)S(1)} %bitcast.83), channel_id=1, replica_groups=mesh['groups'=2,'dev'=8,'pair'=2] {'dev'}, dimensions={1} | all-to-all | bytes 1048576 | tf_op jit(solution)/shard_map/all_to_all | solution.py:55
  39.5 1.7 fusion.72
  41.2 0.0 reduce-scatter.2.cloned.1.call-update
  41.3 0.0 all-reduce.3.cloned.1.call-start
  41.3 0.1 copy.54
  41.4 0.1 eq.43
  41.5 0.1 eq.39
  41.6 0.6 reduce-window.6
  42.2 0.2 slice_reduce_fusion
  42.4 0.1 fusion.65
  42.5 0.1 reduce_sum.64
  42.6 0.2 fusion.58
  42.8 61.6 %reduce-scatter.2.cloned.1.call-done = f32[32,1024]{1,0:T(8,128)} async-done(((f32[256,1024]{1,0:T(8,128)}), f32[32,1024]{1,0:T(8,128)}) %reduce-scatter.2.cloned.1.call-update) | async-done | bytes 131088 | tf_op jit(solution)/shard_map/reduce_scatter | solution.py:56
  104.4 0.0 copy-done.4
  104.4 1.0 multiply_reduce_fusion
  105.4 2.5 %psum.21 = f32[32]{0:T(128)S(1)} all-reduce(f32[32]{0:T(128)S(1)} %multiply_reduce_fusion), channel_id=1, replica_groups=mesh['groups'=2,'dev'=8,'pair'=2] {'pair'}, use_global_device_ids=true, to_apply=%region_9.10 | all-reduce | flops 32 | bytes 256 | tf_op jit(solution)/shard_map/psum | solution.py:63
  107.9 0.0 copy-done.7
  107.9 1.3 convolution_convert_fusion
  109.2 0.0 copy-start.1
  109.2 24.1 %all_to_all.30 = bf16[8,2,24,1024]{3,2,1,0:T(8,128)(2,1)S(1)} all-to-all(bf16[8,2,24,1024]{3,2,1,0:T(8,128)(2,1)S(1)} %bitcast.80), channel_id=1, replica_groups=mesh['groups'=2,'dev'=8,'pair'=2] {'dev'}, dimensions={0} | all-to-all | bytes 1572864 | tf_op jit(solution)/shard_map/all_to_all | solution.py:86
  133.4 3.5 %fusion.28 = bf16[8,2,24,768]{3,2,0,1:T(8,128)(2,1)} fusion(bf16[2,1024,768]{2,1,0:T(8,128)(2,1)} %param.26, bf16[8,2,24,1024]{3,2,1,0:T(8,128)(2,1)S(1)} %all_to_all.30), kind=kOutput, calls=%fused_computation.20 | convolution fusion | flops 604274688 | bytes 4521984 | tf_op jit(solution)/shard_map/sacd,adf->sacf/dot_general | solution.py:88
  136.9 1.6 fusion.31
  138.5 0.0 all-reduce.3.cloned.1.call-update
  138.6 19.1 %all-reduce.3.cloned.1.call-done = (bf16[8,2,24,768]{3,2,0,1:T(8,128)(2,1)}, bf16[8,2,24,768]{3,2,0,1:T(8,128)(2,1)}) async-done(((bf16[8,2,24,768]{3,2,0,1:T(8,128)(2,1)}, bf16[8,2,24,768]{3,2,0,1:T(8,128)(2,1)}), (bf16[8,2,24,768]{3,2,0,1:T(8,128)(2,1)}, bf16[8,2,24,768]{3,2,0,1:T(8,128)(2,1)})) %all-reduce.3.cloned.1.call-update) | async-done | bytes 1179664 | tf_op jit(solution)/shard_map/psum | solution.py:91
  157.6 2.2 %fusion.25 = bf16[8,2,24,1024]{3,2,0,1:T(8,128)(2,1)S(1)} fusion(bf16[2,768,1024]{2,1,0:T(8,128)(2,1)S(1)} %copy-done, bf16[8,2,24,768]{3,2,0,1:T(8,128)(2,1)} %get-tuple-element.5, bf16[8,2,24,768]{3,2,0,1:T(8,128)(2,1)} %get-tuple-element.6), kind=kOutput, calls=%fused_computation.19 | convolution fusion | flops 606732288 | bytes 5111808 | tf_op jit(solution)/shard_map/sacf,afd->sacd/dot_general | solution.py:94
  159.8 0.0 copy-start.6
  159.8 1.0 copy.60
  160.8 5.9 %all-to-all-start.2 = ((bf16[8,2,24,1024]{3,2,1,0:T(8,128)(2,1)}), bf16[8,2,24,1024]{3,2,1,0:T(8,128)(2,1)}, u32[]{:S(2)}, u32[]{:S(2)}) async-start(bf16[8,2,24,1024]{3,2,1,0:T(8,128)(2,1)} %copy.60), calls=%async_computation.3 | async-start | bytes 1572864 | tf_op jit(solution)/shard_map/all_to_all | solution.py:95
  166.7 0.1 mul.100
  166.9 0.1 copy.53
  167.0 20.5 %all-to-all-done.2 = bf16[8,2,24,1024]{3,2,1,0:T(8,128)(2,1)} async-done(((bf16[8,2,24,1024]{3,2,1,0:T(8,128)(2,1)}), bf16[8,2,24,1024]{3,2,1,0:T(8,128)(2,1)}, u32[]{:S(2)}, u32[]{:S(2)}) %all-to-all-start.2) | async-done | bytes 786464 | tf_op jit(solution)/shard_map/all_to_all | solution.py:95
  187.4 3.6 %gather_fusion = bf16[256,1024]{1,0:T(8,128)(2,1)} fusion(bf16[384,1024]{1,0:T(8,128)(2,1)} %bitcast.17, s32[1024]{0:T(1024)S(1)} %pad_clamp_fusion), kind=kCustom, calls=%fused_computation | custom fusion | bytes 1049600 | tf_op jit(solution)/shard_map/gather | solution.py:99
  191.0 1.4 fusion.48
  192.5 0.7 add_convert_fusion
  (23 shorter events, 0.2 us)
Async XLA Ops:
  6.5 151.1 %copy-start = (bf16[2,768,1024]{2,1,0:T(8,128)(2,1)S(1)}, bf16[2,768,1024]{2,1,0:T(8,128)(2,1)}, u32[]{:S(2)}) copy-start(bf16[2,768,1024]{2,1,0:T(8,128)(2,1)} %param.27) | copy-start | bytes 9437188
  6.5 97.8 %reduce-scatter.2.cloned.1.call-start = ((), (), s32[]{:S(2)}) async-start(), calls=%async_computation.4 | async-start | bytes 1179648 | tf_op jit(solution)/shard_map/reduce_scatter | solution.py:56
  8.7 4.2 %copy-start.5 = (bf16[16,4,128]{2,1,0:T(4,128)(2,1)S(1)}, bf16[16,4,128]{2,1,0:T(4,128)(2,1)}, u32[]{:S(2)}) copy-start(bf16[16,4,128]{2,1,0:T(4,128)(2,1)} %param.18) | copy-start | bytes 49156
  8.7 4.3 %copy-start.9 = (bf16[16,256,4,128]{3,2,1,0:T(4,128)(2,1)S(1)}, bf16[16,256,4,128]{3,2,1,0:T(4,128)(2,1)}, u32[]{:S(2)}) copy-start(bf16[16,256,4,128]{3,2,1,0:T(4,128)(2,1)} %param.16) | copy-start | bytes 12582916
  15.0 24.6 %copy-start.2 = (bf16[1024,1024]{1,0:T(8,128)(2,1)S(1)}, bf16[1024,1024]{1,0:T(8,128)(2,1)}, u32[]{:S(2)}) copy-start(bf16[1024,1024]{1,0:T(8,128)(2,1)} %param.20) | copy-start | bytes 6291460
  17.6 23.7 %copy-start.8 = (s32[32,8]{0,1:T(8,128)S(1)}, s32[32,8]{0,1:T(8,128)}, u32[]{:S(2)}) copy-start(s32[32,8]{0,1:T(8,128)} %param.23) | copy-start | bytes 3076
  17.6 86.8 %copy-start.4 = (bf16[32,1024]{1,0:T(8,128)(2,1)S(1)}, bf16[32,1024]{1,0:T(8,128)(2,1)}, u32[]{:S(2)}) copy-start(bf16[32,1024]{1,0:T(8,128)(2,1)} %param.21) | copy-start | bytes 196612
  17.6 90.3 %copy-start.7 = (f32[1024]{0:T(1024)S(1)}, f32[1024]{0:T(1024)}, u32[]{:S(2)}) copy-start(f32[1024]{0:T(1024)} %param.22) | copy-start | bytes 12292
  41.3 116.4 %all-reduce.3.cloned.1.call-start = ((), (), s32[]{:S(2)}) async-start(), calls=%async_computation.5 | async-start | bytes 2359296 | tf_op jit(solution)/shard_map/psum | solution.py:91
  109.2 27.7 %copy-start.1 = (bf16[2,1024,768]{2,1,0:T(8,128)(2,1)S(1)}, bf16[2,1024,768]{2,1,0:T(8,128)(2,1)}, u32[]{:S(2)}) copy-start(bf16[2,1024,768]{2,1,0:T(8,128)(2,1)} %param.25) | copy-start | bytes 9437188
  159.8 7.0 %copy-start.6 = (f32[32,8]{0,1:T(8,128)S(1)}, f32[32,8]{0,1:T(8,128)}, u32[]{:S(2)}) copy-start(f32[32,8]{0,1:T(8,128)} %param.24) | copy-start | bytes 3076
  160.8 31.6 %copy-start.3 = (f32[32,1024]{1,0:T(8,128)S(1)}, f32[32,1024]{1,0:T(8,128)}, u32[]{:S(2)}) copy-start(f32[32,1024]{1,0:T(8,128)} %reduce-scatter.2.cloned.1.call-done) | copy-start | bytes 393220
  160.8 26.6 %all-to-all-start.2 = ((bf16[8,2,24,1024]{3,2,1,0:T(8,128)(2,1)}), bf16[8,2,24,1024]{3,2,1,0:T(8,128)(2,1)}, u32[]{:S(2)}, u32[]{:S(2)}) async-start(bf16[8,2,24,1024]{3,2,1,0:T(8,128)(2,1)} %copy.60), calls=%async_computation.3 | async-start | bytes 1572864 | tf_op jit(solution)/shard_map/all_to_all | solution.py:95
Sparse Core Ops, SparseCore 0:
  41.4 62.9 reduce-scatter.1
  138.7 18.8 all-reduce.2
where the time goes:
time: 200 us
  waiting for transfers between devices  101 us (50%)
  blocking collectives  50.9 us (25%)
  matrix products  17.4 us (9%)
  between operations  13.6 us (7%)
  starting transfers between devices  5.96 us (3%)
  local copies, waits for them, and re-layouts  5.52 us (3%)
  other arithmetic  5.45 us (3%)
    reduce_scatter x1, waiting for transfers between devices, per_device(): lax.psum_scatter(jnp.dot(regrouped, out_weight, preferred_element_type=jn...  61.6 us
    all_to_all x1, blocking collectives, per_device(): lax.all_to_all(outgoing, 'dev', split_axis=0, concat_axis=0, tiled=True)  24.1 us
    all_to_all x1, blocking collectives, per_device(): lax.all_to_all(attended, 'dev', split_axis=1, concat_axis=0, tiled=True)  21.9 us
    all_to_all x1, waiting for transfers between devices, per_device(): lax.all_to_all(produced.astype(jnp.bfloat16), 'dev', split_axis=0, concat...  20.5 us
    psum x1, waiting for transfers between devices, per_device(): lax.psum(up.astype(jnp.bfloat16), 'pair').astype(jnp.float32)  19.1 us
    all_to_all x1, starting transfers between devices, per_device(): lax.all_to_all(produced.astype(jnp.bfloat16), 'dev', split_axis=0, concat...  5.92 us
  transfers between devices with their start and end apart: 3, of which 3 were waited for; matrix products, arithmetic and copies ran while one was open for 1% of the time, Pallas kernels for 0%

commit v1 on v0

v1 whole, which is shorter than its diff:
```python
import functools

import jax
import jax.numpy as jnp
from jax import lax
from jax.experimental import pallas as pl
from jax.experimental.pallas import tpu as pltpu
from jax.sharding import PartitionSpec as P

F32 = jnp.float32
BF16 = jnp.bfloat16


def attend_kernel(kv_heads, len_ref, q_ref, k_ref, v_ref, ik_ref, iv_ref, o_ref):
    block_rows, heads, size = q_ref.shape
    span = k_ref.shape[1]
    per = heads // kv_heads
    factor = size ** (-0.5)
    base = pl.program_id(0) * block_rows
    column = lax.broadcasted_iota(jnp.int32, (heads, span), 1)
    head = lax.broadcasted_iota(jnp.int32, (heads, span), 0)
    same = lax.rem(column, kv_heads) == head // per
    for i in range(block_rows):
        q = q_ref[i]
        scores = lax.dot_general(
            q, k_ref[i], (((1,), (1,)), ((), ())), preferred_element_type=F32
        )
        valid = same & (column < len_ref[base + i] * kv_heads)
        masked = jnp.where(valid, scores * factor, -1e30)
        spread = lambda ref: jnp.concatenate(
            [jnp.broadcast_to(ref[i, g : g + 1, :].astype(F32), (per, size)) for g in range(kv_heads)], axis=0
        )
        own = jnp.sum(q.astype(F32) * spread(ik_ref), axis=1, keepdims=True) * factor
        peak = jnp.maximum(jnp.max(masked, axis=1, keepdims=True), own)
        expo = jnp.exp(masked - peak)
        fresh = jnp.exp(own - peak)
        total = jnp.sum(expo, axis=1, keepdims=True) + fresh
        accum = jnp.dot(expo.astype(BF16), v_ref[i], preferred_element_type=F32)
        accum = accum + fresh * spread(iv_ref)
        o_ref[i] = (accum / total).astype(o_ref.dtype)


def attend(query, keys, values, fresh_key, fresh_value, lengths):
    rows, heads, size = query.shape
    positions, kv_heads = keys.shape[1:3]
    span = positions * kv_heads
    block = 2
    at = lambda i, _: (i, 0, 0)
    grid_spec = pltpu.PrefetchScalarGridSpec(
        num_scalar_prefetch=1,
        grid=(rows // block,),
        in_specs=[
            pl.BlockSpec((block, heads, size), at),
            pl.BlockSpec((block, span, size), at),
            pl.BlockSpec((block, span, size), at),
            pl.BlockSpec((block, kv_heads, size), at),
            pl.BlockSpec((block, kv_heads, size), at),
        ],
        out_specs=pl.BlockSpec((block, heads, size), at),
    )
    return pl.pallas_call(
        functools.partial(attend_kernel, kv_heads),
        out_shape=jax.ShapeDtypeStruct(query.shape, BF16),
        grid_spec=grid_spec,
        compiler_params=pltpu.CompilerParams(vmem_limit_bytes=32 * 1024 * 1024),
    )(
        lengths,
        query,
        keys.reshape(rows, span, size),
        values.reshape(rows, span, size),
        fresh_key,
        fresh_value,
    )


def per_device(
    query,
    stored_keys,
    stored_values,
    incoming_key,
    incoming_value,
    lengths,
    out_weight,
    residual,
    norm_gain,
    expert_ids,
    route_weights,
    w_gate,
    w_up,
    w_down,
):
    devs = lax.axis_size("dev")
    cores = lax.axis_size("pair")
    me = lax.axis_index("dev")
    core = lax.axis_index("pair")
    slots = devs // cores
    offset = [[c * slots + s for s in range(slots)] for c in range(cores)]

    def from_core(value, m):
        return lax.ppermute(value, "pair", [(c, c ^ m) for c in range(cores)])

    def swap(value, s):
        pairs = [
            (d * cores + c, (d ^ offset[c][s]) * cores + c)
            for d in range(devs)
            for c in range(cores)
            if offset[c][s]
        ]
        moved = lax.ppermute(value, ("dev", "pair"), pairs)
        if any(offset[c][s] == 0 for c in range(cores)):
            keep = functools.reduce(
                jnp.logical_or, [core == c for c in range(cores) if offset[c][s] == 0]
            )
            moved = jnp.where(keep, value, moved)
        return moved

    def gathered(value):
        return [value] + [from_core(value, m) for m in range(1, cores)]

    rows, part = residual.shape
    width = part * cores
    wo = gathered(out_weight)
    wg = gathered(w_gate)
    wu = gathered(w_up)
    wd = gathered(w_down)
    stream = jnp.concatenate(gathered(residual), axis=1).astype(F32)
    gain = jnp.concatenate(gathered(norm_gain), axis=0)

    attended = attend(query, stored_keys, stored_values, incoming_key, incoming_value, lengths)
    local_rows = query.shape[0]
    features = out_weight.shape[0]
    attended = attended.reshape(local_rows, devs, features)
    places = jnp.array(offset, dtype=jnp.int32) ^ me

    def blocks_of(c):
        return jnp.take(attended, places[c], axis=1)

    held = [blocks_of(core)]
    for m in range(1, cores):
        held.append(from_core(blocks_of(core ^ m), m))
    stacked = jnp.stack(held, axis=0)
    stacked = jnp.take(stacked, jnp.arange(cores, dtype=jnp.int32) ^ core, axis=0)
    stacked = stacked.reshape(rows, slots, features)
    arrived = jnp.concatenate([swap(stacked[:, s], s) for s in range(slots)], axis=0)
    partial = jnp.concatenate(
        [jnp.dot(arrived, w, preferred_element_type=F32) for w in wo], axis=1
    ).astype(BF16)
    sums = sum(
        swap(partial[s * rows : (s + 1) * rows], s).astype(F32) for s in range(slots)
    )

    def other_order(value, m):
        pieces = [value[:, j * part : (j + 1) * part] for j in range(cores)]
        return jnp.concatenate([pieces[j ^ m] for j in range(cores)], axis=1)

    mixed = stream + sums
    for m in range(1, cores):
        mixed = mixed + other_order(from_core(sums, m), m)
    squares = jnp.sum(mixed * mixed, axis=1, keepdims=True)
    normed = (mixed * lax.rsqrt(squares / width + 1e-06) * gain[None, :]).astype(BF16)

    local_experts = w_gate.shape[0]
    experts = local_experts * devs
    shares = route_weights / jnp.sum(route_weights, axis=1, keepdims=True)
    chosen = expert_ids[:, :, None] == jnp.arange(experts, dtype=jnp.int32)[None, None, :]
    combine = jnp.sum(jnp.where(chosen, shares[:, :, None], 0.0), axis=1)
    upper = combine.astype(BF16)
    lower = (combine - upper.astype(F32)).astype(BF16)
    extra = -(-2 * experts // 128) * 128
    pad = jnp.zeros((rows, extra - 2 * experts), BF16)
    packed = jnp.concatenate([normed, upper, lower, pad], axis=1)
    tokens = jnp.concatenate([swap(packed, s) for s in range(slots)], axis=0)

    total_rows = rows * slots
    tail = tokens[:, width:].astype(F32)
    upper_mine = lax.dynamic_slice_in_dim(tail, me * local_experts, local_experts, 1)
    lower_mine = lax.dynamic_slice_in_dim(tail, experts + me * local_experts, local_experts, 1)
    mine = upper_mine + lower_mine
    outs = [jnp.zeros((total_rows, part), F32) for _ in range(cores)]
    for e in range(local_experts):
        gate = sum(
            jnp.dot(tokens[:, j * part : (j + 1) * part], wg[j][e], preferred_element_type=F32)
            for j in range(cores)
        )
        up = sum(
            jnp.dot(tokens[:, j * part : (j + 1) * part], wu[j][e], preferred_element_type=F32)
            for j in range(cores)
        )
        active = (jax.nn.silu(gate) * up * mine[:, e : e + 1]).astype(BF16)
        outs = [
            o + jnp.dot(active, wd[j][e], preferred_element_type=F32) for j, o in enumerate(outs)
        ]
    produced = jnp.concatenate(outs, axis=1).astype(BF16)
    back = sum(
        swap(produced[s * rows : (s + 1) * rows], s).astype(F32) for s in range(slots)
    )
    result = mixed[:, :part] + back[:, :part]
    for m in range(1, cores):
        result = result + from_core(back[:, m * part : (m + 1) * part], m)
    return result.astype(BF16)


def solution(mesh):
    in_specs = (
        P(("groups", "dev", "pair"), None, None),
        P(("groups", "dev", "pair"), None, None, None),
        P(("groups", "dev", "pair"), None, None, None),
        P(("groups", "dev", "pair"), None, None),
        P(("groups", "dev", "pair"), None, None),
        P(("groups", "dev", "pair")),
        P("dev", "pair"),
        P(("groups", "dev"), "pair"),
        P("pair"),
        P(("groups", "dev"), None),
        P(("groups", "dev"), None),
        P("dev", "pair", None),
        P("dev", "pair", None),
        P("dev", None, "pair"),
    )
    out_specs = P(("groups", "dev"), "pair")
    return jax.shard_map(
        per_device, mesh=mesh, in_specs=in_specs, out_specs=out_specs, check_vma=False
    )
```

time: 200 us -> 109 us (0.55)
  waiting for transfers between devices: 101 us -> 17.8 us
  blocking collectives: 50.9 us -> 0 us
  starting transfers between devices: 5.96 us -> 49.4 us
  between operations: 13.6 us -> 0.46 us
  local copies, waits for them, and re-layouts: 5.52 us -> 13.5 us
  Pallas kernels: 0 us -> 6.98 us
    reduce_scatter x1 -> x0, waiting for transfers between devices: 61.6 us -> none  [per_device(): lax.psum_scatter(jnp.dot(regrouped, out_weight, preferred_element_type=jn...]
    ppermute x0 -> x25, starting transfers between devices: none -> 49.4 us  [the longest x9 31.5 us: from_core(): return lax.ppermute(value, 'pair', [(c, c ^ m) for c in range(cores)])]
    all_to_all x2 -> x0, blocking collectives: 46 us -> none  [the longest x1 24.1 us: per_device(): lax.all_to_all(outgoing, 'dev', split_axis=0, concat_axis=0, tiled=True)]
    all_to_all x1 -> x0, waiting for transfers between devices: 20.5 us -> none  [per_device(): lax.all_to_all(produced.astype(jnp.bfloat16), 'dev', split_axis=0, concat...]
    psum x1 -> x0, waiting for transfers between devices: 19.1 us -> none  [per_device(): lax.psum(up.astype(jnp.bfloat16), 'pair').astype(jnp.float32)]
    ppermute x0 -> x25, waiting for transfers between devices: none -> 17.8 us  [the longest x16 13.5 us: swap(): moved = lax.ppermute(value, ('dev', 'pair'), pairs)]
    unnamed x22 -> x26, local copies, waits for them, and re-layouts: 0.31 us -> 7.85 us
    pallas_call x0 -> x1, Pallas kernels: none -> 6.98 us  [attend(): pl.pallas_call(functools.partial(attend_kernel, kv_heads), out_shape=jax....]
  transfers between devices with their start and end apart: 3 -> 25, of which waited for: 3 -> 11; matrix products, arithmetic and copies ran while one was open for 1% -> 23% of each run, Pallas kernels for 0% -> 6%
where the time goes in v1:
time: 109 us
  starting transfers between devices  49.4 us (45%)
  waiting for transfers between devices  17.8 us (16%)
  matrix products  15.8 us (14%)
  local copies, waits for them, and re-layouts  13.5 us (12%)
  Pallas kernels  6.98 us (6%)
  other arithmetic  4.72 us (4%)
    ppermute x9, starting transfers between devices, from_core(): return lax.ppermute(value, 'pair', [(c, c ^ m) for c in range(cores)])  31.5 us
    ppermute x16, starting transfers between devices, swap(): moved = lax.ppermute(value, ('dev', 'pair'), pairs)  17.9 us
    ppermute x16, waiting for transfers between devices, swap(): moved = lax.ppermute(value, ('dev', 'pair'), pairs)  13.5 us
    unnamed x26, local copies, waits for them, and re-layouts  7.85 us
    dot_general x4, matrix products, per_device(): jnp.dot(tokens[:, j * part:(j + 1) * part], wu[j][e], preferred_element_t...  7.31 us
    pallas_call x1, Pallas kernels, attend(): pl.pallas_call(functools.partial(attend_kernel, kv_heads), out_shape=jax....  6.98 us
    dot_general x4, matrix products, per_device(): jnp.dot(tokens[:, j * part:(j + 1) * part], wg[j][e], preferred_element_t...  4.31 us
    ppermute x9, waiting for transfers between devices, from_core(): return lax.ppermute(value, 'pair', [(c, c ^ m) for c in range(cores)])  4.23 us
  transfers between devices with their start and end apart: 25, of which 11 were waited for; matrix products, arithmetic and copies ran while one was open for 23% of the time, Pallas kernels for 6%

profile of v1, /device:TPU:0, one launch (start us, length us, event | category | flops | bytes accessed | tf_op | source)
XLA Modules:
  0.0 108.6 jit_solution(18418450921897403809)
XLA Ops:
  0.5 0.7 broadcast_xor_fusion
  1.2 2.2 %copy-done = bf16[16,256,4,128]{3,2,1,0:T(4,128)(2,1)S(1)} copy-done((bf16[16,256,4,128]{3,2,1,0:T(4,128)(2,1)S(1)}, bf16[16,256,4,128]{3,2,1,0:T(4,128)(2,1)}, u32[]{:S(2)}) %copy-start) | copy-done | bytes 4194328
  3.4 2.2 %copy-done.1 = bf16[16,256,4,128]{3,2,1,0:T(4,128)(2,1)S(1)} copy-done((bf16[16,256,4,128]{3,2,1,0:T(4,128)(2,1)S(1)}, bf16[16,256,4,128]{3,2,1,0:T(4,128)(2,1)}, u32[]{:S(2)}) %copy-start.1) | copy-done | bytes 4194328
  5.5 0.9 copy-done.2
  6.5 0.7 copy-done.3
  7.2 0.7 copy-done.4
  8.6 7.0 %shard_map.145 = bf16[16,64,128]{2,1,0:T(8,128)(2,1)S(1)} custom-call(s32[16]{0:T(128)S(1)} %copy-done.5, bf16[16,64,128]{2,1,0:T(8,128)(2,1)S(1)} %copy-done.2, bf16[16,1024,128]{2,1,0:T(8,128)(2,1)S(1)} %bitcast.95, bf16[16,1024,128]{2,1,0:T(8,128)(2,1)S(1)} %bitcast.96, bf16[16,4,128]{2,1,0:T(4,128)(2,1)S(1)} %copy-done.3, bf16[16,4,128]{2,1,0:T(4,128)(2,1)S(1)} %copy-done.4), custom_call_target="tpu_custom_call" | custom-call | tf_op jit(solution)/shard_map/pallas_call | solution.py:61
  18.7 0.7 collective-permute-start.2
  19.4 5.1 %collective-permute-start.12 = (f32[1024]{0:T(1024)}, f32[1024]{0:T(1024)}, u32[]{:S(2)}, u32[]{:S(2)}) collective-permute-start(f32[1024]{0:T(1024)} %param.25), channel_id=1, source_target_pairs={{0,1},{1,0},{2,3},{3,2},{4,5},{5,4},{6,7},{7,6},{8,9},{9,8},{10,11... | collective-permute-start | bytes 12296 | tf_op jit(solution)/shard_map/ppermute | solution.py:100
  24.5 2.6 %collective-permute-start.5 = (bf16[32,1024]{1,0:T(8,128)(2,1)S(1)}, bf16[32,1024]{1,0:T(8,128)(2,1)S(1)}, u32[]{:S(2)}, u32[]{:S(2)}) collective-permute-start(bf16[32,1024]{1,0:T(8,128)(2,1)S(1)} %get-tuple-element.27), channel_id=1, source_target_pairs={{0,6},{1,15},{2,4},{3,13},{4,2},{5,11},{6,0},{7,9},{8,14},{9,7},{1... | collective-permute-start | bytes 196616 | tf_op jit(solution)/shard_map/ppermute | solution.py:109
  28.1 1.7 %collective-permute-done.5 = bf16[32,1024]{1,0:T(8,128)(2,1)S(1)} collective-permute-done((bf16[32,1024]{1,0:T(8,128)(2,1)S(1)}, bf16[32,1024]{1,0:T(8,128)(2,1)S(1)}, u32[]{:S(2)}, u32[]{:S(2)}) %collective-permute-start.5) | collective-permute-done | bytes 65568 | tf_op jit(solution)/shard_map/ppermute | solution.py:109
  29.7 2.5 %collective-permute-done.4 = bf16[32,1024]{1,0:T(8,128)(2,1)S(1)} collective-permute-done((bf16[32,1024]{1,0:T(8,128)(2,1)S(1)}, bf16[32,1024]{1,0:T(8,128)(2,1)S(1)}, u32[]{:S(2)}, u32[]{:S(2)}) %collective-permute-start.4) | collective-permute-done | bytes 65568 | tf_op jit(solution)/shard_map/ppermute | solution.py:109
  32.7 2.2 %convolution_convert_fusion = bf16[128,1024]{1,0:T(8,128)(2,1)S(1)} fusion(bf16[1024,1024]{1,0:T(8,128)(2,1)} %collective-permute-done.6, bf16[32,1024]{1,0:T(8,128)(2,1)S(1)} %collective-permute-done.5, bf16[32,1024]{1,0:T(8,128)(2,1)S(1)} %collective-permute-done.4, bf16[32,1024]{1,0:T(8,128)(2,1)S(1)} %collective-permute-done.3, ...), kind=kOutput, calls=%fused_computation.37 | convolution fusion | flops 269615104 | bytes 2621440 | tf_op jit(solution)/shard_map/dot_general | solution.py:146
  35.0 0.8 collective-permute-start.8
  35.7 1.9 %collective-permute-start.10 = (bf16[32,2048]{1,0:T(8,128)(2,1)S(1)}, bf16[32,2048]{1,0:T(8,128)(2,1)S(1)}, u32[]{:S(2)}, u32[]{:S(2)}) collective-permute-start(bf16[32,2048]{1,0:T(8,128)(2,1)S(1)} %get-tuple-element.22), channel_id=1, source_target_pairs={{0,6},{1,15},{2,4},{3,13},{4,2},{5,11},{6,0},{7,9},{8,14},{9,7},{1... | collective-permute-start | bytes 393224 | tf_op jit(solution)/shard_map/ppermute | solution.py:109
  37.7 0.8 collective-permute-start.9
  38.5 0.7 collective-permute-start.7
  39.2 0.8 collective-permute-done.8
  40.0 4.2 %collective-permute-start = (bf16[32,1024]{1,0:T(8,128)(2,1)S(1)}, bf16[32,1024]{1,0:T(8,128)(2,1)S(1)}, u32[]{:S(2)}, u32[]{:S(2)}) collective-permute-start(bf16[32,1024]{1,0:T(8,128)(2,1)S(1)} %copy-done.9), channel_id=1, source_target_pairs={{0,1},{1,0},{2,3},{3,2},{4,5},{5,4},{6,7},{7,6},{8,9},{9,8},{10,11... | collective-permute-start | bytes 196616 | tf_op jit(solution)/shard_map/ppermute | solution.py:100
  44.2 1.1 collective-permute-start.17
  45.2 1.8 %collective-permute-done.9 = bf16[32,2048]{1,0:T(8,128)(2,1)S(1)} collective-permute-done((bf16[32,2048]{1,0:T(8,128)(2,1)S(1)}, bf16[32,2048]{1,0:T(8,128)(2,1)S(1)}, u32[]{:S(2)}, u32[]{:S(2)}) %collective-permute-start.9) | collective-permute-done | bytes 131104 | tf_op jit(solution)/shard_map/ppermute | solution.py:109
  47.2 4.1 %collective-permute-start.11 = (f32[32,2048]{1,0:T(8,128)S(1)}, f32[32,2048]{1,0:T(8,128)}, u32[]{:S(2)}, u32[]{:S(2)}) collective-permute-start(f32[32,2048]{1,0:T(8,128)S(1)} %convert_add_fusion.1), channel_id=1, source_target_pairs={{0,1},{1,0},{2,3},{3,2},{4,5},{5,4},{6,7},{7,6},{8,9},{9,8},{10,11... | collective-permute-start | bytes 786440 | tf_op jit(solution)/shard_map/ppermute | solution.py:100
  51.4 0.7 copy.38
  52.0 0.7 pad_maximum_fusion.7
  52.7 2.8 %collective-permute-done.11 = f32[32,2048]{1,0:T(8,128)} collective-permute-done((f32[32,2048]{1,0:T(8,128)S(1)}, f32[32,2048]{1,0:T(8,128)}, u32[]{:S(2)}, u32[]{:S(2)}) %collective-permute-start.11) | collective-permute-done | bytes 262176 | tf_op jit(solution)/shard_map/ppermute | solution.py:100
  55.5 1.0 fusion.73
  56.5 1.1 %multiply_reduce_fusion = (f32[32]{0:T(128)S(1)}, f32[32,2048]{1,0:T(8,128)S(1)}) fusion(f32[32,1024]{1,0:T(8,128)S(1)} %get-tuple-element.25, f32[32,1024]{1,0:T(8,128)S(1)} %get-tuple-element.24, f32[32,2048]{1,0:T(8,128)} %copy-done.8, bf16[32,1024]{1,0:T(8,128)(2,1)S(1)} %collective-permute-done, bf16[32,1024]{1,0:T(8,128)(2,1)S(1)} %copy-done.9), kind=kLoop, calls=%fused_computation.64 | loop fusion | flops 589792 | bytes 917632 | tf_op jit(solution)/shard_map/reduce_sum | solution.py:159
  57.7 0.7 multiply_convert_fusion.2
  59.0 1.0 concatenate.31
  60.0 1.3 %collective-permute-start.13 = (bf16[32,2176]{1,0:T(8,128)(2,1)S(1)}, bf16[32,2176]{1,0:T(8,128)(2,1)}, u32[]{:S(2)}, u32[]{:S(2)}) collective-permute-start(bf16[32,2176]{1,0:T(8,128)(2,1)S(1)} %concatenate.31), channel_id=1, source_target_pairs={{1,9},{3,11},{5,13},{7,15},{9,1},{11,3},{13,5},{15,7},{17,25},{19,... | collective-permute-start | bytes 417800 | tf_op jit(solution)/shard_map/ppermute | solution.py:109
  61.7 2.3 %collective-permute-start.15 = (bf16[32,2176]{1,0:T(8,128)(2,1)S(1)}, bf16[32,2176]{1,0:T(8,128)(2,1)S(1)}, u32[]{:S(2)}, u32[]{:S(2)}) collective-permute-start(bf16[32,2176]{1,0:T(8,128)(2,1)S(1)} %concatenate.31), channel_id=1, source_target_pairs={{0,4},{1,13},{2,6},{3,15},{4,0},{5,9},{6,2},{7,11},{8,12},{9,5},{1... | collective-permute-start | bytes 417800 | tf_op jit(solution)/shard_map/ppermute | solution.py:109
  64.1 0.9 collective-permute-start.14
  65.0 3.1 %collective-permute-done.16 = bf16[32,2176]{1,0:T(8,128)(2,1)S(1)} collective-permute-done((bf16[32,2176]{1,0:T(8,128)(2,1)S(1)}, bf16[32,2176]{1,0:T(8,128)(2,1)S(1)}, u32[]{:S(2)}, u32[]{:S(2)}) %collective-permute-start.16) | collective-permute-done | bytes 139296 | tf_op jit(solution)/shard_map/ppermute | solution.py:109
  68.1 4.3 %collective-permute-start.19 = (bf16[2,768,1024]{2,1,0:T(8,128)(2,1)}, bf16[2,768,1024]{2,1,0:T(8,128)(2,1)S(1)}, u32[]{:S(2)}, u32[]{:S(2)}) collective-permute-start(bf16[2,768,1024]{2,1,0:T(8,128)(2,1)} %param.30), channel_id=1, source_target_pairs={{0,1},{1,0},{2,3},{3,2},{4,5},{5,4},{6,7},{7,6},{8,9},{9,8},{10,11... | collective-permute-start | bytes 9437192 | tf_op jit(solution)/shard_map/ppermute | solution.py:100
  72.8 1.8 %fusion.3 = f32[128,768]{1,0:T(8,128)S(1)} fusion(bf16[2,1024,768]{2,1,0:T(8,128)(2,1)} %collective-permute-done.17, bf16[128,2176]{1,0:T(8,128)(2,1)S(1)} %pad_maximum_fusion), kind=kOutput, calls=%fused_computation.10 | convolution fusion | flops 201326592 | bytes 2228224 | tf_op jit(solution)/shard_map/dot_general | solution.py:182
  74.6 1.8 %fusion.5 = f32[128,768]{1,0:T(8,128)S(1)} fusion(bf16[2,1024,768]{2,1,0:T(8,128)(2,1)} %collective-permute-done.17, bf16[128,2176]{1,0:T(8,128)(2,1)S(1)} %pad_maximum_fusion), kind=kOutput, calls=%fused_computation.14 | convolution fusion | flops 201326592 | bytes 2228224 | tf_op jit(solution)/shard_map/dot_general | solution.py:182
  76.4 1.8 %fusion.2 = f32[128,768]{1,0:T(8,128)S(1)} fusion(bf16[2,1024,768]{2,1,0:T(8,128)(2,1)} %collective-permute-done.18, bf16[128,2176]{1,0:T(8,128)(2,1)S(1)} %pad_maximum_fusion), kind=kOutput, calls=%fused_computation.8 | convolution fusion | flops 201326592 | bytes 2228224 | tf_op jit(solution)/shard_map/dot_general | solution.py:186
  78.2 1.8 %fusion.4 = f32[128,768]{1,0:T(8,128)S(1)} fusion(bf16[2,1024,768]{2,1,0:T(8,128)(2,1)} %collective-permute-done.18, bf16[128,2176]{1,0:T(8,128)(2,1)S(1)} %pad_maximum_fusion), kind=kOutput, calls=%fused_computation.12 | convolution fusion | flops 201326592 | bytes 2228224 | tf_op jit(solution)/shard_map/dot_general | solution.py:186
  80.4 1.9 %multiply_convert_fusion = bf16[128,768]{1,0:T(8,128)(2,1)S(1)} fusion(f32[128,768]{1,0:T(8,128)S(1)} %fusion.38, f32[128]{0:T(128)S(1)} %get-tuple-element.7, f32[128,768]{1,0:T(8,128)S(1)} %fusion.2, bf16[2,1024,768]{2,1,0:T(8,128)(2,1)} %param.29, bf16[128,2176]{1,0:T(8,128)(2,1)S(1)} %pad_maximum_fusion), kind=kOutput, calls=%fused_computation.56 | convolution fusion | flops 202113024 | bytes 2818560 | tf_op jit(solution)/shard_map/dot_general | solution.py:186
  83.5 1.8 %multiply_convert_fusion.1 = bf16[128,768]{1,0:T(8,128)(2,1)S(1)} fusion(f32[128,768]{1,0:T(8,128)S(1)} %fusion.32, f32[128]{0:T(128)S(1)} %get-tuple-element.6, f32[128,768]{1,0:T(8,128)S(1)} %fusion.4, bf16[2,1024,768]{2,1,0:T(8,128)(2,1)} %param.29, bf16[128,2176]{1,0:T(8,128)(2,1)S(1)} %pad_maximum_fusion), kind=kOutput, calls=%fused_computation.57 | convolution fusion | flops 202113024 | bytes 2818560 | tf_op jit(solution)/shard_map/dot_general | solution.py:186
  86.5 2.3 %collective-permute-start.21 = (bf16[32,2048]{1,0:T(8,128)(2,1)S(1)}, bf16[32,2048]{1,0:T(8,128)(2,1)S(1)}, u32[]{:S(2)}, u32[]{:S(2)}) collective-permute-start(bf16[32,2048]{1,0:T(8,128)(2,1)S(1)} %get-tuple-element.17), channel_id=1, source_target_pairs={{0,2},{1,11},{2,0},{3,9},{4,6},{5,15},{6,4},{7,13},{8,10},{9,3},{1... | collective-permute-start | bytes 393224 | tf_op jit(solution)/shard_map/ppermute | solution.py:109
  88.8 0.8 collective-permute-start.23
  89.6 0.7 collective-permute-start.22
  90.3 0.7 collective-permute-start.20
  91.0 1.7 %collective-permute-done.21 = bf16[32,2048]{1,0:T(8,128)(2,1)S(1)} collective-permute-done((bf16[32,2048]{1,0:T(8,128)(2,1)S(1)}, bf16[32,2048]{1,0:T(8,128)(2,1)S(1)}, u32[]{:S(2)}, u32[]{:S(2)}) %collective-permute-start.21) | collective-permute-done | bytes 131104 | tf_op jit(solution)/shard_map/ppermute | solution.py:109
  92.7 1.9 %collective-permute-done.23 = bf16[32,2048]{1,0:T(8,128)(2,1)S(1)} collective-permute-done((bf16[32,2048]{1,0:T(8,128)(2,1)S(1)}, bf16[32,2048]{1,0:T(8,128)(2,1)S(1)}, u32[]{:S(2)}, u32[]{:S(2)}) %collective-permute-start.23) | collective-permute-done | bytes 131104 | tf_op jit(solution)/shard_map/ppermute | solution.py:109
  94.8 12.1 %collective-permute-start.24 = (f32[32,1024]{1,0:T(8,128)S(1)}, f32[32,1024]{1,0:T(8,128)S(1)}, u32[]{:S(2)}, u32[]{:S(2)}) collective-permute-start(f32[32,1024]{1,0:T(8,128)S(1)} %slice.178), channel_id=1, source_target_pairs={{0,1},{1,0},{2,3},{3,2},{4,5},{5,4},{6,7},{7,6},{8,9},{9,8},{10,11... | collective-permute-start | bytes 393224 | tf_op jit(solution)/shard_map/ppermute | solution.py:100
  107.0 1.0 collective-permute-done.24
  (88 shorter events, 10.8 us)
Async XLA Ops:
  0.0 32.7 %collective-permute-start.6 = (bf16[1024,1024]{1,0:T(8,128)(2,1)}, bf16[1024,1024]{1,0:T(8,128)(2,1)}, u32[]{:S(2)}, u32[]{:S(2)}) collective-permute-start(bf16[1024,1024]{1,0:T(8,128)(2,1)} %param.23), channel_id=1, source_target_pairs={{0,1},{1,0},{2,3},{3,2},{4,5},{5,4},{6,7},{7,6},{8,9},{9,8},{10,11... | collective-permute-start | bytes 6291464 | tf_op jit(solution)/shard_map/ppermute | solution.py:100
  1.2 2.2 %copy-start = (bf16[16,256,4,128]{3,2,1,0:T(4,128)(2,1)S(1)}, bf16[16,256,4,128]{3,2,1,0:T(4,128)(2,1)}, u32[]{:S(2)}) copy-start(bf16[16,256,4,128]{3,2,1,0:T(4,128)(2,1)} %param.18) | copy-start | bytes 12582916
  3.4 2.2 %copy-start.1 = (bf16[16,256,4,128]{3,2,1,0:T(4,128)(2,1)S(1)}, bf16[16,256,4,128]{3,2,1,0:T(4,128)(2,1)}, u32[]{:S(2)}) copy-start(bf16[16,256,4,128]{3,2,1,0:T(4,128)(2,1)} %param.19) | copy-start | bytes 12582916
  5.5 0.9 copy-start.2
  6.5 0.7 copy-start.3
  7.2 0.7 copy-start.4
  7.9 0.7 copy-start.5
  15.7 8.8 %copy-start.10 = (f32[32,8]{0,1:T(8,128)S(1)}, f32[32,8]{0,1:T(8,128)}, u32[]{:S(2)}) copy-start(f32[32,8]{0,1:T(8,128)} %param.27) | copy-start | bytes 3076
  15.7 16.5 %copy-start.12 = (bf16[1024,1024]{1,0:T(8,128)(2,1)S(1)}, bf16[1024,1024]{1,0:T(8,128)(2,1)}, u32[]{:S(2)}) copy-start(bf16[1024,1024]{1,0:T(8,128)(2,1)} %param.23) | copy-start | bytes 6291460
  16.5 1.4 %collective-permute-start.1 = (bf16[16,4,1024]{2,0,1:T(8,128)(2,1)S(1)}, bf16[16,4,1024]{2,0,1:T(8,128)(2,1)S(1)}, u32[]{:S(2)}, u32[]{:S(2)}) collective-permute-start(bf16[16,4,1024]{2,0,1:T(8,128)(2,1)S(1)} %select_bitcast_fusion), channel_id=1, source_target_pairs={{0,1},{1,0},{2,3},{3,2},{4,5},{5,4},{6,7},{7,6},{8,9},{9,8},{10,11... | collective-permute-start | bytes 393224 | tf_op jit(solution)/shard_map/ppermute | solution.py:100
  18.7 8.8 %collective-permute-start.2 = (bf16[32,1024]{1,0:T(8,128)(2,1)S(1)}, bf16[32,1024]{1,0:T(8,128)(2,1)S(1)}, u32[]{:S(2)}, u32[]{:S(2)}) collective-permute-start(bf16[32,1024]{1,0:T(8,128)(2,1)S(1)} %get-tuple-element.26), channel_id=1, source_target_pairs={{1,9},{3,11},{5,13},{7,15},{9,1},{11,3},{13,5},{15,7},{17,25},{19,... | collective-permute-start | bytes 196616 | tf_op jit(solution)/shard_map/ppermute | solution.py:109
  19.4 32.7 %collective-permute-start.12 = (f32[1024]{0:T(1024)}, f32[1024]{0:T(1024)}, u32[]{:S(2)}, u32[]{:S(2)}) collective-permute-start(f32[1024]{0:T(1024)} %param.25), channel_id=1, source_target_pairs={{0,1},{1,0},{2,3},{3,2},{4,5},{5,4},{6,7},{7,6},{8,9},{9,8},{10,11... | collective-permute-start | bytes 12296 | tf_op jit(solution)/shard_map/ppermute | solution.py:100
  24.5 5.2 %collective-permute-start.5 = (bf16[32,1024]{1,0:T(8,128)(2,1)S(1)}, bf16[32,1024]{1,0:T(8,128)(2,1)S(1)}, u32[]{:S(2)}, u32[]{:S(2)}) collective-permute-start(bf16[32,1024]{1,0:T(8,128)(2,1)S(1)} %get-tuple-element.27), channel_id=1, source_target_pairs={{0,6},{1,15},{2,4},{3,13},{4,2},{5,11},{6,0},{7,9},{8,14},{9,7},{1... | collective-permute-start | bytes 196616 | tf_op jit(solution)/shard_map/ppermute | solution.py:109
  27.1 5.1 %collective-permute-start.4 = (bf16[32,1024]{1,0:T(8,128)(2,1)S(1)}, bf16[32,1024]{1,0:T(8,128)(2,1)S(1)}, u32[]{:S(2)}, u32[]{:S(2)}) collective-permute-start(bf16[32,1024]{1,0:T(8,128)(2,1)S(1)} %get-tuple-element.28), channel_id=1, source_target_pairs={{0,4},{1,13},{2,6},{3,15},{4,0},{5,9},{6,2},{7,11},{8,12},{9,5},{1... | collective-permute-start | bytes 196616 | tf_op jit(solution)/shard_map/ppermute | solution.py:109
  27.5 4.7 %collective-permute-start.3 = (bf16[32,1024]{1,0:T(8,128)(2,1)S(1)}, bf16[32,1024]{1,0:T(8,128)(2,1)S(1)}, u32[]{:S(2)}, u32[]{:S(2)}) collective-permute-start(bf16[32,1024]{1,0:T(8,128)(2,1)S(1)} %get-tuple-element.29), channel_id=1, source_target_pairs={{0,2},{1,11},{2,0},{3,9},{4,6},{5,15},{6,4},{7,13},{8,10},{9,3},{1... | collective-permute-start | bytes 196616 | tf_op jit(solution)/shard_map/ppermute | solution.py:109
  32.7 6.5 %copy-start.11 = (s32[32,8]{0,1:T(8,128)S(1)}, s32[32,8]{0,1:T(8,128)}, u32[]{:S(2)}) copy-start(s32[32,8]{0,1:T(8,128)} %param.26) | copy-start | bytes 3076
  32.7 7.3 %copy-start.9 = (bf16[32,1024]{1,0:T(8,128)(2,1)S(1)}, bf16[32,1024]{1,0:T(8,128)(2,1)}, u32[]{:S(2)}) copy-start(bf16[32,1024]{1,0:T(8,128)(2,1)} %param.24) | copy-start | bytes 196612
  32.7 11.5 %copy-start.6 = (bf16[2,1024,768]{2,1,0:T(8,128)(2,1)S(1)}, bf16[2,1024,768]{2,1,0:T(8,128)(2,1)}, u32[]{:S(2)}) copy-start(bf16[2,1024,768]{2,1,0:T(8,128)(2,1)} %param.28) | copy-start | bytes 9437188
  35.0 5.0 %collective-permute-start.8 = (bf16[32,2048]{1,0:T(8,128)(2,1)S(1)}, bf16[32,2048]{1,0:T(8,128)(2,1)S(1)}, u32[]{:S(2)}, u32[]{:S(2)}) collective-permute-start(bf16[32,2048]{1,0:T(8,128)(2,1)S(1)} %get-tuple-element.21), channel_id=1, source_target_pairs={{0,2},{1,11},{2,0},{3,9},{4,6},{5,15},{6,4},{7,13},{8,10},{9,3},{1... | collective-permute-start | bytes 393224 | tf_op jit(solution)/shard_map/ppermute | solution.py:109
  35.7 8.5 %collective-permute-start.10 = (bf16[32,2048]{1,0:T(8,128)(2,1)S(1)}, bf16[32,2048]{1,0:T(8,128)(2,1)S(1)}, u32[]{:S(2)}, u32[]{:S(2)}) collective-permute-start(bf16[32,2048]{1,0:T(8,128)(2,1)S(1)} %get-tuple-element.22), channel_id=1, source_target_pairs={{0,6},{1,15},{2,4},{3,13},{4,2},{5,11},{6,0},{7,9},{8,14},{9,7},{1... | collective-permute-start | bytes 393224 | tf_op jit(solution)/shard_map/ppermute | solution.py:109
  37.7 9.4 %collective-permute-start.9 = (bf16[32,2048]{1,0:T(8,128)(2,1)S(1)}, bf16[32,2048]{1,0:T(8,128)(2,1)S(1)}, u32[]{:S(2)}, u32[]{:S(2)}) collective-permute-start(bf16[32,2048]{1,0:T(8,128)(2,1)S(1)} %get-tuple-element.23), channel_id=1, source_target_pairs={{0,4},{1,13},{2,6},{3,15},{4,0},{5,9},{6,2},{7,11},{8,12},{9,5},{1... | collective-permute-start | bytes 393224 | tf_op jit(solution)/shard_map/ppermute | solution.py:109
  38.5 8.6 %collective-permute-start.7 = (bf16[32,2048]{1,0:T(8,128)(2,1)S(1)}, bf16[32,2048]{1,0:T(8,128)(2,1)S(1)}, u32[]{:S(2)}, u32[]{:S(2)}) collective-permute-start(bf16[32,2048]{1,0:T(8,128)(2,1)S(1)} %get-tuple-element.20), channel_id=1, source_target_pairs={{1,9},{3,11},{5,13},{7,15},{9,1},{11,3},{13,5},{15,7},{17,25},{19,... | collective-permute-start | bytes 393224 | tf_op jit(solution)/shard_map/ppermute | solution.py:109
  40.0 16.5 %collective-permute-start = (bf16[32,1024]{1,0:T(8,128)(2,1)S(1)}, bf16[32,1024]{1,0:T(8,128)(2,1)S(1)}, u32[]{:S(2)}, u32[]{:S(2)}) collective-permute-start(bf16[32,1024]{1,0:T(8,128)(2,1)S(1)} %copy-done.9), channel_id=1, source_target_pairs={{0,1},{1,0},{2,3},{3,2},{4,5},{5,4},{6,7},{7,6},{8,9},{9,8},{10,11... | collective-permute-start | bytes 196616 | tf_op jit(solution)/shard_map/ppermute | solution.py:100
  44.2 28.6 %collective-permute-start.17 = (bf16[2,1024,768]{2,1,0:T(8,128)(2,1)S(1)}, bf16[2,1024,768]{2,1,0:T(8,128)(2,1)}, u32[]{:S(2)}, u32[]{:S(2)}) collective-permute-start(bf16[2,1024,768]{2,1,0:T(8,128)(2,1)S(1)} %copy-done.6), channel_id=1, source_target_pairs={{0,1},{1,0},{2,3},{3,2},{4,5},{5,4},{6,7},{7,6},{8,9},{9,8},{10,11... | collective-permute-start | bytes 9437192 | tf_op jit(solution)/shard_map/ppermute | solution.py:100
  47.1 29.3 %collective-permute-start.18 = (bf16[2,1024,768]{2,1,0:T(8,128)(2,1)}, bf16[2,1024,768]{2,1,0:T(8,128)(2,1)}, u32[]{:S(2)}, u32[]{:S(2)}) collective-permute-start(bf16[2,1024,768]{2,1,0:T(8,128)(2,1)} %param.29), channel_id=1, source_target_pairs={{0,1},{1,0},{2,3},{3,2},{4,5},{5,4},{6,7},{7,6},{8,9},{9,8},{10,11... | collective-permute-start | bytes 9437192 | tf_op jit(solution)/shard_map/ppermute | solution.py:100
  47.2 9.4 %copy-start.8 = (f32[32,2048]{1,0:T(8,128)}, f32[32,2048]{1,0:T(8,128)S(1)}, u32[]{:S(2)}) copy-start(f32[32,2048]{1,0:T(8,128)S(1)} %convert_add_fusion.1) | copy-start | bytes 786436
  47.2 8.4 %collective-permute-start.11 = (f32[32,2048]{1,0:T(8,128)S(1)}, f32[32,2048]{1,0:T(8,128)}, u32[]{:S(2)}, u32[]{:S(2)}) collective-permute-start(f32[32,2048]{1,0:T(8,128)S(1)} %convert_add_fusion.1), channel_id=1, source_target_pairs={{0,1},{1,0},{2,3},{3,2},{4,5},{5,4},{6,7},{7,6},{8,9},{9,8},{10,11... | collective-permute-start | bytes 786440 | tf_op jit(solution)/shard_map/ppermute | solution.py:100
  60.0 4.1 %collective-permute-start.13 = (bf16[32,2176]{1,0:T(8,128)(2,1)S(1)}, bf16[32,2176]{1,0:T(8,128)(2,1)}, u32[]{:S(2)}, u32[]{:S(2)}) collective-permute-start(bf16[32,2176]{1,0:T(8,128)(2,1)S(1)} %concatenate.31), channel_id=1, source_target_pairs={{1,9},{3,11},{5,13},{7,15},{9,1},{11,3},{13,5},{15,7},{17,25},{19,... | collective-permute-start | bytes 417800 | tf_op jit(solution)/shard_map/ppermute | solution.py:109
  61.3 6.8 %collective-permute-start.16 = (bf16[32,2176]{1,0:T(8,128)(2,1)S(1)}, bf16[32,2176]{1,0:T(8,128)(2,1)S(1)}, u32[]{:S(2)}, u32[]{:S(2)}) collective-permute-start(bf16[32,2176]{1,0:T(8,128)(2,1)S(1)} %concatenate.31), channel_id=1, source_target_pairs={{0,6},{1,15},{2,4},{3,13},{4,2},{5,11},{6,0},{7,9},{8,14},{9,7},{1... | collective-permute-start | bytes 417800 | tf_op jit(solution)/shard_map/ppermute | solution.py:109
  61.7 10.7 %collective-permute-start.15 = (bf16[32,2176]{1,0:T(8,128)(2,1)S(1)}, bf16[32,2176]{1,0:T(8,128)(2,1)S(1)}, u32[]{:S(2)}, u32[]{:S(2)}) collective-permute-start(bf16[32,2176]{1,0:T(8,128)(2,1)S(1)} %concatenate.31), channel_id=1, source_target_pairs={{0,4},{1,13},{2,6},{3,15},{4,0},{5,9},{6,2},{7,11},{8,12},{9,5},{1... | collective-permute-start | bytes 417800 | tf_op jit(solution)/shard_map/ppermute | solution.py:109
  64.1 8.4 %collective-permute-start.14 = (bf16[32,2176]{1,0:T(8,128)(2,1)S(1)}, bf16[32,2176]{1,0:T(8,128)(2,1)S(1)}, u32[]{:S(2)}, u32[]{:S(2)}) collective-permute-start(bf16[32,2176]{1,0:T(8,128)(2,1)S(1)} %concatenate.31), channel_id=1, source_target_pairs={{0,2},{1,11},{2,0},{3,9},{4,6},{5,15},{6,4},{7,13},{8,10},{9,3},{1... | collective-permute-start | bytes 417800 | tf_op jit(solution)/shard_map/ppermute | solution.py:109
  68.1 17.6 %collective-permute-start.19 = (bf16[2,768,1024]{2,1,0:T(8,128)(2,1)}, bf16[2,768,1024]{2,1,0:T(8,128)(2,1)S(1)}, u32[]{:S(2)}, u32[]{:S(2)}) collective-permute-start(bf16[2,768,1024]{2,1,0:T(8,128)(2,1)} %param.30), channel_id=1, source_target_pairs={{0,1},{1,0},{2,3},{3,2},{4,5},{5,4},{6,7},{7,6},{8,9},{9,8},{10,11... | collective-permute-start | bytes 9437192 | tf_op jit(solution)/shard_map/ppermute | solution.py:100
  80.4 2.4 %copy-start.7 = (bf16[2,768,1024]{2,1,0:T(8,128)(2,1)S(1)}, bf16[2,768,1024]{2,1,0:T(8,128)(2,1)}, u32[]{:S(2)}) copy-start(bf16[2,768,1024]{2,1,0:T(8,128)(2,1)} %param.30) | copy-start | bytes 9437188
  86.5 6.2 %collective-permute-start.21 = (bf16[32,2048]{1,0:T(8,128)(2,1)S(1)}, bf16[32,2048]{1,0:T(8,128)(2,1)S(1)}, u32[]{:S(2)}, u32[]{:S(2)}) collective-permute-start(bf16[32,2048]{1,0:T(8,128)(2,1)S(1)} %get-tuple-element.17), channel_id=1, source_target_pairs={{0,2},{1,11},{2,0},{3,9},{4,6},{5,15},{6,4},{7,13},{8,10},{9,3},{1... | collective-permute-start | bytes 393224 | tf_op jit(solution)/shard_map/ppermute | solution.py:109
  88.8 5.9 %collective-permute-start.23 = (bf16[32,2048]{1,0:T(8,128)(2,1)S(1)}, bf16[32,2048]{1,0:T(8,128)(2,1)S(1)}, u32[]{:S(2)}, u32[]{:S(2)}) collective-permute-start(bf16[32,2048]{1,0:T(8,128)(2,1)S(1)} %get-tuple-element.18), channel_id=1, source_target_pairs={{0,6},{1,15},{2,4},{3,13},{4,2},{5,11},{6,0},{7,9},{8,14},{9,7},{1... | collective-permute-start | bytes 393224 | tf_op jit(solution)/shard_map/ppermute | solution.py:109
  89.6 5.1 %collective-permute-start.22 = (bf16[32,2048]{1,0:T(8,128)(2,1)S(1)}, bf16[32,2048]{1,0:T(8,128)(2,1)S(1)}, u32[]{:S(2)}, u32[]{:S(2)}) collective-permute-start(bf16[32,2048]{1,0:T(8,128)(2,1)S(1)} %get-tuple-element.19), channel_id=1, source_target_pairs={{0,4},{1,13},{2,6},{3,15},{4,0},{5,9},{6,2},{7,11},{8,12},{9,5},{1... | collective-permute-start | bytes 393224 | tf_op jit(solution)/shard_map/ppermute | solution.py:109
  90.3 4.4 %collective-permute-start.20 = (bf16[32,2048]{1,0:T(8,128)(2,1)S(1)}, bf16[32,2048]{1,0:T(8,128)(2,1)S(1)}, u32[]{:S(2)}, u32[]{:S(2)}) collective-permute-start(bf16[32,2048]{1,0:T(8,128)(2,1)S(1)} %get-tuple-element.16), channel_id=1, source_target_pairs={{1,9},{3,11},{5,13},{7,15},{9,1},{11,3},{13,5},{15,7},{17,25},{19,... | collective-permute-start | bytes 393224 | tf_op jit(solution)/shard_map/ppermute | solution.py:109
  94.8 13.1 %collective-permute-start.24 = (f32[32,1024]{1,0:T(8,128)S(1)}, f32[32,1024]{1,0:T(8,128)S(1)}, u32[]{:S(2)}, u32[]{:S(2)}) collective-permute-start(f32[32,1024]{1,0:T(8,128)S(1)} %slice.178), channel_id=1, source_target_pairs={{0,1},{1,0},{2,3},{3,2},{4,5},{5,4},{6,7},{7,6},{8,9},{9,8},{10,11... | collective-permute-start | bytes 393224 | tf_op jit(solution)/shard_map/ppermute | solution.py:100

commit v2 on v0

v2 whole, which is shorter than its diff:
```python
import functools
import math

import jax
import jax.numpy as jnp
from jax import lax
from jax.experimental import pallas as pl
from jax.experimental.pallas import tpu as pltpu
from jax.sharding import PartitionSpec as P

F32 = jnp.float32
BF16 = jnp.bfloat16
VMEM = pl.BlockSpec(memory_space=pltpu.VMEM)
SMEM = pl.BlockSpec(memory_space=pltpu.SMEM)
ANY = pl.BlockSpec(memory_space=pl.ANY)
MIB = 1024 * 1024


def choose(core, values):
    result = jnp.int32(values[0])
    for c in range(1, len(values)):
        result = jnp.where(core == c, jnp.int32(values[c]), result)
    return result


def turned(value, m, cores):
    band = value.shape[0] // cores
    pieces = [value[i * band : (i + 1) * band] for i in range(cores)]
    return jnp.concatenate([pieces[i ^ m] for i in range(cores)], axis=0) if m else value


def from_natural(core, value, cores):
    result = value
    for c in range(1, cores):
        result = jnp.where(core == c, turned(value, c, cores), result)
    return result


def attend_kernel(
    kv_heads, offset, len_ref, place_ref, q_ref, k_hbm, v_hbm, ik_ref, iv_ref, *refs
):
    cores, slots = len(offset), len(offset[0])
    out_refs = refs[:cores]
    k_buf, v_buf, mask_ref, all_ref, sems = refs[cores:]
    rows, heads, size = q_ref.shape
    span = k_buf.shape[1]
    per = heads // kv_heads
    block = heads // (cores * slots)
    scale = size ** (-0.5) * math.log2(math.e)
    step = 2

    def copies(r):
        return (
            pltpu.make_async_copy(k_hbm.at[r], k_buf.at[r], sems.at[0, r]),
            pltpu.make_async_copy(v_hbm.at[r], v_buf.at[r], sems.at[1, r]),
        )

    for r in range(rows):
        for copy in copies(r):
            copy.start()
    column = lax.broadcasted_iota(jnp.int32, (heads, span), 1)
    head = lax.broadcasted_iota(jnp.int32, (heads, span), 0)
    mask_ref[...] = jnp.where(lax.rem(column, kv_heads) == head // per, column, 1 << 30)

    def spread(value):
        return jnp.concatenate(
            [
                jnp.broadcast_to(value[g : g + 1, :].astype(F32), (per, size))
                for g in range(kv_heads)
            ],
            axis=0,
        )

    def one(r):
        q = q_ref[r]
        scores = lax.dot_general(
            q, k_buf[r], (((1,), (1,)), ((), ())), preferred_element_type=F32
        )
        scores = jnp.where(mask_ref[...] < len_ref[r] * kv_heads, scores, -1e30)
        own = jnp.sum(q.astype(F32) * spread(ik_ref[r]), axis=1, keepdims=True)
        peak = jnp.maximum(jnp.max(scores, axis=1, keepdims=True), own)
        expo = jnp.exp2((scores - peak) * scale)
        fresh = jnp.exp2((own - peak) * scale)
        total = jnp.sum(expo, axis=1, keepdims=True) + fresh
        accum = jnp.dot(expo.astype(BF16), v_buf[r], preferred_element_type=F32)
        all_ref[pl.ds(r, heads, stride=rows), :] = (accum + fresh * spread(iv_ref[r])) / total

    def body(i, carry):
        for j in range(step):
            for copy in copies(i * step + j):
                copy.wait()
        for j in range(step):
            one(i * step + j)
        return carry

    lax.fori_loop(0, rows // step, body, 0)
    me, core = place_ref[0], place_ref[1]
    for m in range(cores):
        for s in range(slots):
            which = me ^ choose(core, [offset[c ^ m][s] for c in range(cores)])
            for h in range(block):
                at = pl.multiple_of((which * block + h) * rows, rows)
                out_refs[m][s, :, h * size : (h + 1) * size] = all_ref[
                    pl.ds(at, rows), :
                ].astype(BF16)


def attend(query, keys, values, fresh_key, fresh_value, lengths, place, offset):
    rows, heads, size = query.shape
    positions, kv_heads = keys.shape[1:3]
    span = positions * kv_heads
    cores, slots = len(offset), len(offset[0])
    width = heads * size // (cores * slots)
    return pl.pallas_call(
        functools.partial(attend_kernel, kv_heads, offset),
        out_shape=[jax.ShapeDtypeStruct((slots, rows, width), BF16)] * cores,
        in_specs=[SMEM, SMEM, VMEM, ANY, ANY, VMEM, VMEM],
        out_specs=[VMEM] * cores,
        scratch_shapes=[
            pltpu.VMEM((rows, span, size), BF16),
            pltpu.VMEM((rows, span, size), BF16),
            pltpu.VMEM((heads, span), jnp.int32),
            pltpu.VMEM((heads * rows, size), F32),
            pltpu.SemaphoreType.DMA((2, rows)),
        ],
        compiler_params=pltpu.CompilerParams(vmem_limit_bytes=60 * MIB),
    )(
        lengths,
        place,
        query,
        keys.reshape(rows, span, size),
        values.reshape(rows, span, size),
        fresh_key,
        fresh_value,
    )


def take_slots(offset, place_ref, own_ref, moved_refs):
    core = place_ref[1]
    result = []
    for s, ref in enumerate(moved_refs):
        block = ref[...]
        for c in range(len(offset)):
            if offset[c][s] == 0:
                block = jnp.where(core == c, own_ref[...], block)
        result.append(block)
    return jnp.concatenate(result, axis=0)


def project_kernel(offset, place_ref, own_ref, *refs):
    cores, slots = len(offset), len(offset[0])
    moved_refs, w_refs = refs[:slots], refs[slots : slots + cores]
    out_refs = refs[slots + cores : 2 * slots + cores]
    left = take_slots(offset, place_ref, own_ref, moved_refs)
    rows, part = own_ref.shape[0], w_refs[0].shape[1]
    for j in range(cores):
        product = jnp.dot(left, w_refs[j][...], preferred_element_type=F32).astype(BF16)
        for s in range(slots):
            out_refs[s][:, j * part : (j + 1) * part] = product[s * rows : (s + 1) * rows]


def project(place, own, moved, weights, offset):
    rows = own.shape[0]
    depth, part = weights[0].shape
    cores, slots = len(offset), len(offset[0])
    return pl.pallas_call(
        functools.partial(project_kernel, offset),
        out_shape=[jax.ShapeDtypeStruct((rows, part * cores), BF16)] * slots,
        in_specs=[SMEM, VMEM] + [VMEM] * (slots + cores),
        out_specs=[VMEM] * slots,
        compiler_params=pltpu.CompilerParams(vmem_limit_bytes=12 * MIB),
    )(place, own, *moved, *weights)


def norm_kernel(cores, experts, place_ref, *refs):
    sums_refs, stream_refs, gain_refs = refs[:cores], refs[cores : 2 * cores], refs[2 * cores : 3 * cores]
    ids_ref, routes_ref, mixed_ref, out_ref = refs[3 * cores :]
    rows, part = stream_refs[0].shape
    width = part * cores
    core = place_ref[1]
    squares = 0.0
    mixed = []
    for j in range(cores):
        block = from_natural(core, stream_refs[j][...].astype(F32), cores)
        for m in range(cores):
            other = sums_refs[m][:, (j ^ m) * part : ((j ^ m) + 1) * part]
            block = block + turned(other, m, cores)
        mixed.append(block)
        squares = squares + jnp.sum(block * block, axis=1, keepdims=True)
    mixed_ref[...] = mixed[0]
    scale = lax.rsqrt(squares / width + 1e-06)
    for j in range(cores):
        out_ref[:, j * part : (j + 1) * part] = (mixed[j] * scale * gain_refs[j][...]).astype(BF16)
    picks = ids_ref.shape[0]
    extra = out_ref.shape[1] - width
    ids, routes = ids_ref[...], routes_ref[...]
    shares = routes / jnp.sum(routes, axis=0, keepdims=True)
    line = lax.broadcasted_iota(jnp.int32, (extra, rows), 0)
    line = jnp.where(line < experts, line, line - experts)
    combine = jnp.zeros((extra, rows), F32)
    for k in range(picks):
        combine = jnp.where(ids[k : k + 1, :] == line, shares[k : k + 1, :], combine)
    combine = jnp.concatenate([combine, jnp.zeros((extra, 128 - rows), F32)], axis=1)
    combine = from_natural(core, jnp.transpose(combine)[:rows], cores)
    upper = combine.astype(BF16)
    lower = (combine - upper.astype(F32)).astype(BF16)
    lane = lax.broadcasted_iota(jnp.int32, (rows, extra), 1)
    out_ref[:, width:] = jnp.where(lane < experts, upper.astype(F32), lower.astype(F32)).astype(BF16)


def normalise(place, sums, stream, gain, ids, routes, experts):
    rows, part = stream[0].shape
    cores = len(sums)
    extra = -(-2 * experts // 128) * 128
    return pl.pallas_call(
        functools.partial(norm_kernel, cores, experts),
        out_shape=(
            jax.ShapeDtypeStruct((rows, part), F32),
            jax.ShapeDtypeStruct((rows, part * cores + extra), BF16),
        ),
        in_specs=[SMEM] + [VMEM] * (3 * cores + 2),
        out_specs=(VMEM, VMEM),
        compiler_params=pltpu.CompilerParams(vmem_limit_bytes=8 * MIB),
    )(place, *sums, *stream, *gain, ids.T, routes.T)


def expert_kernel(offset, devs, place_ref, own_ref, *refs):
    cores, slots = len(offset), len(offset[0])
    moved_refs, refs = refs[:slots], refs[slots:]
    gate_refs, up_refs, down_refs = refs[:cores], refs[cores : 2 * cores], refs[2 * cores : 3 * cores]
    out_refs = refs[3 * cores : 3 * cores + slots]
    gate_buf, up_buf, down_buf, sems = refs[3 * cores + slots :]
    local, part, hidden = gate_refs[0].shape
    rows = own_ref.shape[0]
    width = part * cores

    def copy(kind, j, e):
        source = (gate_refs, up_refs, down_refs)[kind][j]
        target = (gate_buf, up_buf, down_buf)[kind]
        return pltpu.make_async_copy(source.at[e], target.at[j, e], sems.at[kind, j, e])

    for e in range(local):
        for kind in range(3):
            for j in range(cores):
                copy(kind, j, e).start()
    tokens = take_slots(offset, place_ref, own_ref, moved_refs)
    tail = tokens[:, width:].astype(F32)
    lane = lax.broadcasted_iota(jnp.int32, tail.shape, 1)
    experts = local * devs
    total = [0.0] * cores
    for e in range(local):
        mine = place_ref[0] * local + e
        share = jnp.sum(
            jnp.where((lane == mine) | (lane == mine + experts), tail, 0.0), axis=1, keepdims=True
        )
        sums = []
        for kind in range(2):
            value = 0.0
            for j in range(cores):
                copy(kind, j, e).wait()
                value = value + jnp.dot(
                    tokens[:, j * part : (j + 1) * part],
                    (gate_buf, up_buf)[kind][j, e],
                    preferred_element_type=F32,
                )
            sums.append(value)
        gate, up = sums
        active = (gate / (1.0 + jnp.exp(-gate)) * up * share).astype(BF16)
        for j in range(cores):
            copy(2, j, e).wait()
            total[j] = total[j] + jnp.dot(active, down_buf[j, e], preferred_element_type=F32)
    for j in range(cores):
        for s in range(slots):
            out_refs[s][:, j * part : (j + 1) * part] = total[j][
                s * rows : (s + 1) * rows
            ].astype(BF16)


def apply_experts(place, own, moved, gate, up, down, offset, devs):
    cores, slots = len(offset), len(offset[0])
    local, part, hidden = gate[0].shape
    rows = own.shape[0]
    return pl.pallas_call(
        functools.partial(expert_kernel, offset, devs),
        out_shape=[jax.ShapeDtypeStruct((rows, part * cores), BF16)] * slots,
        in_specs=[SMEM, VMEM] + [VMEM] * slots + [ANY] * (3 * cores),
        out_specs=[VMEM] * slots,
        scratch_shapes=[
            pltpu.VMEM((cores, local, part, hidden), BF16),
            pltpu.VMEM((cores, local, part, hidden), BF16),
            pltpu.VMEM((cores, local, hidden, part), BF16),
            pltpu.SemaphoreType.DMA((3, cores, local)),
        ],
        compiler_params=pltpu.CompilerParams(vmem_limit_bytes=56 * MIB),
    )(place, own, *moved, *gate, *up, *down)


def per_device(
    query,
    stored_keys,
    stored_values,
    incoming_key,
    incoming_value,
    lengths,
    out_weight,
    residual,
    norm_gain,
    expert_ids,
    route_weights,
    w_gate,
    w_up,
    w_down,
):
    devs = lax.axis_size("dev")
    cores = lax.axis_size("pair")
    me = lax.axis_index("dev")
    core = lax.axis_index("pair")
    slots = devs // cores
    offset = [[c * slots + s for s in range(slots)] for c in range(cores)]
    place = jnp.stack([me, core]).astype(jnp.int32)
    rows, part = residual.shape
    barrier = lax.optimization_barrier

    def from_core(value, m):
        return lax.ppermute(value, "pair", [(c, c ^ m) for c in range(cores)])

    def gathered(value):
        return [value] + [from_core(value, m) for m in range(1, cores)]

    def swap(value, s):
        pairs = [
            (d * cores + c, (d ^ offset[c][s]) * cores + c)
            for d in range(devs)
            for c in range(cores)
            if offset[c][s]
        ]
        return lax.ppermute(value, ("dev", "pair"), pairs)

    own_slot = [[c for c in range(cores) if offset[c][s] == 0] for s in range(slots)]

    def total_of(own, moved):
        result = 0.0
        for s in range(slots):
            block = moved[s]
            for c in own_slot[s]:
                block = jnp.where(core == c, own[s], block)
            result = result + block.astype(F32)
        return result

    def own_block(blocks):
        return blocks[[s for s in range(slots) if own_slot[s]][0]]

    stream = gathered(residual)
    gain = gathered(norm_gain.reshape(1, part))
    wg = gathered(w_gate)
    wu = gathered(w_up)
    attended = attend(
        query, stored_keys, stored_values, incoming_key, incoming_value, lengths, place, offset
    )
    attended, wg, wu, stream, gain = barrier((attended, wg, wu, stream, gain))
    held = [attended[0]] + [from_core(attended[m], m) for m in range(1, cores)]
    held, out_weight, w_down = barrier((held, out_weight, w_down))
    wo = gathered(out_weight)
    outgoing = [jnp.concatenate([h[s] for h in held], axis=0) for s in range(slots)]
    arrived = [swap(outgoing[s], s) for s in range(slots)]
    arrived, wo, w_down = barrier((arrived, wo, w_down))
    wd = gathered(w_down)
    partial = project(place, own_block(outgoing), arrived, wo, offset)
    sums = total_of(partial, [swap(partial[s], s) for s in range(slots)])
    sums, wd = barrier((sums, wd))
    mixed, packed = normalise(
        place, gathered(sums), stream, gain, expert_ids, route_weights, w_gate.shape[0] * devs
    )
    tokens = [swap(packed, s) for s in range(slots)]
    produced = apply_experts(place, packed, tokens, wg, wu, wd, offset, devs)
    back = total_of(produced, [swap(produced[s], s) for s in range(slots)])
    result = mixed + back[:, :part]
    for m in range(1, cores):
        other = from_core(back[:, m * part : (m + 1) * part], m)
        result = result + turned(other, m, cores)
    return from_natural(core, result, cores).astype(BF16)


def solution(mesh):
    in_specs = (
        P(("groups", "dev", "pair"), None, None),
        P(("groups", "dev", "pair"), None, None, None),
        P(("groups", "dev", "pair"), None, None, None),
        P(("groups", "dev", "pair"), None, None),
        P(("groups", "dev", "pair"), None, None),
        P(("groups", "dev", "pair")),
        P("dev", "pair"),
        P(("groups", "dev"), "pair"),
        P("pair"),
        P(("groups", "dev"), None),
        P(("groups", "dev"), None),
        P("dev", "pair", None),
        P("dev", "pair", None),
        P("dev", None, "pair"),
    )
    out_specs = P(("groups", "dev"), "pair")
    return jax.shard_map(
        per_device, mesh=mesh, in_specs=in_specs, out_specs=out_specs, check_vma=False
    )
```

time: 200 us -> 89.3 us (0.45)
  waiting for transfers between devices: 101 us -> 27.3 us
  blocking collectives: 50.9 us -> 0 us
  starting transfers between devices: 5.96 us -> 35.4 us
  Pallas kernels: 0 us -> 21.3 us
  matrix products: 17.4 us -> 0 us
  between operations: 13.6 us -> 0.27 us
  local copies, waits for them, and re-layouts: 5.52 us -> 2.24 us
  other arithmetic: 5.45 us -> 2.43 us
    reduce_scatter x1 -> x0, waiting for transfers between devices: 61.6 us -> none  [per_device(): lax.psum_scatter(jnp.dot(regrouped, out_weight, preferred_element_type=jn...]
    all_to_all x2 -> x0, blocking collectives: 46 us -> none  [the longest x1 24.1 us: per_device(): lax.all_to_all(outgoing, 'dev', split_axis=0, concat_axis=0, tiled=True)]
    ppermute x0 -> x25, starting transfers between devices: none -> 35.4 us  [the longest x9 17.8 us: from_core(): return lax.ppermute(value, 'pair', [(c, c ^ m) for c in range(cores)])]
    ppermute x0 -> x25, waiting for transfers between devices: none -> 27.3 us  [the longest x16 24 us: swap(): return lax.ppermute(value, ('dev', 'pair'), pairs)]
    pallas_call x0 -> x4, Pallas kernels: none -> 21.3 us  [the longest x1 9.88 us: attend(): pl.pallas_call(functools.partial(attend_kernel, kv_heads, offset), out_sh...]
    all_to_all x1 -> x0, waiting for transfers between devices: 20.5 us -> none  [per_device(): lax.all_to_all(produced.astype(jnp.bfloat16), 'dev', split_axis=0, concat...]
    psum x1 -> x0, waiting for transfers between devices: 19.1 us -> none  [per_device(): lax.psum(up.astype(jnp.bfloat16), 'pair').astype(jnp.float32)]
    dot_general x8 -> x0, matrix products: 17.4 us -> none  [the longest x1 3.71 us: per_device(): jnp.einsum('bgjd,btgd->bgjt', grouped_queries, stored_keys, preferred_ele...]
  transfers between devices with their start and end apart: 3 -> 25, of which waited for: 3 -> 13; matrix products, arithmetic and copies ran while one was open for 1% -> 2% of each run, Pallas kernels for 0% -> 13%
where the time goes in v2:
time: 89.3 us; the launch traced here: 89 us
  starting transfers between devices  35.4 us (40%)
  waiting for transfers between devices  27.3 us (31%)
  Pallas kernels  21.3 us (24%)
  other arithmetic  2.43 us (3%)
  local copies, waits for them, and re-layouts  2.24 us (3%)
    ppermute x16, waiting for transfers between devices, swap(): return lax.ppermute(value, ('dev', 'pair'), pairs)  24 us
    ppermute x9, starting transfers between devices, from_core(): return lax.ppermute(value, 'pair', [(c, c ^ m) for c in range(cores)])  17.8 us
    ppermute x16, starting transfers between devices, swap(): return lax.ppermute(value, ('dev', 'pair'), pairs)  17.6 us
    pallas_call x1, Pallas kernels, attend(): pl.pallas_call(functools.partial(attend_kernel, kv_heads, offset), out_sh...  9.88 us
    pallas_call x1, Pallas kernels, apply_experts(): pl.pallas_call(functools.partial(expert_kernel, offset, devs), out_shape=...  9.48 us
    ppermute x9, waiting for transfers between devices, from_core(): return lax.ppermute(value, 'pair', [(c, c ^ m) for c in range(cores)])  3.36 us
  transfers between devices with their start and end apart: 25, of which 13 were waited for; matrix products, arithmetic and copies ran while one was open for 2% of the time, Pallas kernels for 13%

profile of v2, /device:TPU:0, one launch (start us, length us, event | category | flops | bytes accessed | tf_op | source)
XLA Modules:
  0.0 89.0 jit_solution(14647964802708306059)
XLA Ops:
  0.0 0.5 collective-permute-start
  0.5 0.1 collective-permute-start.1
  0.5 0.5 collective-permute-start.3
  1.0 0.1 collective-permute-start.2
  1.0 0.7 pad_add_fusion.place_ref
  1.7 9.9 %shard_map.136 = (bf16[4,16,1024]{2,1,0:T(8,128)(2,1)}, bf16[4,16,1024]{2,1,0:T(8,128)(2,1)}) custom-call(s32[16]{0:T(128)} %len_ref.1, s32[2]{0:T(128)} %pad_add_fusion.place_ref, bf16[16,64,128]{2,1,0:T(8,128)(2,1)} %q_ref.1, bf16[16,1024,128]{2,1,0:T(8,128)(2,1)} %bitcast.27, bf16[16,1024,128]{2,1,0:T(8,128)(2,1)} %bitcast.28, ...), custom_call_target="tpu_custom_call" | custom-call | tf_op jit(solution)/shard_map/pallas_call | solution.py:114
  11.7 0.5 collective-permute-start.4
  12.2 1.2 %collective-permute-done.4 = bf16[4,16,1024]{2,1,0:T(8,128)(2,1)S(1)} collective-permute-done((bf16[4,16,1024]{2,1,0:T(8,128)(2,1)}, bf16[4,16,1024]{2,1,0:T(8,128)(2,1)S(1)}, u32[]{:S(2)}, u32[]{:S(2)}) %collective-permute-start.4) | collective-permute-done | bytes 131104 | tf_op jit(solution)/shard_map/ppermute | solution.py:325
  13.4 0.4 collective-permute-start.9
  13.7 0.8 slice_bitcast_fusion
  14.6 2.7 %collective-permute-start.6 = (bf16[32,1024]{1,0:T(8,128)(2,1)S(1)}, bf16[32,1024]{1,0:T(8,128)(2,1)S(1)}, u32[]{:S(2)}, u32[]{:S(2)}) collective-permute-start(bf16[32,1024]{1,0:T(8,128)(2,1)S(1)} %pad_maximum_fusion.1), channel_id=1, source_target_pairs={{0,2},{1,11},{2,0},{3,9},{4,6},{5,15},{6,4},{7,13},{8,10},{9,3},{1... | collective-permute-start | bytes 196616 | tf_op jit(solution)/shard_map/ppermute | solution.py:337
  17.3 1.6 %collective-permute-start.7 = (bf16[32,1024]{1,0:T(8,128)(2,1)S(1)}, bf16[32,1024]{1,0:T(8,128)(2,1)S(1)}, u32[]{:S(2)}, u32[]{:S(2)}) collective-permute-start(bf16[32,1024]{1,0:T(8,128)(2,1)S(1)} %pad_maximum_fusion.2), channel_id=1, source_target_pairs={{0,4},{1,13},{2,6},{3,15},{4,0},{5,9},{6,2},{7,11},{8,12},{9,5},{1... | collective-permute-start | bytes 196616 | tf_op jit(solution)/shard_map/ppermute | solution.py:337
  18.9 0.7 collective-permute-start.5
  19.6 0.1 collective-permute-start.8
  19.6 2.3 %collective-permute-done.7.refs_2_ = bf16[32,1024]{1,0:T(8,128)(2,1)S(1)} collective-permute-done((bf16[32,1024]{1,0:T(8,128)(2,1)S(1)}, bf16[32,1024]{1,0:T(8,128)(2,1)S(1)}, u32[]{:S(2)}, u32[]{:S(2)}) %collective-permute-start.7) | collective-permute-done | bytes 65568 | tf_op jit(solution)/shard_map/ppermute | solution.py:337
  22.0 3.2 %collective-permute-done.8.refs_3_ = bf16[32,1024]{1,0:T(8,128)(2,1)S(1)} collective-permute-done((bf16[32,1024]{1,0:T(8,128)(2,1)S(1)}, bf16[32,1024]{1,0:T(8,128)(2,1)S(1)}, u32[]{:S(2)}, u32[]{:S(2)}) %collective-permute-start.8) | collective-permute-done | bytes 65568 | tf_op jit(solution)/shard_map/ppermute | solution.py:337
  25.2 4.5 %collective-permute-start.14 = (bf16[2,768,1024]{2,1,0:T(8,128)(2,1)}, bf16[2,768,1024]{2,1,0:T(8,128)(2,1)}, u32[]{:S(2)}, u32[]{:S(2)}) collective-permute-start(bf16[2,768,1024]{2,1,0:T(8,128)(2,1)} %refs_8_), channel_id=1, source_target_pairs={{0,1},{1,0},{2,3},{3,2},{4,5},{5,4},{6,7},{7,6},{8,9},{9,8},{10,11... | collective-permute-start | bytes 9437192 | tf_op jit(solution)/shard_map/ppermute | solution.py:325
  29.7 1.3 %shard_map.137 = (bf16[32,2048]{1,0:T(8,128)(2,1)S(1)}, bf16[32,2048]{1,0:T(8,128)(2,1)S(1)}, bf16[32,2048]{1,0:T(8,128)(2,1)S(1)}, bf16[32,2048]{1,0:T(8,128)(2,1)S(1)}) custom-call(s32[2]{0:T(128)S(1)} %copy-done.3, bf16[32,1024]{1,0:T(8,128)(2,1)S(1)} %pad_maximum_fusion.own_ref, bf16[32,1024]{1,0:T(8,128)(2,1)S(1)} %collective-permute-done.5.refs_0_, ...), custom_call_target="tpu_custom_call" | custom-call | tf_op jit(solution)/shard_map/pallas_call | solution.py:166
  31.0 0.6 collective-permute-start.11
  31.6 3.0 %collective-permute-start.13 = (bf16[32,2048]{1,0:T(8,128)(2,1)S(1)}, bf16[32,2048]{1,0:T(8,128)(2,1)S(1)}, u32[]{:S(2)}, u32[]{:S(2)}) collective-permute-start(bf16[32,2048]{1,0:T(8,128)(2,1)S(1)} %get-tuple-element.58), channel_id=1, source_target_pairs={{0,6},{1,15},{2,4},{3,13},{4,2},{5,11},{6,0},{7,9},{8,14},{9,7},{1... | collective-permute-start | bytes 393224 | tf_op jit(solution)/shard_map/ppermute | solution.py:337
  34.5 0.7 collective-permute-start.10
  35.2 1.2 %collective-permute-done.11 = bf16[32,2048]{1,0:T(8,128)(2,1)S(1)} collective-permute-done((bf16[32,2048]{1,0:T(8,128)(2,1)S(1)}, bf16[32,2048]{1,0:T(8,128)(2,1)S(1)}, u32[]{:S(2)}, u32[]{:S(2)}) %collective-permute-start.11) | collective-permute-done | bytes 131104 | tf_op jit(solution)/shard_map/ppermute | solution.py:337
  36.4 2.7 %collective-permute-done.12 = bf16[32,2048]{1,0:T(8,128)(2,1)S(1)} collective-permute-done((bf16[32,2048]{1,0:T(8,128)(2,1)S(1)}, bf16[32,2048]{1,0:T(8,128)(2,1)S(1)}, u32[]{:S(2)}, u32[]{:S(2)}) %collective-permute-start.12) | collective-permute-done | bytes 131104 | tf_op jit(solution)/shard_map/ppermute | solution.py:337
  39.2 3.6 %collective-permute-done.13 = bf16[32,2048]{1,0:T(8,128)(2,1)S(1)} collective-permute-done((bf16[32,2048]{1,0:T(8,128)(2,1)S(1)}, bf16[32,2048]{1,0:T(8,128)(2,1)S(1)}, u32[]{:S(2)}, u32[]{:S(2)}) %collective-permute-start.13) | collective-permute-done | bytes 131104 | tf_op jit(solution)/shard_map/ppermute | solution.py:337
  42.8 0.1 convert_add_fusion.1.refs_0_
  42.9 1.9 %collective-permute-start.15 = (f32[32,2048]{1,0:T(8,128)S(1)}, f32[32,2048]{1,0:T(8,128)S(1)}, u32[]{:S(2)}, u32[]{:S(2)}) collective-permute-start(f32[32,2048]{1,0:T(8,128)S(1)} %convert_add_fusion.1.refs_0_), channel_id=1, source_target_pairs={{0,1},{1,0},{2,3},{3,2},{4,5},{5,4},{6,7},{7,6},{8,9},{9,8},{10,11... | collective-permute-start | bytes 786440 | tf_op jit(solution)/shard_map/ppermute | solution.py:325
  44.8 1.2 %collective-permute-done.15.refs_1_ = f32[32,2048]{1,0:T(8,128)S(1)} collective-permute-done((f32[32,2048]{1,0:T(8,128)S(1)}, f32[32,2048]{1,0:T(8,128)S(1)}, u32[]{:S(2)}, u32[]{:S(2)}) %collective-permute-start.15) | collective-permute-done | bytes 262176 | tf_op jit(solution)/shard_map/ppermute | solution.py:325
  45.9 0.7 shard_map.138
  46.7 0.1 collective-permute-start.19
  46.8 2.9 %collective-permute-start.18 = (bf16[32,2176]{1,0:T(8,128)(2,1)S(1)}, bf16[32,2176]{1,0:T(8,128)(2,1)S(1)}, u32[]{:S(2)}, u32[]{:S(2)}) collective-permute-start(bf16[32,2176]{1,0:T(8,128)(2,1)S(1)} %get-tuple-element.66.own_ref), channel_id=1, source_target_pairs={{0,4},{1,13},{2,6},{3,15},{4,0},{5,9},{6,2},{7,11},{8,12},{9,5},{1... | collective-permute-start | bytes 417800 | tf_op jit(solution)/shard_map/ppermute | solution.py:337
  49.7 0.5 collective-permute-start.17
  50.2 0.7 collective-permute-start.16
  50.9 1.9 %collective-permute-done.19.refs_3_ = bf16[32,2176]{1,0:T(8,128)(2,1)S(1)} collective-permute-done((bf16[32,2176]{1,0:T(8,128)(2,1)S(1)}, bf16[32,2176]{1,0:T(8,128)(2,1)S(1)}, u32[]{:S(2)}, u32[]{:S(2)}) %collective-permute-start.19) | collective-permute-done | bytes 139296 | tf_op jit(solution)/shard_map/ppermute | solution.py:337
  52.8 5.0 %collective-permute-done.18.refs_2_ = bf16[32,2176]{1,0:T(8,128)(2,1)S(1)} collective-permute-done((bf16[32,2176]{1,0:T(8,128)(2,1)S(1)}, bf16[32,2176]{1,0:T(8,128)(2,1)S(1)}, u32[]{:S(2)}, u32[]{:S(2)}) %collective-permute-start.18) | collective-permute-done | bytes 139296 | tf_op jit(solution)/shard_map/ppermute | solution.py:337
  57.9 0.6 copy-done.8
  58.5 0.1 copy-done.9
  58.5 0.7 copy-done.10
  59.2 9.5 %shard_map.139 = (bf16[32,2048]{1,0:T(8,128)(2,1)}, bf16[32,2048]{1,0:T(8,128)(2,1)}, bf16[32,2048]{1,0:T(8,128)(2,1)}, bf16[32,2048]{1,0:T(8,128)(2,1)}) custom-call(s32[2]{0:T(128)} %pad_add_fusion.place_ref, bf16[32,2176]{1,0:T(8,128)(2,1)} %copy-done.1, bf16[32,2176]{1,0:T(8,128)(2,1)} %copy-done.10, bf16[32,2176]{1,0:T(8,128)(2,1)} %copy-done.9, ...), custom_call_target="tpu_custom_call" | custom-call | tf_op jit(solution)/shard_map/pallas_call | solution.py:283
  68.7 0.3 collective-permute-start.21
  69.0 3.3 %collective-permute-start.23 = (bf16[32,2048]{1,0:T(8,128)(2,1)}, bf16[32,2048]{1,0:T(8,128)(2,1)S(1)}, u32[]{:S(2)}, u32[]{:S(2)}) collective-permute-start(bf16[32,2048]{1,0:T(8,128)(2,1)} %get-tuple-element.76), channel_id=1, source_target_pairs={{0,6},{1,15},{2,4},{3,13},{4,2},{5,11},{6,0},{7,9},{8,14},{9,7},{1... | collective-permute-start | bytes 393224 | tf_op jit(solution)/shard_map/ppermute | solution.py:337
  72.2 0.7 collective-permute-start.20
  72.9 1.0 %collective-permute-done.21 = bf16[32,2048]{1,0:T(8,128)(2,1)S(1)} collective-permute-done((bf16[32,2048]{1,0:T(8,128)(2,1)}, bf16[32,2048]{1,0:T(8,128)(2,1)S(1)}, u32[]{:S(2)}, u32[]{:S(2)}) %collective-permute-start.21) | collective-permute-done | bytes 131104 | tf_op jit(solution)/shard_map/ppermute | solution.py:337
  73.9 0.2 collective-permute-done.22
  74.2 2.6 %collective-permute-done.23 = bf16[32,2048]{1,0:T(8,128)(2,1)S(1)} collective-permute-done((bf16[32,2048]{1,0:T(8,128)(2,1)}, bf16[32,2048]{1,0:T(8,128)(2,1)S(1)}, u32[]{:S(2)}, u32[]{:S(2)}) %collective-permute-start.23) | collective-permute-done | bytes 131104 | tf_op jit(solution)/shard_map/ppermute | solution.py:337
  76.8 1.0 %convert_add_fusion = f32[32,2048]{1,0:T(8,128)S(1)} fusion(bf16[32,2048]{1,0:T(8,128)(2,1)S(1)} %collective-permute-done.23, bf16[32,2048]{1,0:T(8,128)(2,1)S(1)} %collective-permute-done.22, bf16[32,2048]{1,0:T(8,128)(2,1)S(1)} %collective-permute-done.21, bf16[32,2048]{1,0:T(8,128)(2,1)} %get-tuple-element.73, ...), kind=kLoop, calls=%fused_computation | loop fusion | flops 524288 | bytes 917505 | tf_op jit(solution)/shard_map/add | solution.py:347
  77.8 9.5 %collective-permute-start.24 = (f32[32,1024]{1,0:T(8,128)S(1)}, f32[32,1024]{1,0:T(8,128)S(1)}, u32[]{:S(2)}, u32[]{:S(2)}) collective-permute-start(f32[32,1024]{1,0:T(8,128)S(1)} %slice.57), channel_id=1, source_target_pairs={{0,1},{1,0},{2,3},{3,2},{4,5},{5,4},{6,7},{7,6},{8,9},{9,8},{10,11... | collective-permute-start | bytes 393224 | tf_op jit(solution)/shard_map/ppermute | solution.py:325
  87.3 1.0 %collective-permute-done.24 = f32[32,1024]{1,0:T(8,128)S(1)} collective-permute-done((f32[32,1024]{1,0:T(8,128)S(1)}, f32[32,1024]{1,0:T(8,128)S(1)}, u32[]{:S(2)}, u32[]{:S(2)}) %collective-permute-start.24) | collective-permute-done | bytes 131104 | tf_op jit(solution)/shard_map/ppermute | solution.py:325
  88.4 0.7 fusion.1
  (41 shorter events, 0.2 us)
Async XLA Ops:
  0.0 11.6 %collective-permute-start = (bf16[2,1024,768]{2,1,0:T(8,128)(2,1)}, bf16[2,1024,768]{2,1,0:T(8,128)(2,1)}, u32[]{:S(2)}, u32[]{:S(2)}) collective-permute-start(bf16[2,1024,768]{2,1,0:T(8,128)(2,1)} %refs_4_.1), channel_id=1, source_target_pairs={{0,1},{1,0},{2,3},{3,2},{4,5},{5,4},{6,7},{7,6},{8,9},{9,8},{10,11... | collective-permute-start | bytes 9437192 | tf_op jit(solution)/shard_map/ppermute | solution.py:325
  0.5 11.2 %collective-permute-start.1 = (bf16[2,1024,768]{2,1,0:T(8,128)(2,1)}, bf16[2,1024,768]{2,1,0:T(8,128)(2,1)}, u32[]{:S(2)}, u32[]{:S(2)}) collective-permute-start(bf16[2,1024,768]{2,1,0:T(8,128)(2,1)} %refs_6_), channel_id=1, source_target_pairs={{0,1},{1,0},{2,3},{3,2},{4,5},{5,4},{6,7},{7,6},{8,9},{9,8},{10,11... | collective-permute-start | bytes 9437192 | tf_op jit(solution)/shard_map/ppermute | solution.py:325
  0.5 11.1 %collective-permute-start.3 = (f32[1,1024]{1,0:T(1,128)}, f32[1,1024]{1,0:T(1,128)S(1)}, u32[]{:S(2)}, u32[]{:S(2)}) collective-permute-start(f32[1,1024]{1,0:T(1,128)} %bitcast.23), channel_id=1, source_target_pairs={{0,1},{1,0},{2,3},{3,2},{4,5},{5,4},{6,7},{7,6},{8,9},{9,8},{10,11... | collective-permute-start | bytes 12296 | tf_op jit(solution)/shard_map/ppermute | solution.py:325
  1.0 10.6 %collective-permute-start.2 = (bf16[32,1024]{1,0:T(8,128)(2,1)}, bf16[32,1024]{1,0:T(8,128)(2,1)S(1)}, u32[]{:S(2)}, u32[]{:S(2)}) collective-permute-start(bf16[32,1024]{1,0:T(8,128)(2,1)} %refs_2_), channel_id=1, source_target_pairs={{0,1},{1,0},{2,3},{3,2},{4,5},{5,4},{6,7},{7,6},{8,9},{9,8},{10,11... | collective-permute-start | bytes 196616 | tf_op jit(solution)/shard_map/ppermute | solution.py:325
  1.7 11.7 %copy-start = (bf16[1024,1024]{1,0:T(8,128)(2,1)S(1)}, bf16[1024,1024]{1,0:T(8,128)(2,1)}, u32[]{:S(2)}) copy-start(bf16[1024,1024]{1,0:T(8,128)(2,1)} %refs_4_) | copy-start | bytes 6291460
  1.7 28.0 %copy-start.3 = (s32[2]{0:T(128)S(1)}, s32[2]{0:T(128)}, u32[]{:S(2)}) copy-start(s32[2]{0:T(128)} %pad_add_fusion.place_ref) | copy-start | bytes 28
  11.6 34.3 %copy-start.2 = (bf16[32,1024]{1,0:T(8,128)(2,1)S(1)}, bf16[32,1024]{1,0:T(8,128)(2,1)}, u32[]{:S(2)}) copy-start(bf16[32,1024]{1,0:T(8,128)(2,1)} %refs_2_) | copy-start | bytes 196612
  11.6 34.3 %copy-start.4 = (f32[1024]{0:T(1024)S(1)}, f32[1024]{0:T(1024)}, u32[]{:S(2)}) copy-start(f32[1024]{0:T(1024)} %param.22) | copy-start | bytes 12292
  11.6 34.3 %copy-start.5 = (s32[32,8]{0,1:T(8,128)S(1)}, s32[32,8]{0,1:T(8,128)}, u32[]{:S(2)}) copy-start(s32[32,8]{0,1:T(8,128)} %param.23) | copy-start | bytes 3076
  11.7 34.3 %copy-start.6 = (f32[32,8]{0,1:T(8,128)S(1)}, f32[32,8]{0,1:T(8,128)}, u32[]{:S(2)}) copy-start(f32[32,8]{0,1:T(8,128)} %param.24) | copy-start | bytes 3076
  11.7 1.7 %collective-permute-start.4 = (bf16[4,16,1024]{2,1,0:T(8,128)(2,1)}, bf16[4,16,1024]{2,1,0:T(8,128)(2,1)S(1)}, u32[]{:S(2)}, u32[]{:S(2)}) collective-permute-start(bf16[4,16,1024]{2,1,0:T(8,128)(2,1)} %get-tuple-element.44), channel_id=1, source_target_pairs={{0,1},{1,0},{2,3},{3,2},{4,5},{5,4},{6,7},{7,6},{8,9},{9,8},{10,11... | collective-permute-start | bytes 393224 | tf_op jit(solution)/shard_map/ppermute | solution.py:325
  13.4 11.8 %collective-permute-start.9 = (bf16[1024,1024]{1,0:T(8,128)(2,1)S(1)}, bf16[1024,1024]{1,0:T(8,128)(2,1)S(1)}, u32[]{:S(2)}, u32[]{:S(2)}) collective-permute-start(bf16[1024,1024]{1,0:T(8,128)(2,1)S(1)} %copy-done), channel_id=1, source_target_pairs={{0,1},{1,0},{2,3},{3,2},{4,5},{5,4},{6,7},{7,6},{8,9},{9,8},{10,11... | collective-permute-start | bytes 6291464 | tf_op jit(solution)/shard_map/ppermute | solution.py:325
  14.6 5.0 %collective-permute-start.6 = (bf16[32,1024]{1,0:T(8,128)(2,1)S(1)}, bf16[32,1024]{1,0:T(8,128)(2,1)S(1)}, u32[]{:S(2)}, u32[]{:S(2)}) collective-permute-start(bf16[32,1024]{1,0:T(8,128)(2,1)S(1)} %pad_maximum_fusion.1), channel_id=1, source_target_pairs={{0,2},{1,11},{2,0},{3,9},{4,6},{5,15},{6,4},{7,13},{8,10},{9,3},{1... | collective-permute-start | bytes 196616 | tf_op jit(solution)/shard_map/ppermute | solution.py:337
  17.3 4.7 %collective-permute-start.7 = (bf16[32,1024]{1,0:T(8,128)(2,1)S(1)}, bf16[32,1024]{1,0:T(8,128)(2,1)S(1)}, u32[]{:S(2)}, u32[]{:S(2)}) collective-permute-start(bf16[32,1024]{1,0:T(8,128)(2,1)S(1)} %pad_maximum_fusion.2), channel_id=1, source_target_pairs={{0,4},{1,13},{2,6},{3,15},{4,0},{5,9},{6,2},{7,11},{8,12},{9,5},{1... | collective-permute-start | bytes 196616 | tf_op jit(solution)/shard_map/ppermute | solution.py:337
  18.9 3.1 %collective-permute-start.5 = (bf16[32,1024]{1,0:T(8,128)(2,1)S(1)}, bf16[32,1024]{1,0:T(8,128)(2,1)S(1)}, u32[]{:S(2)}, u32[]{:S(2)}) collective-permute-start(bf16[32,1024]{1,0:T(8,128)(2,1)S(1)} %pad_maximum_fusion.own_ref), channel_id=1, source_target_pairs={{1,9},{3,11},{5,13},{7,15},{9,1},{11,3},{13,5},{15,7},{17,25},{19,... | collective-permute-start | bytes 196616 | tf_op jit(solution)/shard_map/ppermute | solution.py:337
  19.6 5.6 %collective-permute-start.8 = (bf16[32,1024]{1,0:T(8,128)(2,1)S(1)}, bf16[32,1024]{1,0:T(8,128)(2,1)S(1)}, u32[]{:S(2)}, u32[]{:S(2)}) collective-permute-start(bf16[32,1024]{1,0:T(8,128)(2,1)S(1)} %pad_maximum_fusion.3), channel_id=1, source_target_pairs={{0,6},{1,15},{2,4},{3,13},{4,2},{5,11},{6,0},{7,9},{8,14},{9,7},{1... | collective-permute-start | bytes 196616 | tf_op jit(solution)/shard_map/ppermute | solution.py:337
  25.2 17.7 %collective-permute-start.14 = (bf16[2,768,1024]{2,1,0:T(8,128)(2,1)}, bf16[2,768,1024]{2,1,0:T(8,128)(2,1)}, u32[]{:S(2)}, u32[]{:S(2)}) collective-permute-start(bf16[2,768,1024]{2,1,0:T(8,128)(2,1)} %refs_8_), channel_id=1, source_target_pairs={{0,1},{1,0},{2,3},{3,2},{4,5},{5,4},{6,7},{7,6},{8,9},{9,8},{10,11... | collective-permute-start | bytes 9437192 | tf_op jit(solution)/shard_map/ppermute | solution.py:325
  31.0 5.5 %collective-permute-start.11 = (bf16[32,2048]{1,0:T(8,128)(2,1)S(1)}, bf16[32,2048]{1,0:T(8,128)(2,1)S(1)}, u32[]{:S(2)}, u32[]{:S(2)}) collective-permute-start(bf16[32,2048]{1,0:T(8,128)(2,1)S(1)} %get-tuple-element.56), channel_id=1, source_target_pairs={{0,2},{1,11},{2,0},{3,9},{4,6},{5,15},{6,4},{7,13},{8,10},{9,3},{1... | collective-permute-start | bytes 393224 | tf_op jit(solution)/shard_map/ppermute | solution.py:337
  31.6 7.6 %collective-permute-start.12 = (bf16[32,2048]{1,0:T(8,128)(2,1)S(1)}, bf16[32,2048]{1,0:T(8,128)(2,1)S(1)}, u32[]{:S(2)}, u32[]{:S(2)}) collective-permute-start(bf16[32,2048]{1,0:T(8,128)(2,1)S(1)} %get-tuple-element.57), channel_id=1, source_target_pairs={{0,4},{1,13},{2,6},{3,15},{4,0},{5,9},{6,2},{7,11},{8,12},{9,5},{1... | collective-permute-start | bytes 393224 | tf_op jit(solution)/shard_map/ppermute | solution.py:337
  31.6 11.2 %collective-permute-start.13 = (bf16[32,2048]{1,0:T(8,128)(2,1)S(1)}, bf16[32,2048]{1,0:T(8,128)(2,1)S(1)}, u32[]{:S(2)}, u32[]{:S(2)}) collective-permute-start(bf16[32,2048]{1,0:T(8,128)(2,1)S(1)} %get-tuple-element.58), channel_id=1, source_target_pairs={{0,6},{1,15},{2,4},{3,13},{4,2},{5,11},{6,0},{7,9},{8,14},{9,7},{1... | collective-permute-start | bytes 393224 | tf_op jit(solution)/shard_map/ppermute | solution.py:337
  34.5 8.3 %collective-permute-start.10 = (bf16[32,2048]{1,0:T(8,128)(2,1)S(1)}, bf16[32,2048]{1,0:T(8,128)(2,1)S(1)}, u32[]{:S(2)}, u32[]{:S(2)}) collective-permute-start(bf16[32,2048]{1,0:T(8,128)(2,1)S(1)} %get-tuple-element.55), channel_id=1, source_target_pairs={{1,9},{3,11},{5,13},{7,15},{9,1},{11,3},{13,5},{15,7},{17,25},{19,... | collective-permute-start | bytes 393224 | tf_op jit(solution)/shard_map/ppermute | solution.py:337
  42.9 3.0 %collective-permute-start.15 = (f32[32,2048]{1,0:T(8,128)S(1)}, f32[32,2048]{1,0:T(8,128)S(1)}, u32[]{:S(2)}, u32[]{:S(2)}) collective-permute-start(f32[32,2048]{1,0:T(8,128)S(1)} %convert_add_fusion.1.refs_0_), channel_id=1, source_target_pairs={{0,1},{1,0},{2,3},{3,2},{4,5},{5,4},{6,7},{7,6},{8,9},{9,8},{10,11... | collective-permute-start | bytes 786440 | tf_op jit(solution)/shard_map/ppermute | solution.py:325
  46.7 11.2 %copy-start.1 = (bf16[32,2176]{1,0:T(8,128)(2,1)}, bf16[32,2176]{1,0:T(8,128)(2,1)S(1)}, u32[]{:S(2)}) copy-start(bf16[32,2176]{1,0:T(8,128)(2,1)S(1)} %get-tuple-element.66.own_ref) | copy-start | bytes 417796
  46.7 6.2 %collective-permute-start.19 = (bf16[32,2176]{1,0:T(8,128)(2,1)S(1)}, bf16[32,2176]{1,0:T(8,128)(2,1)S(1)}, u32[]{:S(2)}, u32[]{:S(2)}) collective-permute-start(bf16[32,2176]{1,0:T(8,128)(2,1)S(1)} %get-tuple-element.66.own_ref), channel_id=1, source_target_pairs={{0,6},{1,15},{2,4},{3,13},{4,2},{5,11},{6,0},{7,9},{8,14},{9,7},{1... | collective-permute-start | bytes 417800 | tf_op jit(solution)/shard_map/ppermute | solution.py:337
  46.8 11.0 %collective-permute-start.18 = (bf16[32,2176]{1,0:T(8,128)(2,1)S(1)}, bf16[32,2176]{1,0:T(8,128)(2,1)S(1)}, u32[]{:S(2)}, u32[]{:S(2)}) collective-permute-start(bf16[32,2176]{1,0:T(8,128)(2,1)S(1)} %get-tuple-element.66.own_ref), channel_id=1, source_target_pairs={{0,4},{1,13},{2,6},{3,15},{4,0},{5,9},{6,2},{7,11},{8,12},{9,5},{1... | collective-permute-start | bytes 417800 | tf_op jit(solution)/shard_map/ppermute | solution.py:337
  49.7 8.1 %collective-permute-start.17 = (bf16[32,2176]{1,0:T(8,128)(2,1)S(1)}, bf16[32,2176]{1,0:T(8,128)(2,1)S(1)}, u32[]{:S(2)}, u32[]{:S(2)}) collective-permute-start(bf16[32,2176]{1,0:T(8,128)(2,1)S(1)} %get-tuple-element.66.own_ref), channel_id=1, source_target_pairs={{0,2},{1,11},{2,0},{3,9},{4,6},{5,15},{6,4},{7,13},{8,10},{9,3},{1... | collective-permute-start | bytes 417800 | tf_op jit(solution)/shard_map/ppermute | solution.py:337
  50.2 7.6 %collective-permute-start.16 = (bf16[32,2176]{1,0:T(8,128)(2,1)S(1)}, bf16[32,2176]{1,0:T(8,128)(2,1)S(1)}, u32[]{:S(2)}, u32[]{:S(2)}) collective-permute-start(bf16[32,2176]{1,0:T(8,128)(2,1)S(1)} %get-tuple-element.66.own_ref), channel_id=1, source_target_pairs={{1,9},{3,11},{5,13},{7,15},{9,1},{11,3},{13,5},{15,7},{17,25},{19,... | collective-permute-start | bytes 417800 | tf_op jit(solution)/shard_map/ppermute | solution.py:337
  52.8 5.0 %copy-start.7 = (bf16[32,2176]{1,0:T(8,128)(2,1)}, bf16[32,2176]{1,0:T(8,128)(2,1)S(1)}, u32[]{:S(2)}) copy-start(bf16[32,2176]{1,0:T(8,128)(2,1)S(1)} %collective-permute-done.19.refs_3_) | copy-start | bytes 417796
  57.8 0.7 copy-start.8
  57.8 0.7 copy-start.9
  58.5 0.7 copy-start.10
  68.7 5.2 %collective-permute-start.21 = (bf16[32,2048]{1,0:T(8,128)(2,1)}, bf16[32,2048]{1,0:T(8,128)(2,1)S(1)}, u32[]{:S(2)}, u32[]{:S(2)}) collective-permute-start(bf16[32,2048]{1,0:T(8,128)(2,1)} %get-tuple-element.74), channel_id=1, source_target_pairs={{0,2},{1,11},{2,0},{3,9},{4,6},{5,15},{6,4},{7,13},{8,10},{9,3},{1... | collective-permute-start | bytes 393224 | tf_op jit(solution)/shard_map/ppermute | solution.py:337
  69.0 5.2 %collective-permute-start.22 = (bf16[32,2048]{1,0:T(8,128)(2,1)}, bf16[32,2048]{1,0:T(8,128)(2,1)S(1)}, u32[]{:S(2)}, u32[]{:S(2)}) collective-permute-start(bf16[32,2048]{1,0:T(8,128)(2,1)} %get-tuple-element.75), channel_id=1, source_target_pairs={{0,4},{1,13},{2,6},{3,15},{4,0},{5,9},{6,2},{7,11},{8,12},{9,5},{1... | collective-permute-start | bytes 393224 | tf_op jit(solution)/shard_map/ppermute | solution.py:337
  69.0 7.8 %collective-permute-start.23 = (bf16[32,2048]{1,0:T(8,128)(2,1)}, bf16[32,2048]{1,0:T(8,128)(2,1)S(1)}, u32[]{:S(2)}, u32[]{:S(2)}) collective-permute-start(bf16[32,2048]{1,0:T(8,128)(2,1)} %get-tuple-element.76), channel_id=1, source_target_pairs={{0,6},{1,15},{2,4},{3,13},{4,2},{5,11},{6,0},{7,9},{8,14},{9,7},{1... | collective-permute-start | bytes 393224 | tf_op jit(solution)/shard_map/ppermute | solution.py:337
  72.2 4.6 %collective-permute-start.20 = (bf16[32,2048]{1,0:T(8,128)(2,1)}, bf16[32,2048]{1,0:T(8,128)(2,1)S(1)}, u32[]{:S(2)}, u32[]{:S(2)}) collective-permute-start(bf16[32,2048]{1,0:T(8,128)(2,1)} %get-tuple-element.73), channel_id=1, source_target_pairs={{1,9},{3,11},{5,13},{7,15},{9,1},{11,3},{13,5},{15,7},{17,25},{19,... | collective-permute-start | bytes 393224 | tf_op jit(solution)/shard_map/ppermute | solution.py:337
  77.8 10.5 %collective-permute-start.24 = (f32[32,1024]{1,0:T(8,128)S(1)}, f32[32,1024]{1,0:T(8,128)S(1)}, u32[]{:S(2)}, u32[]{:S(2)}) collective-permute-start(f32[32,1024]{1,0:T(8,128)S(1)} %slice.57), channel_id=1, source_target_pairs={{0,1},{1,0},{2,3},{3,2},{4,5},{5,4},{6,7},{7,6},{8,9},{9,8},{10,11... | collective-permute-start | bytes 393224 | tf_op jit(solution)/shard_map/ppermute | solution.py:325

commit v3 on v2

--- a/solution.py
+++ b/solution.py
@@ -14,6 +14,7 @@
 SMEM = pl.BlockSpec(memory_space=pltpu.SMEM)
 ANY = pl.BlockSpec(memory_space=pl.ANY)
 MIB = 1024 * 1024
+TUNED = {(8, 2): ((5, 0, 3, 6), (7, 1, 2, 4))}
 
 
 def choose(core, values):
@@ -37,30 +38,59 @@
 
 
 def attend_kernel(
-    kv_heads, offset, len_ref, place_ref, q_ref, k_hbm, v_hbm, ik_ref, iv_ref, *refs
+    kv_heads, offset, len_ref, me_ref, core_ref, q_ref, k_hbm, v_hbm, ik_ref, iv_ref, *refs
 ):
     cores, slots = len(offset), len(offset[0])
     out_refs = refs[:cores]
-    k_buf, v_buf, mask_ref, all_ref, sems = refs[cores:]
+    k_buf, v_buf, mask_ref, all_ref, order_ref, sems = refs[cores:]
     rows, heads, size = q_ref.shape
     span = k_buf.shape[1]
     per = heads // kv_heads
     block = heads // (cores * slots)
     scale = size ** (-0.5) * math.log2(math.e)
-    step = 2
-
-    def copies(r):
+    step = 4
+    chunks = 4
+    chunk = span // chunks
+
+    lengths = [len_ref[r] for r in range(rows)]
+    ranks = [jnp.int32(0)] * rows
+    for i in range(rows):
+        for j in range(i + 1, rows):
+            later = (lengths[i] < lengths[j]).astype(jnp.int32)
+            ranks[i] = ranks[i] + later
+            ranks[j] = ranks[j] + (1 - later)
+    for r in range(rows):
+        order_ref[ranks[r]] = jnp.int32(r)
+
+    def copies(i, used):
+        r = order_ref[i]
+        part = pl.ds(0, used)
         return (
-            pltpu.make_async_copy(k_hbm.at[r], k_buf.at[r], sems.at[0, r]),
-            pltpu.make_async_copy(v_hbm.at[r], v_buf.at[r], sems.at[1, r]),
+            pltpu.make_async_copy(k_hbm.at[r, part], k_buf.at[r, part], sems.at[0, i]),
+            pltpu.make_async_copy(v_hbm.at[r, part], v_buf.at[r, part], sems.at[1, i]),
         )
 
-    for r in range(rows):
-        for copy in copies(r):
-            copy.start()
+    def by_length(i, work):
+        needed = (len_ref[order_ref[i * step]] * kv_heads + (chunk - 1)) // chunk
+        for n in range(1, chunks + 1):
+
+            @pl.when(needed == n)
+            def _():
+                work(n * chunk)
+
+    def begin(i, carry):
+        def work(used):
+            for j in range(step):
+                for copy in copies(i * step + j, used):
+                    copy.start()
+
+        by_length(i, work)
+        return carry
+
+    lax.fori_loop(0, rows // step, begin, 0)
     column = lax.broadcasted_iota(jnp.int32, (heads, span), 1)
     head = lax.broadcasted_iota(jnp.int32, (heads, span), 0)
-    mask_ref[...] = jnp.where(lax.rem(column, kv_heads) == head // per, column, 1 << 30)
+    mask_ref[...] = jnp.where((column & (kv_heads - 1)) == (head >> (per.bit_length() - 1)), column, 1 << 30)
 
     def spread(value):
         return jnp.concatenate(
@@ -71,30 +101,47 @@
             axis=0,
         )
 
-    def one(r):
-        q = q_ref[r]
-        scores = lax.dot_general(
-            q, k_buf[r], (((1,), (1,)), ((), ())), preferred_element_type=F32
-        )
-        scores = jnp.where(mask_ref[...] < len_ref[r] * kv_heads, scores, -1e30)
-        own = jnp.sum(q.astype(F32) * spread(ik_ref[r]), axis=1, keepdims=True)
-        peak = jnp.maximum(jnp.max(scores, axis=1, keepdims=True), own)
-        expo = jnp.exp2((scores - peak) * scale)
-        fresh = jnp.exp2((own - peak) * scale)
-        total = jnp.sum(expo, axis=1, keepdims=True) + fresh
-        accum = jnp.dot(expo.astype(BF16), v_buf[r], preferred_element_type=F32)
-        all_ref[pl.ds(r, heads, stride=rows), :] = (accum + fresh * spread(iv_ref[r])) / total
+    def several(group, used):
+        queries = [q_ref[r] for r in group]
+        scores = [
+            lax.dot_general(
+                q, k_buf[r, :used], (((1,), (1,)), ((), ())), preferred_element_type=F32
+            )
+            for q, r in zip(queries, group)
+        ]
+        own = [
+            jnp.sum(q.astype(F32) * spread(ik_ref[r]), axis=1, keepdims=True)
+            for q, r in zip(queries, group)
+        ]
+        scores = [
+            jnp.where(mask_ref[:, :used] < len_ref[r] * kv_heads, x, -1e30)
+            for x, r in zip(scores, group)
+        ]
+        peak = [
+            jnp.maximum(jnp.max(x, axis=1, keepdims=True), o) for x, o in zip(scores, own)
+        ]
+        expo = [jnp.exp2((x - p) * scale) for x, p in zip(scores, peak)]
+        accum = [
+            jnp.dot(x.astype(BF16), v_buf[r, :used], preferred_element_type=F32)
+            for x, r in zip(expo, group)
+        ]
+        fresh = [jnp.exp2((o - p) * scale) for o, p in zip(own, peak)]
+        total = [jnp.sum(x, axis=1, keepdims=True) + f for x, f in zip(expo, fresh)]
+        for x, f, t, r in zip(accum, fresh, total, group):
+            all_ref[pl.ds(r, heads, stride=rows), :] = (x + f * spread(iv_ref[r])) / t
 
     def body(i, carry):
-        for j in range(step):
-            for copy in copies(i * step + j):
-                copy.wait()
-        for j in range(step):
-            one(i * step + j)
+        def work(used):
+            for j in range(step):
+                for copy in copies(i * step + j, used):
+                    copy.wait()
+            several([order_ref[i * step + j] for j in range(step)], used)
+
+        by_length(i, work)
         return carry
 
     lax.fori_loop(0, rows // step, body, 0)
-    me, core = place_ref[0], place_ref[1]
+    me, core = me_ref[0], core_ref[0]
     for m in range(cores):
         for s in range(slots):
             which = me ^ choose(core, [offset[c ^ m][s] for c in range(cores)])
@@ -114,19 +161,20 @@
     return pl.pallas_call(
         functools.partial(attend_kernel, kv_heads, offset),
         out_shape=[jax.ShapeDtypeStruct((slots, rows, width), BF16)] * cores,
-        in_specs=[SMEM, SMEM, VMEM, ANY, ANY, VMEM, VMEM],
+        in_specs=[SMEM, SMEM, SMEM, VMEM, ANY, ANY, VMEM, VMEM],
         out_specs=[VMEM] * cores,
         scratch_shapes=[
             pltpu.VMEM((rows, span, size), BF16),
             pltpu.VMEM((rows, span, size), BF16),
             pltpu.VMEM((heads, span), jnp.int32),
             pltpu.VMEM((heads * rows, size), F32),
+            pltpu.SMEM((rows,), jnp.int32),
             pltpu.SemaphoreType.DMA((2, rows)),
         ],
         compiler_params=pltpu.CompilerParams(vmem_limit_bytes=60 * MIB),
     )(
         lengths,
-        place,
+        *place,
         query,
         keys.reshape(rows, span, size),
         values.reshape(rows, span, size),
@@ -135,8 +183,8 @@
     )
 
 
-def take_slots(offset, place_ref, own_ref, moved_refs):
-    core = place_ref[1]
+def take_slots(offset, core_ref, own_ref, moved_refs):
+    core = core_ref[0]
     result = []
     for s, ref in enumerate(moved_refs):
         block = ref[...]
@@ -147,11 +195,11 @@
     return jnp.concatenate(result, axis=0)
 
 
-def project_kernel(offset, place_ref, own_ref, *refs):
+def project_kernel(offset, core_ref, own_ref, *refs):
     cores, slots = len(offset), len(offset[0])
     moved_refs, w_refs = refs[:slots], refs[slots : slots + cores]
     out_refs = refs[slots + cores : 2 * slots + cores]
-    left = take_slots(offset, place_ref, own_ref, moved_refs)
+    left = take_slots(offset, core_ref, own_ref, moved_refs)
     rows, part = own_ref.shape[0], w_refs[0].shape[1]
     for j in range(cores):
         product = jnp.dot(left, w_refs[j][...], preferred_element_type=F32).astype(BF16)
@@ -169,15 +217,15 @@
         in_specs=[SMEM, VMEM] + [VMEM] * (slots + cores),
         out_specs=[VMEM] * slots,
         compiler_params=pltpu.CompilerParams(vmem_limit_bytes=12 * MIB),
-    )(place, own, *moved, *weights)
-
-
-def norm_kernel(cores, experts, place_ref, *refs):
+    )(place[1], own, *moved, *weights)
+
+
+def norm_kernel(cores, experts, core_ref, *refs):
     sums_refs, stream_refs, gain_refs = refs[:cores], refs[cores : 2 * cores], refs[2 * cores : 3 * cores]
     ids_ref, routes_ref, mixed_ref, out_ref = refs[3 * cores :]
     rows, part = stream_refs[0].shape
     width = part * cores
-    core = place_ref[1]
+    core = core_ref[0]
     squares = 0.0
     mixed = []
     for j in range(cores):
@@ -221,35 +269,66 @@
         in_specs=[SMEM] + [VMEM] * (3 * cores + 2),
         out_specs=(VMEM, VMEM),
         compiler_params=pltpu.CompilerParams(vmem_limit_bytes=8 * MIB),
-    )(place, *sums, *stream, *gain, ids.T, routes.T)
-
-
-def expert_kernel(offset, devs, place_ref, own_ref, *refs):
+    )(place[1], *sums, *stream, *gain, ids.T, routes.T)
+
+
+def fetch_kernel(count, *refs):
+    sources, targets, sems = refs[:count], refs[count : 2 * count], refs[2 * count]
+    copies = [
+        pltpu.make_async_copy(sources[i].at[0], targets[i], sems.at[i]) for i in range(count)
+    ]
+    for copy in copies:
+        copy.start()
+    for copy in copies:
+        copy.wait()
+
+
+def fetch(weights):
+    count = len(weights)
+    return pl.pallas_call(
+        functools.partial(fetch_kernel, count),
+        out_shape=[jax.ShapeDtypeStruct(w.shape[1:], w.dtype) for w in weights],
+        in_specs=[ANY] * count,
+        out_specs=[VMEM] * count,
+        scratch_shapes=[pltpu.SemaphoreType.DMA((count,))],
+        compiler_params=pltpu.CompilerParams(vmem_limit_bytes=43 * MIB),
+    )(*weights)
+
+
+def expert_kernel(offset, devs, me_ref, core_ref, own_ref, *refs):
     cores, slots = len(offset), len(offset[0])
     moved_refs, refs = refs[:slots], refs[slots:]
-    gate_refs, up_refs, down_refs = refs[:cores], refs[cores : 2 * cores], refs[2 * cores : 3 * cores]
+    first_refs, refs = refs[: 3 * cores], refs[3 * cores :]
+    weight_refs = refs[: 3 * cores]
     out_refs = refs[3 * cores : 3 * cores + slots]
     gate_buf, up_buf, down_buf, sems = refs[3 * cores + slots :]
-    local, part, hidden = gate_refs[0].shape
+    local, part, hidden = weight_refs[0].shape
     rows = own_ref.shape[0]
     width = part * cores
+    bufs = (gate_buf, up_buf, down_buf)
 
     def copy(kind, j, e):
-        source = (gate_refs, up_refs, down_refs)[kind][j]
-        target = (gate_buf, up_buf, down_buf)[kind]
-        return pltpu.make_async_copy(source.at[e], target.at[j, e], sems.at[kind, j, e])
-
-    for e in range(local):
+        return pltpu.make_async_copy(
+            weight_refs[kind * cores + j].at[e], bufs[kind].at[j, e - 1], sems.at[kind, j, e - 1]
+        )
+
+    def weight(kind, j, e):
+        if e == 0:
+            return first_refs[kind * cores + j][...]
+        copy(kind, j, e).wait()
+        return bufs[kind][j, e - 1]
+
+    for e in range(1, local):
         for kind in range(3):
             for j in range(cores):
                 copy(kind, j, e).start()
-    tokens = take_slots(offset, place_ref, own_ref, moved_refs)
+    tokens = take_slots(offset, core_ref, own_ref, moved_refs)
     tail = tokens[:, width:].astype(F32)
     lane = lax.broadcasted_iota(jnp.int32, tail.shape, 1)
     experts = local * devs
     total = [0.0] * cores
     for e in range(local):
-        mine = place_ref[0] * local + e
+        mine = me_ref[0] * local + e
         share = jnp.sum(
             jnp.where((lane == mine) | (lane == mine + experts), tail, 0.0), axis=1, keepdims=True
         )
@@ -257,18 +336,16 @@
         for kind in range(2):
             value = 0.0
             for j in range(cores):
-                copy(kind, j, e).wait()
                 value = value + jnp.dot(
                     tokens[:, j * part : (j + 1) * part],
-                    (gate_buf, up_buf)[kind][j, e],
+                    weight(kind, j, e),
                     preferred_element_type=F32,
                 )
             sums.append(value)
         gate, up = sums
         active = (gate / (1.0 + jnp.exp(-gate)) * up * share).astype(BF16)
         for j in range(cores):
-            copy(2, j, e).wait()
-            total[j] = total[j] + jnp.dot(active, down_buf[j, e], preferred_element_type=F32)
+            total[j] = total[j] + jnp.dot(active, weight(2, j, e), preferred_element_type=F32)
     for j in range(cores):
         for s in range(slots):
             out_refs[s][:, j * part : (j + 1) * part] = total[j][
@@ -276,23 +353,23 @@
             ].astype(BF16)
 
 
-def apply_experts(place, own, moved, gate, up, down, offset, devs):
-    cores, slots = len(offset), len(offset[0])
-    local, part, hidden = gate[0].shape
+def apply_experts(place, own, moved, first, weights, offset, devs):
+    cores, slots = len(offset), len(offset[0])
+    local, part, hidden = weights[0].shape
     rows = own.shape[0]
     return pl.pallas_call(
         functools.partial(expert_kernel, offset, devs),
         out_shape=[jax.ShapeDtypeStruct((rows, part * cores), BF16)] * slots,
-        in_specs=[SMEM, VMEM] + [VMEM] * slots + [ANY] * (3 * cores),
+        in_specs=[SMEM, SMEM, VMEM] + [VMEM] * (slots + 3 * cores) + [ANY] * (3 * cores),
         out_specs=[VMEM] * slots,
         scratch_shapes=[
-            pltpu.VMEM((cores, local, part, hidden), BF16),
-            pltpu.VMEM((cores, local, part, hidden), BF16),
-            pltpu.VMEM((cores, local, hidden, part), BF16),
-            pltpu.SemaphoreType.DMA((3, cores, local)),
+            pltpu.VMEM((cores, local - 1, part, hidden), BF16),
+            pltpu.VMEM((cores, local - 1, part, hidden), BF16),
+            pltpu.VMEM((cores, local - 1, hidden, part), BF16),
+            pltpu.SemaphoreType.DMA((3, cores, local - 1)),
         ],
-        compiler_params=pltpu.CompilerParams(vmem_limit_bytes=56 * MIB),
-    )(place, own, *moved, *gate, *up, *down)
+        compiler_params=pltpu.CompilerParams(vmem_limit_bytes=43 * MIB),
+    )(*place, own, *moved, *first, *weights)
 
 
 def per_device(
@@ -316,8 +393,10 @@
     me = lax.axis_index("dev")
     core = lax.axis_index("pair")
     slots = devs // cores
-    offset = [[c * slots + s for s in range(slots)] for c in range(cores)]
-    place = jnp.stack([me, core]).astype(jnp.int32)
+    offset = TUNED.get(
+        (devs, cores), [[c * slots + s for s in range(slots)] for c in range(cores)]
+    )
+    place = (me.astype(jnp.int32).reshape(1), core.astype(jnp.int32).reshape(1))
     rows, part = residual.shape
     barrier = lax.optimization_barrier
 
@@ -353,26 +432,28 @@
     stream = gathered(residual)
     gain = gathered(norm_gain.reshape(1, part))
     wg = gathered(w_gate)
-    wu = gathered(w_up)
     attended = attend(
         query, stored_keys, stored_values, incoming_key, incoming_value, lengths, place, offset
     )
-    attended, wg, wu, stream, gain = barrier((attended, wg, wu, stream, gain))
+    attended, wg, stream, gain = barrier((attended, wg, stream, gain))
     held = [attended[0]] + [from_core(attended[m], m) for m in range(1, cores)]
-    held, out_weight, w_down = barrier((held, out_weight, w_down))
+    held, out_weight, w_up, w_down = barrier((held, out_weight, w_up, w_down))
     wo = gathered(out_weight)
     outgoing = [jnp.concatenate([h[s] for h in held], axis=0) for s in range(slots)]
     arrived = [swap(outgoing[s], s) for s in range(slots)]
-    arrived, wo, w_down = barrier((arrived, wo, w_down))
-    wd = gathered(w_down)
+    arrived, wo, w_up, w_down = barrier((arrived, wo, w_up, w_down))
+    wu = gathered(w_up)
     partial = project(place, own_block(outgoing), arrived, wo, offset)
     sums = total_of(partial, [swap(partial[s], s) for s in range(slots)])
-    sums, wd = barrier((sums, wd))
+    sums, wu, w_down = barrier((sums, wu, w_down))
     mixed, packed = normalise(
         place, gathered(sums), stream, gain, expert_ids, route_weights, w_gate.shape[0] * devs
     )
+    packed, weights, w_down = barrier((packed, wg + wu, w_down))
     tokens = [swap(packed, s) for s in range(slots)]
-    produced = apply_experts(place, packed, tokens, wg, wu, wd, offset, devs)
+    weights = weights + gathered(w_down)
+    first = fetch(weights)
+    produced = apply_experts(place, packed, tokens, first, weights, offset, devs)
     back = total_of(produced, [swap(produced[s], s) for s in range(slots)])
     result = mixed + back[:, :part]
     for m in range(1, cores):

time: 89.3 us -> 79.8 us (0.89)
  starting transfers between devices: 35.4 us -> 27 us
  waiting for transfers between devices: 27.3 us -> 31.8 us
  Pallas kernels: 21.3 us -> 17 us
  other arithmetic: 2.43 us -> 0.86 us
    ppermute x9, starting transfers between devices: 17.8 us -> 1.72 us  [from_core(): return lax.ppermute(value, 'pair', [(c, c ^ m) for c in range(cores)])]
    ppermute x16, starting transfers between devices: 17.6 us -> 25.3 us  [swap(): return lax.ppermute(value, ('dev', 'pair'), pairs)]
    pallas_call x1, Pallas kernels: 9.48 us -> 5.7 us  [apply_experts(): pl.pallas_call(functools.partial(expert_kernel, offset, devs), out_shape=...]
    pallas_call x0 -> x1, Pallas kernels: none -> 3.79 us  [fetch(): pl.pallas_call(functools.partial(fetch_kernel, count), out_shape=[jax.Sha...]
    ppermute x16, waiting for transfers between devices: 24 us -> 27.5 us  [swap(): return lax.ppermute(value, ('dev', 'pair'), pairs)]
    pallas_call x1, Pallas kernels: 9.88 us -> 6.62 us  [attend(): pl.pallas_call(functools.partial(attend_kernel, kv_heads, offset), out_sh...]
    add x2, other arithmetic: 1.07 us -> 0.16 us  [total_of(): result = result + block.astype(F32)]
    ppermute x9, waiting for transfers between devices: 3.36 us -> 4.25 us  [from_core(): return lax.ppermute(value, 'pair', [(c, c ^ m) for c in range(cores)])]
  transfers between devices with their start and end apart: 25 -> 25, of which waited for: 13 -> 14; matrix products, arithmetic and copies ran while one was open for 2% -> 1% of each run, Pallas kernels for 13% -> 14%
where the time goes in v3:
time: 79.8 us; the launch traced here: 79.5 us
  waiting for transfers between devices  31.8 us (40%)
  starting transfers between devices  27 us (34%)
  Pallas kernels  17 us (21%)
  local copies, waits for them, and re-layouts  2.59 us (3%)
  other arithmetic  0.86 us (1%)
    ppermute x16, waiting for transfers between devices, swap(): return lax.ppermute(value, ('dev', 'pair'), pairs)  27.5 us
    ppermute x16, starting transfers between devices, swap(): return lax.ppermute(value, ('dev', 'pair'), pairs)  25.3 us
    pallas_call x1, Pallas kernels, attend(): pl.pallas_call(functools.partial(attend_kernel, kv_heads, offset), out_sh...  6.62 us
    pallas_call x1, Pallas kernels, apply_experts(): pl.pallas_call(functools.partial(expert_kernel, offset, devs), out_shape=...  5.7 us
    ppermute x9, waiting for transfers between devices, from_core(): return lax.ppermute(value, 'pair', [(c, c ^ m) for c in range(cores)])  4.25 us
    pallas_call x1, Pallas kernels, fetch(): pl.pallas_call(functools.partial(fetch_kernel, count), out_shape=[jax.Sha...  3.79 us
    unnamed x12, local copies, waits for them, and re-layouts  1.74 us
    ppermute x9, starting transfers between devices, from_core(): return lax.ppermute(value, 'pair', [(c, c ^ m) for c in range(cores)])  1.72 us
  transfers between devices with their start and end apart: 25, of which 14 were waited for; matrix products, arithmetic and copies ran while one was open for 1% of the time, Pallas kernels for 14%

profile of v3, /device:TPU:0, one launch (start us, length us, event | category | flops | bytes accessed | tf_op | source)
XLA Modules:
  0.0 79.5 jit_solution(1322906955625243445)
XLA Ops:
  0.0 0.5 collective-permute-start
  0.5 0.1 collective-permute-start.1
  0.5 0.5 collective-permute-start.2
  1.0 6.6 %shard_map.136 = (bf16[4,16,1024]{2,1,0:T(8,128)(2,1)}, bf16[4,16,1024]{2,1,0:T(8,128)(2,1)}) custom-call(s32[16]{0:T(128)} %len_ref.1, s32[1]{0:T(128)} %bitcast.1.me_ref, s32[1]{0:T(128)} %bitcast.core_ref, bf16[16,64,128]{2,1,0:T(8,128)(2,1)} %q_ref.1, bf16[16,1024,128]{2,1,0:T(8,128)(2,1)} %bitcast.27, bf16[16,1024,128]{2,1,0:T(8,128)(2,1)} %bitcast.28, ...), custom_call_target="tpu_custom_call" | custom-call | tf_op jit(solution)/shard_map/pallas_call | solution.py:161
  7.7 0.2 collective-permute-start.3
  7.9 1.4 %collective-permute-done.3 = bf16[4,16,1024]{2,1,0:T(8,128)(2,1)S(1)} collective-permute-done((bf16[4,16,1024]{2,1,0:T(8,128)(2,1)}, bf16[4,16,1024]{2,1,0:T(8,128)(2,1)S(1)}, u32[]{:S(2)}, u32[]{:S(2)}) %collective-permute-start.3) | collective-permute-done | bytes 131104 | tf_op jit(solution)/shard_map/ppermute | solution.py:404
  9.3 0.2 collective-permute-start.8
  9.5 0.8 %slice_bitcast_fusion = (bf16[16,1024]{1,0:T(8,128)(2,1)S(1)}, bf16[16,1024]{1,0:T(8,128)(2,1)S(1)}, bf16[16,1024]{1,0:T(8,128)(2,1)S(1)}, bf16[16,1024]{1,0:T(8...) fusion(bf16[4,16,1024]{2,1,0:T(8,128)(2,1)S(1)} %collective-per, ...), kind=kLoop, calls=%fused_computation.10 | loop fusion | bytes 524288 | tf_op jit(solution)/shard_map/squeeze | solution.py:442
  10.3 4.9 %collective-permute-start.4 = (bf16[32,1024]{1,0:T(8,128)(2,1)S(1)}, bf16[32,1024]{1,0:T(8,128)(2,1)S(1)}, u32[]{:S(2)}, u32[]{:S(2)}) collective-permute-start(bf16[32,1024]{1,0:T(8,128)(2,1)S(1)} %pad_maximum_fusion.1), channel_id=1, source_target_pairs={{0,10},{1,15},{2,8},{3,13},{4,14},{5,11},{6,12},{7,9},{8,2},{9,7},... | collective-permute-start | bytes 196616 | tf_op jit(solution)/shard_map/ppermute | solution.py:416
  15.2 0.7 collective-permute-start.5
  15.9 1.6 %collective-permute-start.6 = (bf16[32,1024]{1,0:T(8,128)(2,1)S(1)}, bf16[32,1024]{1,0:T(8,128)(2,1)S(1)}, u32[]{:S(2)}, u32[]{:S(2)}) collective-permute-start(bf16[32,1024]{1,0:T(8,128)(2,1)S(1)} %pad_maximum_fusion.2), channel_id=1, source_target_pairs={{0,6},{1,5},{2,4},{3,7},{4,2},{5,1},{6,0},{7,3},{8,14},{9,13},{10,... | collective-permute-start | bytes 196616 | tf_op jit(solution)/shard_map/ppermute | solution.py:416
  17.5 0.1 collective-permute-start.7
  17.6 1.7 %collective-permute-done.4.refs_0_ = bf16[32,1024]{1,0:T(8,128)(2,1)S(1)} collective-permute-done((bf16[32,1024]{1,0:T(8,128)(2,1)S(1)}, bf16[32,1024]{1,0:T(8,128)(2,1)S(1)}, u32[]{:S(2)}, u32[]{:S(2)}) %collective-permute-start.4) | collective-permute-done | bytes 65568 | tf_op jit(solution)/shard_map/ppermute | solution.py:416
  19.3 1.9 %collective-permute-done.6.refs_2_ = bf16[32,1024]{1,0:T(8,128)(2,1)S(1)} collective-permute-done((bf16[32,1024]{1,0:T(8,128)(2,1)S(1)}, bf16[32,1024]{1,0:T(8,128)(2,1)S(1)}, u32[]{:S(2)}, u32[]{:S(2)}) %collective-permute-start.6) | collective-permute-done | bytes 65568 | tf_op jit(solution)/shard_map/ppermute | solution.py:416
  21.2 2.9 %collective-permute-done.7.refs_3_ = bf16[32,1024]{1,0:T(8,128)(2,1)S(1)} collective-permute-done((bf16[32,1024]{1,0:T(8,128)(2,1)S(1)}, bf16[32,1024]{1,0:T(8,128)(2,1)S(1)}, u32[]{:S(2)}, u32[]{:S(2)}) %collective-permute-start.7) | collective-permute-done | bytes 65568 | tf_op jit(solution)/shard_map/ppermute | solution.py:416
  24.0 0.7 shard_map.137
  24.8 1.5 %collective-permute-start.12 = (bf16[32,2048]{1,0:T(8,128)(2,1)S(1)}, bf16[32,2048]{1,0:T(8,128)(2,1)S(1)}, u32[]{:S(2)}, u32[]{:S(2)}) collective-permute-start(bf16[32,2048]{1,0:T(8,128)(2,1)S(1)} %get-tuple-element.72), channel_id=1, source_target_pairs={{0,12},{1,9},{2,14},{3,11},{4,8},{5,13},{6,10},{7,15},{8,4},{9,1},... | collective-permute-start | bytes 393224 | tf_op jit(solution)/shard_map/ppermute | solution.py:416
  26.2 0.8 %collective-permute-start.11 = (bf16[32,2048]{1,0:T(8,128)(2,1)S(1)}, bf16[32,2048]{1,0:T(8,128)(2,1)S(1)}, u32[]{:S(2)}, u32[]{:S(2)}) collective-permute-start(bf16[32,2048]{1,0:T(8,128)(2,1)S(1)} %get-tuple-element.71), channel_id=1, source_target_pairs={{0,6},{1,5},{2,4},{3,7},{4,2},{5,1},{6,0},{7,3},{8,14},{9,13},{10,... | collective-permute-start | bytes 393224 | tf_op jit(solution)/shard_map/ppermute | solution.py:416
  27.1 3.1 %collective-permute-start.9 = (bf16[32,2048]{1,0:T(8,128)(2,1)S(1)}, bf16[32,2048]{1,0:T(8,128)(2,1)S(1)}, u32[]{:S(2)}, u32[]{:S(2)}) collective-permute-start(bf16[32,2048]{1,0:T(8,128)(2,1)S(1)} %get-tuple-element.69), channel_id=1, source_target_pairs={{0,10},{1,15},{2,8},{3,13},{4,14},{5,11},{6,12},{7,9},{8,2},{9,7},... | collective-permute-start | bytes 393224 | tf_op jit(solution)/shard_map/ppermute | solution.py:416
  30.1 0.7 collective-permute-start.10
  30.8 2.2 %collective-permute-done.12 = bf16[32,2048]{1,0:T(8,128)(2,1)S(1)} collective-permute-done((bf16[32,2048]{1,0:T(8,128)(2,1)S(1)}, bf16[32,2048]{1,0:T(8,128)(2,1)S(1)}, u32[]{:S(2)}, u32[]{:S(2)}) %collective-permute-start.12) | collective-permute-done | bytes 131104 | tf_op jit(solution)/shard_map/ppermute | solution.py:416
  33.0 2.4 %collective-permute-done.11 = bf16[32,2048]{1,0:T(8,128)(2,1)S(1)} collective-permute-done((bf16[32,2048]{1,0:T(8,128)(2,1)S(1)}, bf16[32,2048]{1,0:T(8,128)(2,1)S(1)}, u32[]{:S(2)}, u32[]{:S(2)}) %collective-permute-start.11) | collective-permute-done | bytes 131104 | tf_op jit(solution)/shard_map/ppermute | solution.py:416
  35.5 5.2 %collective-permute-done.9 = bf16[32,2048]{1,0:T(8,128)(2,1)S(1)} collective-permute-done((bf16[32,2048]{1,0:T(8,128)(2,1)S(1)}, bf16[32,2048]{1,0:T(8,128)(2,1)S(1)}, u32[]{:S(2)}, u32[]{:S(2)}) %collective-permute-start.9) | collective-permute-done | bytes 131104 | tf_op jit(solution)/shard_map/ppermute | solution.py:416
  40.7 0.1 convert_add_fusion.1.refs_0_
  40.8 0.1 collective-permute-start.14
  40.9 1.5 %collective-permute-done.14.refs_1_ = f32[32,2048]{1,0:T(8,128)S(1)} collective-permute-done((f32[32,2048]{1,0:T(8,128)S(1)}, f32[32,2048]{1,0:T(8,128)S(1)}, u32[]{:S(2)}, u32[]{:S(2)}) %collective-permute-start.14) | collective-permute-done | bytes 262176 | tf_op jit(solution)/shard_map/ppermute | solution.py:404
  42.4 0.2 shard_map.138
  42.6 0.2 collective-permute-start.19
  42.8 0.1 collective-permute-start.15
  42.9 0.7 collective-permute-start.16
  43.6 2.6 %collective-permute-start.17 = (bf16[32,2176]{1,0:T(8,128)(2,1)S(1)}, bf16[32,2176]{1,0:T(8,128)(2,1)S(1)}, u32[]{:S(2)}, u32[]{:S(2)}) collective-permute-start(bf16[32,2176]{1,0:T(8,128)(2,1)S(1)} %get-tuple-element.87.own_ref), channel_id=1, source_target_pairs={{0,6},{1,5},{2,4},{3,7},{4,2},{5,1},{6,0},{7,3},{8,14},{9,13},{10,... | collective-permute-start | bytes 417800 | tf_op jit(solution)/shard_map/ppermute | solution.py:416
  46.2 2.6 %collective-permute-start.18 = (bf16[32,2176]{1,0:T(8,128)(2,1)S(1)}, bf16[32,2176]{1,0:T(8,128)(2,1)S(1)}, u32[]{:S(2)}, u32[]{:S(2)}) collective-permute-start(bf16[32,2176]{1,0:T(8,128)(2,1)S(1)} %get-tuple-element.87.own_ref), channel_id=1, source_target_pairs={{0,12},{1,9},{2,14},{3,11},{4,8},{5,13},{6,10},{7,15},{8,4},{9,1},... | collective-permute-start | bytes 417800 | tf_op jit(solution)/shard_map/ppermute | solution.py:416
  48.8 1.7 %copy-done.5 = bf16[2,768,1024]{2,1,0:T(8,128)(2,1)} copy-done((bf16[2,768,1024]{2,1,0:T(8,128)(2,1)}, bf16[2,768,1024]{2,1,0:T(8,128)(2,1)S(1)}, u32[]{:S(2)}) %copy-start.5) | copy-done | bytes 3145752
  50.5 3.8 %shard_map.139 = (bf16[1024,768]{1,0:T(8,128)(2,1)S(1)}, bf16[1024,768]{1,0:T(8,128)(2,1)S(1)}, bf16[1024,768]{1,0:T(8,128)(2,1)S(1)}, bf16[1024,768]{1,0:T(8,12...) custom-call(bf16[2,1024,768]{2,1,0:T(8,128)(2,1)} %refs_10_, ...), custom_call_target="tpu_custom_call" | custom-call | tf_op jit(solution)/shard_map/pallas_call | solution.py:288
  54.3 1.3 %collective-permute-done.17.refs_2_ = bf16[32,2176]{1,0:T(8,128)(2,1)S(1)} collective-permute-done((bf16[32,2176]{1,0:T(8,128)(2,1)S(1)}, bf16[32,2176]{1,0:T(8,128)(2,1)S(1)}, u32[]{:S(2)}, u32[]{:S(2)}) %collective-permute-start.17) | collective-permute-done | bytes 139296 | tf_op jit(solution)/shard_map/ppermute | solution.py:416
  55.6 0.5 collective-permute-done.18.refs_3_
  56.1 5.7 %shard_map.140 = (bf16[32,2048]{1,0:T(8,128)(2,1)S(1)}, bf16[32,2048]{1,0:T(8,128)(2,1)S(1)}, bf16[32,2048]{1,0:T(8,128)(2,1)S(1)}, bf16[32,2048]{1,0:T(8,128)(2,1)S(1)}) custom-call(s32[1]{0:T(128)} %bitcast.1.me_ref, s32[1]{0:T(128)} %bitcast.core_ref, bf16[32,2176]{1,0:T(8,128)(2,1)S(1)} %get-tuple-element.87.own_ref, ...), custom_call_target="tpu_custom_call" | custom-call | tf_op jit(solution)/shard_map/pallas_call | solution.py:360
  61.8 1.3 %collective-permute-start.23 = (bf16[32,2048]{1,0:T(8,128)(2,1)S(1)}, bf16[32,2048]{1,0:T(8,128)(2,1)S(1)}, u32[]{:S(2)}, u32[]{:S(2)}) collective-permute-start(bf16[32,2048]{1,0:T(8,128)(2,1)S(1)} %get-tuple-element.102), channel_id=1, source_target_pairs={{0,12},{1,9},{2,14},{3,11},{4,8},{5,13},{6,10},{7,15},{8,4},{9,1},... | collective-permute-start | bytes 393224 | tf_op jit(solution)/shard_map/ppermute | solution.py:416
  63.1 2.2 %collective-permute-start.22 = (bf16[32,2048]{1,0:T(8,128)(2,1)S(1)}, bf16[32,2048]{1,0:T(8,128)(2,1)S(1)}, u32[]{:S(2)}, u32[]{:S(2)}) collective-permute-start(bf16[32,2048]{1,0:T(8,128)(2,1)S(1)} %get-tuple-element.101), channel_id=1, source_target_pairs={{0,6},{1,5},{2,4},{3,7},{4,2},{5,1},{6,0},{7,3},{8,14},{9,13},{10,... | collective-permute-start | bytes 393224 | tf_op jit(solution)/shard_map/ppermute | solution.py:416
  65.3 1.9 %collective-permute-start.20 = (bf16[32,2048]{1,0:T(8,128)(2,1)S(1)}, bf16[32,2048]{1,0:T(8,128)(2,1)S(1)}, u32[]{:S(2)}, u32[]{:S(2)}) collective-permute-start(bf16[32,2048]{1,0:T(8,128)(2,1)S(1)} %get-tuple-element.99), channel_id=1, source_target_pairs={{0,10},{1,15},{2,8},{3,13},{4,14},{5,11},{6,12},{7,9},{8,2},{9,7},... | collective-permute-start | bytes 393224 | tf_op jit(solution)/shard_map/ppermute | solution.py:416
  67.2 0.7 collective-permute-start.21
  67.8 2.1 %collective-permute-done.23 = bf16[32,2048]{1,0:T(8,128)(2,1)S(1)} collective-permute-done((bf16[32,2048]{1,0:T(8,128)(2,1)S(1)}, bf16[32,2048]{1,0:T(8,128)(2,1)S(1)}, u32[]{:S(2)}, u32[]{:S(2)}) %collective-permute-start.23) | collective-permute-done | bytes 131104 | tf_op jit(solution)/shard_map/ppermute | solution.py:416
  70.0 3.1 %collective-permute-done.22 = bf16[32,2048]{1,0:T(8,128)(2,1)S(1)} collective-permute-done((bf16[32,2048]{1,0:T(8,128)(2,1)S(1)}, bf16[32,2048]{1,0:T(8,128)(2,1)S(1)}, u32[]{:S(2)}, u32[]{:S(2)}) %collective-permute-start.22) | collective-permute-done | bytes 131104 | tf_op jit(solution)/shard_map/ppermute | solution.py:416
  73.1 4.2 %collective-permute-done.20 = bf16[32,2048]{1,0:T(8,128)(2,1)S(1)} collective-permute-done((bf16[32,2048]{1,0:T(8,128)(2,1)S(1)}, bf16[32,2048]{1,0:T(8,128)(2,1)S(1)}, u32[]{:S(2)}, u32[]{:S(2)}) %collective-permute-start.20) | collective-permute-done | bytes 131104 | tf_op jit(solution)/shard_map/ppermute | solution.py:416
  77.3 0.1 convert_add_fusion
  77.4 0.1 collective-permute-start.24
  77.5 1.3 %collective-permute-done.24 = f32[32,1024]{1,0:T(8,128)S(1)} collective-permute-done((f32[32,1024]{1,0:T(8,128)S(1)}, f32[32,1024]{1,0:T(8,128)S(1)}, u32[]{:S(2)}, u32[]{:S(2)}) %collective-permute-start.24) | collective-permute-done | bytes 131104 | tf_op jit(solution)/shard_map/ppermute | solution.py:404
  78.8 0.6 fusion.1
  (31 shorter events, 0.1 us)
Async XLA Ops:
  0.0 7.6 %collective-permute-start = (bf16[2,1024,768]{2,1,0:T(8,128)(2,1)}, bf16[2,1024,768]{2,1,0:T(8,128)(2,1)}, u32[]{:S(2)}, u32[]{:S(2)}) collective-permute-start(bf16[2,1024,768]{2,1,0:T(8,128)(2,1)} %refs_10_), channel_id=1, source_target_pairs={{0,1},{1,0},{2,3},{3,2},{4,5},{5,4},{6,7},{7,6},{8,9},{9,8},{10,11... | collective-permute-start | bytes 9437192 | tf_op jit(solution)/shard_map/ppermute | solution.py:404
  0.5 7.2 %collective-permute-start.1 = (bf16[32,1024]{1,0:T(8,128)(2,1)}, bf16[32,1024]{1,0:T(8,128)(2,1)S(1)}, u32[]{:S(2)}, u32[]{:S(2)}) collective-permute-start(bf16[32,1024]{1,0:T(8,128)(2,1)} %refs_2_), channel_id=1, source_target_pairs={{0,1},{1,0},{2,3},{3,2},{4,5},{5,4},{6,7},{7,6},{8,9},{9,8},{10,11... | collective-permute-start | bytes 196616 | tf_op jit(solution)/shard_map/ppermute | solution.py:404
  0.5 7.1 %collective-permute-start.2 = (f32[1,1024]{1,0:T(1,128)}, f32[1,1024]{1,0:T(1,128)S(1)}, u32[]{:S(2)}, u32[]{:S(2)}) collective-permute-start(f32[1,1024]{1,0:T(1,128)} %bitcast.23), channel_id=1, source_target_pairs={{0,1},{1,0},{2,3},{3,2},{4,5},{5,4},{6,7},{7,6},{8,9},{9,8},{10,11... | collective-permute-start | bytes 12296 | tf_op jit(solution)/shard_map/ppermute | solution.py:404
  1.0 8.3 %copy-start = (bf16[1024,1024]{1,0:T(8,128)(2,1)S(1)}, bf16[1024,1024]{1,0:T(8,128)(2,1)}, u32[]{:S(2)}) copy-start(bf16[1024,1024]{1,0:T(8,128)(2,1)} %refs_4_) | copy-start | bytes 6291460
  7.6 34.8 %copy-start.1 = (bf16[32,1024]{1,0:T(8,128)(2,1)S(1)}, bf16[32,1024]{1,0:T(8,128)(2,1)}, u32[]{:S(2)}) copy-start(bf16[32,1024]{1,0:T(8,128)(2,1)} %refs_2_) | copy-start | bytes 196612
  7.6 34.7 %copy-start.2 = (f32[1024]{0:T(1024)S(1)}, f32[1024]{0:T(1024)}, u32[]{:S(2)}) copy-start(f32[1024]{0:T(1024)} %param.22) | copy-start | bytes 12292
  7.6 34.7 %copy-start.3 = (s32[32,8]{0,1:T(8,128)S(1)}, s32[32,8]{0,1:T(8,128)}, u32[]{:S(2)}) copy-start(s32[32,8]{0,1:T(8,128)} %param.23) | copy-start | bytes 3076
  7.7 34.7 %copy-start.4 = (f32[32,8]{0,1:T(8,128)S(1)}, f32[32,8]{0,1:T(8,128)}, u32[]{:S(2)}) copy-start(f32[32,8]{0,1:T(8,128)} %param.24) | copy-start | bytes 3076
  7.7 1.6 %collective-permute-start.3 = (bf16[4,16,1024]{2,1,0:T(8,128)(2,1)}, bf16[4,16,1024]{2,1,0:T(8,128)(2,1)S(1)}, u32[]{:S(2)}, u32[]{:S(2)}) collective-permute-start(bf16[4,16,1024]{2,1,0:T(8,128)(2,1)} %get-tuple-element.57), channel_id=1, source_target_pairs={{0,1},{1,0},{2,3},{3,2},{4,5},{5,4},{6,7},{7,6},{8,9},{9,8},{10,11... | collective-permute-start | bytes 393224 | tf_op jit(solution)/shard_map/ppermute | solution.py:404
  9.3 14.7 %collective-permute-start.8 = (bf16[1024,1024]{1,0:T(8,128)(2,1)S(1)}, bf16[1024,1024]{1,0:T(8,128)(2,1)S(1)}, u32[]{:S(2)}, u32[]{:S(2)}) collective-permute-start(bf16[1024,1024]{1,0:T(8,128)(2,1)S(1)} %copy-done), channel_id=1, source_target_pairs={{0,1},{1,0},{2,3},{3,2},{4,5},{5,4},{6,7},{7,6},{8,9},{9,8},{10,11... | collective-permute-start | bytes 6291464 | tf_op jit(solution)/shard_map/ppermute | solution.py:404
  10.3 9.0 %collective-permute-start.4 = (bf16[32,1024]{1,0:T(8,128)(2,1)S(1)}, bf16[32,1024]{1,0:T(8,128)(2,1)S(1)}, u32[]{:S(2)}, u32[]{:S(2)}) collective-permute-start(bf16[32,1024]{1,0:T(8,128)(2,1)S(1)} %pad_maximum_fusion.1), channel_id=1, source_target_pairs={{0,10},{1,15},{2,8},{3,13},{4,14},{5,11},{6,12},{7,9},{8,2},{9,7},... | collective-permute-start | bytes 196616 | tf_op jit(solution)/shard_map/ppermute | solution.py:416
  15.2 4.1 %collective-permute-start.5 = (bf16[32,1024]{1,0:T(8,128)(2,1)S(1)}, bf16[32,1024]{1,0:T(8,128)(2,1)S(1)}, u32[]{:S(2)}, u32[]{:S(2)}) collective-permute-start(bf16[32,1024]{1,0:T(8,128)(2,1)S(1)} %pad_maximum_fusion.own_ref), channel_id=1, source_target_pairs={{1,3},{3,1},{5,7},{7,5},{9,11},{11,9},{13,15},{15,13},{17,19},{19,... | collective-permute-start | bytes 196616 | tf_op jit(solution)/shard_map/ppermute | solution.py:416
  15.9 5.3 %collective-permute-start.6 = (bf16[32,1024]{1,0:T(8,128)(2,1)S(1)}, bf16[32,1024]{1,0:T(8,128)(2,1)S(1)}, u32[]{:S(2)}, u32[]{:S(2)}) collective-permute-start(bf16[32,1024]{1,0:T(8,128)(2,1)S(1)} %pad_maximum_fusion.2), channel_id=1, source_target_pairs={{0,6},{1,5},{2,4},{3,7},{4,2},{5,1},{6,0},{7,3},{8,14},{9,13},{10,... | collective-permute-start | bytes 196616 | tf_op jit(solution)/shard_map/ppermute | solution.py:416
  17.5 6.5 %collective-permute-start.7 = (bf16[32,1024]{1,0:T(8,128)(2,1)S(1)}, bf16[32,1024]{1,0:T(8,128)(2,1)S(1)}, u32[]{:S(2)}, u32[]{:S(2)}) collective-permute-start(bf16[32,1024]{1,0:T(8,128)(2,1)S(1)} %pad_maximum_fusion.3), channel_id=1, source_target_pairs={{0,12},{1,9},{2,14},{3,11},{4,8},{5,13},{6,10},{7,15},{8,4},{9,1},... | collective-permute-start | bytes 196616 | tf_op jit(solution)/shard_map/ppermute | solution.py:416
  24.0 16.7 %collective-permute-start.13 = (bf16[2,1024,768]{2,1,0:T(8,128)(2,1)}, bf16[2,1024,768]{2,1,0:T(8,128)(2,1)}, u32[]{:S(2)}, u32[]{:S(2)}) collective-permute-start(bf16[2,1024,768]{2,1,0:T(8,128)(2,1)} %refs_12_), channel_id=1, source_target_pairs={{0,1},{1,0},{2,3},{3,2},{4,5},{5,4},{6,7},{7,6},{8,9},{9,8},{10,11... | collective-permute-start | bytes 9437192 | tf_op jit(solution)/shard_map/ppermute | solution.py:404
  24.8 8.2 %collective-permute-start.12 = (bf16[32,2048]{1,0:T(8,128)(2,1)S(1)}, bf16[32,2048]{1,0:T(8,128)(2,1)S(1)}, u32[]{:S(2)}, u32[]{:S(2)}) collective-permute-start(bf16[32,2048]{1,0:T(8,128)(2,1)S(1)} %get-tuple-element.72), channel_id=1, source_target_pairs={{0,12},{1,9},{2,14},{3,11},{4,8},{5,13},{6,10},{7,15},{8,4},{9,1},... | collective-permute-start | bytes 393224 | tf_op jit(solution)/shard_map/ppermute | solution.py:416
  26.2 9.2 %collective-permute-start.11 = (bf16[32,2048]{1,0:T(8,128)(2,1)S(1)}, bf16[32,2048]{1,0:T(8,128)(2,1)S(1)}, u32[]{:S(2)}, u32[]{:S(2)}) collective-permute-start(bf16[32,2048]{1,0:T(8,128)(2,1)S(1)} %get-tuple-element.71), channel_id=1, source_target_pairs={{0,6},{1,5},{2,4},{3,7},{4,2},{5,1},{6,0},{7,3},{8,14},{9,13},{10,... | collective-permute-start | bytes 393224 | tf_op jit(solution)/shard_map/ppermute | solution.py:416
  27.1 13.6 %collective-permute-start.9 = (bf16[32,2048]{1,0:T(8,128)(2,1)S(1)}, bf16[32,2048]{1,0:T(8,128)(2,1)S(1)}, u32[]{:S(2)}, u32[]{:S(2)}) collective-permute-start(bf16[32,2048]{1,0:T(8,128)(2,1)S(1)} %get-tuple-element.69), channel_id=1, source_target_pairs={{0,10},{1,15},{2,8},{3,13},{4,14},{5,11},{6,12},{7,9},{8,2},{9,7},... | collective-permute-start | bytes 393224 | tf_op jit(solution)/shard_map/ppermute | solution.py:416
  30.1 10.5 %collective-permute-start.10 = (bf16[32,2048]{1,0:T(8,128)(2,1)S(1)}, bf16[32,2048]{1,0:T(8,128)(2,1)S(1)}, u32[]{:S(2)}, u32[]{:S(2)}) collective-permute-start(bf16[32,2048]{1,0:T(8,128)(2,1)S(1)} %get-tuple-element.70), channel_id=1, source_target_pairs={{1,3},{3,1},{5,7},{7,5},{9,11},{11,9},{13,15},{15,13},{17,19},{19,... | collective-permute-start | bytes 393224 | tf_op jit(solution)/shard_map/ppermute | solution.py:416
  40.8 1.6 %collective-permute-start.14 = (f32[32,2048]{1,0:T(8,128)S(1)}, f32[32,2048]{1,0:T(8,128)S(1)}, u32[]{:S(2)}, u32[]{:S(2)}) collective-permute-start(f32[32,2048]{1,0:T(8,128)S(1)} %convert_add_fusion.1.refs_0_), channel_id=1, source_target_pairs={{0,1},{1,0},{2,3},{3,2},{4,5},{5,4},{6,7},{7,6},{8,9},{9,8},{10,11... | collective-permute-start | bytes 786440 | tf_op jit(solution)/shard_map/ppermute | solution.py:404
  42.6 6.2 %collective-permute-start.19 = (bf16[2,768,1024]{2,1,0:T(8,128)(2,1)}, bf16[2,768,1024]{2,1,0:T(8,128)(2,1)S(1)}, u32[]{:S(2)}, u32[]{:S(2)}) collective-permute-start(bf16[2,768,1024]{2,1,0:T(8,128)(2,1)} %refs_14_), channel_id=1, source_target_pairs={{0,1},{1,0},{2,3},{3,2},{4,5},{5,4},{6,7},{7,6},{8,9},{9,8},{10,11... | collective-permute-start | bytes 9437192 | tf_op jit(solution)/shard_map/ppermute | solution.py:404
  42.8 11.5 %collective-permute-start.15 = (bf16[32,2176]{1,0:T(8,128)(2,1)S(1)}, bf16[32,2176]{1,0:T(8,128)(2,1)S(1)}, u32[]{:S(2)}, u32[]{:S(2)}) collective-permute-start(bf16[32,2176]{1,0:T(8,128)(2,1)S(1)} %get-tuple-element.87.own_ref), channel_id=1, source_target_pairs={{0,10},{1,15},{2,8},{3,13},{4,14},{5,11},{6,12},{7,9},{8,2},{9,7},... | collective-permute-start | bytes 417800 | tf_op jit(solution)/shard_map/ppermute | solution.py:416
  42.9 11.4 %collective-permute-start.16 = (bf16[32,2176]{1,0:T(8,128)(2,1)S(1)}, bf16[32,2176]{1,0:T(8,128)(2,1)S(1)}, u32[]{:S(2)}, u32[]{:S(2)}) collective-permute-start(bf16[32,2176]{1,0:T(8,128)(2,1)S(1)} %get-tuple-element.87.own_ref), channel_id=1, source_target_pairs={{1,3},{3,1},{5,7},{7,5},{9,11},{11,9},{13,15},{15,13},{17,19},{19,... | collective-permute-start | bytes 417800 | tf_op jit(solution)/shard_map/ppermute | solution.py:416
  43.6 12.0 %collective-permute-start.17 = (bf16[32,2176]{1,0:T(8,128)(2,1)S(1)}, bf16[32,2176]{1,0:T(8,128)(2,1)S(1)}, u32[]{:S(2)}, u32[]{:S(2)}) collective-permute-start(bf16[32,2176]{1,0:T(8,128)(2,1)S(1)} %get-tuple-element.87.own_ref), channel_id=1, source_target_pairs={{0,6},{1,5},{2,4},{3,7},{4,2},{5,1},{6,0},{7,3},{8,14},{9,13},{10,... | collective-permute-start | bytes 417800 | tf_op jit(solution)/shard_map/ppermute | solution.py:416
  46.2 9.9 %collective-permute-start.18 = (bf16[32,2176]{1,0:T(8,128)(2,1)S(1)}, bf16[32,2176]{1,0:T(8,128)(2,1)S(1)}, u32[]{:S(2)}, u32[]{:S(2)}) collective-permute-start(bf16[32,2176]{1,0:T(8,128)(2,1)S(1)} %get-tuple-element.87.own_ref), channel_id=1, source_target_pairs={{0,12},{1,9},{2,14},{3,11},{4,8},{5,13},{6,10},{7,15},{8,4},{9,1},... | collective-permute-start | bytes 417800 | tf_op jit(solution)/shard_map/ppermute | solution.py:416
  48.8 1.7 %copy-start.5 = (bf16[2,768,1024]{2,1,0:T(8,128)(2,1)}, bf16[2,768,1024]{2,1,0:T(8,128)(2,1)S(1)}, u32[]{:S(2)}) copy-start(bf16[2,768,1024]{2,1,0:T(8,128)(2,1)S(1)} %collective-permute-done.19.refs_5_.refs_15_) | copy-start | bytes 9437188
  61.8 8.2 %collective-permute-start.23 = (bf16[32,2048]{1,0:T(8,128)(2,1)S(1)}, bf16[32,2048]{1,0:T(8,128)(2,1)S(1)}, u32[]{:S(2)}, u32[]{:S(2)}) collective-permute-start(bf16[32,2048]{1,0:T(8,128)(2,1)S(1)} %get-tuple-element.102), channel_id=1, source_target_pairs={{0,12},{1,9},{2,14},{3,11},{4,8},{5,13},{6,10},{7,15},{8,4},{9,1},... | collective-permute-start | bytes 393224 | tf_op jit(solution)/shard_map/ppermute | solution.py:416
  63.1 10.0 %collective-permute-start.22 = (bf16[32,2048]{1,0:T(8,128)(2,1)S(1)}, bf16[32,2048]{1,0:T(8,128)(2,1)S(1)}, u32[]{:S(2)}, u32[]{:S(2)}) collective-permute-start(bf16[32,2048]{1,0:T(8,128)(2,1)S(1)} %get-tuple-element.101), channel_id=1, source_target_pairs={{0,6},{1,5},{2,4},{3,7},{4,2},{5,1},{6,0},{7,3},{8,14},{9,13},{10,... | collective-permute-start | bytes 393224 | tf_op jit(solution)/shard_map/ppermute | solution.py:416
  65.3 12.0 %collective-permute-start.20 = (bf16[32,2048]{1,0:T(8,128)(2,1)S(1)}, bf16[32,2048]{1,0:T(8,128)(2,1)S(1)}, u32[]{:S(2)}, u32[]{:S(2)}) collective-permute-start(bf16[32,2048]{1,0:T(8,128)(2,1)S(1)} %get-tuple-element.99), channel_id=1, source_target_pairs={{0,10},{1,15},{2,8},{3,13},{4,14},{5,11},{6,12},{7,9},{8,2},{9,7},... | collective-permute-start | bytes 393224 | tf_op jit(solution)/shard_map/ppermute | solution.py:416
  67.2 10.1 %collective-permute-start.21 = (bf16[32,2048]{1,0:T(8,128)(2,1)S(1)}, bf16[32,2048]{1,0:T(8,128)(2,1)S(1)}, u32[]{:S(2)}, u32[]{:S(2)}) collective-permute-start(bf16[32,2048]{1,0:T(8,128)(2,1)S(1)} %get-tuple-element.100), channel_id=1, source_target_pairs={{1,3},{3,1},{5,7},{7,5},{9,11},{11,9},{13,15},{15,13},{17,19},{19,... | collective-permute-start | bytes 393224 | tf_op jit(solution)/shard_map/ppermute | solution.py:416
  77.4 1.4 %collective-permute-start.24 = (f32[32,1024]{1,0:T(8,128)S(1)}, f32[32,1024]{1,0:T(8,128)S(1)}, u32[]{:S(2)}, u32[]{:S(2)}) collective-permute-start(f32[32,1024]{1,0:T(8,128)S(1)} %slice.57), channel_id=1, source_target_pairs={{0,1},{1,0},{2,3},{3,2},{4,5},{5,4},{6,7},{7,6},{8,9},{9,8},{10,11... | collective-permute-start | bytes 393224 | tf_op jit(solution)/shard_map/ppermute | solution.py:404

commit v4 on v3

--- a/solution.py
+++ b/solution.py
@@ -38,11 +38,11 @@
 
 
 def attend_kernel(
-    kv_heads, offset, len_ref, me_ref, core_ref, q_ref, k_hbm, v_hbm, ik_ref, iv_ref, *refs
+    kv_heads, offset, len_ref, me_ref, core_ref, q_hbm, k_hbm, v_hbm, ik_hbm, iv_hbm, *refs
 ):
     cores, slots = len(offset), len(offset[0])
     out_refs = refs[:cores]
-    k_buf, v_buf, mask_ref, all_ref, order_ref, sems = refs[cores:]
+    q_ref, ik_ref, iv_ref, k_buf, v_buf, mask_ref, all_ref, order_ref, sems, small_sems = refs[cores:]
     rows, heads, size = q_ref.shape
     span = k_buf.shape[1]
     per = heads // kv_heads
@@ -51,6 +51,15 @@
     step = 4
     chunks = 4
     chunk = span // chunks
+
+    small = [
+        pltpu.make_async_copy(source, target, small_sems.at[n])
+        for n, (source, target) in enumerate(
+            ((q_hbm, q_ref), (ik_hbm, ik_ref), (iv_hbm, iv_ref))
+        )
+    ]
+    for copy in small:
+        copy.start()
 
     lengths = [len_ref[r] for r in range(rows)]
     ranks = [jnp.int32(0)] * rows
@@ -140,6 +149,8 @@
         by_length(i, work)
         return carry
 
+    for copy in small:
+        copy.wait()
     lax.fori_loop(0, rows // step, body, 0)
     me, core = me_ref[0], core_ref[0]
     for m in range(cores):
@@ -161,15 +172,19 @@
     return pl.pallas_call(
         functools.partial(attend_kernel, kv_heads, offset),
         out_shape=[jax.ShapeDtypeStruct((slots, rows, width), BF16)] * cores,
-        in_specs=[SMEM, SMEM, SMEM, VMEM, ANY, ANY, VMEM, VMEM],
+        in_specs=[SMEM, SMEM, SMEM] + [ANY] * 5,
         out_specs=[VMEM] * cores,
         scratch_shapes=[
+            pltpu.VMEM(query.shape, BF16),
+            pltpu.VMEM(fresh_key.shape, BF16),
+            pltpu.VMEM(fresh_value.shape, BF16),
             pltpu.VMEM((rows, span, size), BF16),
             pltpu.VMEM((rows, span, size), BF16),
             pltpu.VMEM((heads, span), jnp.int32),
             pltpu.VMEM((heads * rows, size), F32),
             pltpu.SMEM((rows,), jnp.int32),
             pltpu.SemaphoreType.DMA((2, rows)),
+            pltpu.SemaphoreType.DMA((3,)),
         ],
         compiler_params=pltpu.CompilerParams(vmem_limit_bytes=60 * MIB),
     )(
@@ -291,7 +306,7 @@
         in_specs=[ANY] * count,
         out_specs=[VMEM] * count,
         scratch_shapes=[pltpu.SemaphoreType.DMA((count,))],
-        compiler_params=pltpu.CompilerParams(vmem_limit_bytes=43 * MIB),
+        compiler_params=pltpu.CompilerParams(vmem_limit_bytes=42 * MIB),
     )(*weights)
 
 
@@ -368,7 +383,7 @@
             pltpu.VMEM((cores, local - 1, hidden, part), BF16),
             pltpu.SemaphoreType.DMA((3, cores, local - 1)),
         ],
-        compiler_params=pltpu.CompilerParams(vmem_limit_bytes=43 * MIB),
+        compiler_params=pltpu.CompilerParams(vmem_limit_bytes=42 * MIB),
     )(*place, own, *moved, *first, *weights)
 
 
@@ -419,7 +434,7 @@
 
     def total_of(own, moved):
         result = 0.0
-        for s in range(slots):
+        for s in (2, 3, 0, 1):
             block = moved[s]
             for c in own_slot[s]:
                 block = jnp.where(core == c, own[s], block)

time: 79.8 us -> 78.3 us (0.981)
  starting transfers between devices: 27 us -> 26 us
    ppermute x16, starting transfers between devices: 25.3 us -> 24.4 us  [swap(): return lax.ppermute(value, ('dev', 'pair'), pairs)]
  transfers between devices with their start and end apart: 25 -> 25, of which waited for: 14 -> 11; matrix products, arithmetic and copies ran while one was open for 1% -> 1% of each run, Pallas kernels for 14% -> 14%
where the time goes in v4:
time: 78.3 us; the launch traced here: 78.2 us
  waiting for transfers between devices  31.5 us (40%)
  starting transfers between devices  26 us (33%)
  Pallas kernels  17.1 us (22%)
  local copies, waits for them, and re-layouts  2.59 us (3%)
  other arithmetic  0.86 us (1%)
    ppermute x16, waiting for transfers between devices, swap(): return lax.ppermute(value, ('dev', 'pair'), pairs)  27 us
    ppermute x16, starting transfers between devices, swap(): return lax.ppermute(value, ('dev', 'pair'), pairs)  24.4 us
    pallas_call x1, Pallas kernels, attend(): pl.pallas_call(functools.partial(attend_kernel, kv_heads, offset), out_sh...  6.71 us
    pallas_call x1, Pallas kernels, apply_experts(): pl.pallas_call(functools.partial(expert_kernel, offset, devs), out_shape=...  5.7 us
    ppermute x9, waiting for transfers between devices, from_core(): return lax.ppermute(value, 'pair', [(c, c ^ m) for c in range(cores)])  4.42 us
    pallas_call x1, Pallas kernels, fetch(): pl.pallas_call(functools.partial(fetch_kernel, count), out_shape=[jax.Sha...  3.79 us
    unnamed x12, local copies, waits for them, and re-layouts  1.74 us
  transfers between devices with their start and end apart: 25, of which 11 were waited for; matrix products, arithmetic and copies ran while one was open for 1% of the time, Pallas kernels for 14%

profile of v4, /device:TPU:0, one launch (start us, length us, event | category | flops | bytes accessed | tf_op | source)
XLA Modules:
  0.0 78.2 jit_solution(13158429765004250537)
XLA Ops:
  0.0 0.5 collective-permute-start
  0.5 0.1 collective-permute-start.1
  0.5 0.5 collective-permute-start.2
  1.0 6.7 %shard_map.136 = (bf16[4,16,1024]{2,1,0:T(8,128)(2,1)}, bf16[4,16,1024]{2,1,0:T(8,128)(2,1)}) custom-call(s32[16]{0:T(128)} %len_ref.1, s32[1]{0:T(128)} %bitcast.1.me_ref, s32[1]{0:T(128)} %bitcast.core_ref, bf16[16,64,128]{2,1,0:T(8,128)(2,1)} %q_hbm.1, bf16[16,1024,128]{2,1,0:T(8,128)(2,1)} %bitcast.27, bf16[16,1024,128]{2,1,0:T(8,128)(2,1)} %bitcast.28, ...), custom_call_target="tpu_custom_call" | custom-call | tf_op jit(solution)/shard_map/pallas_call | solution.py:172
  7.7 0.0 copy-start.1
  7.7 0.0 copy-start.2
  7.7 0.0 copy-start.3
  7.7 0.0 copy-start.4
  7.8 0.1 collective-permute-start.3
  7.8 1.5 %collective-permute-done.3 = bf16[4,16,1024]{2,1,0:T(8,128)(2,1)S(1)} collective-permute-done((bf16[4,16,1024]{2,1,0:T(8,128)(2,1)}, bf16[4,16,1024]{2,1,0:T(8,128)(2,1)S(1)}, u32[]{:S(2)}, u32[]{:S(2)}) %collective-permute-start.3) | collective-permute-done | bytes 131104 | tf_op jit(solution)/shard_map/ppermute | solution.py:419
  9.4 0.1 collective-permute-start.8
  9.5 0.8 %slice_bitcast_fusion = (bf16[16,1024]{1,0:T(8,128)(2,1)S(1)}, bf16[16,1024]{1,0:T(8,128)(2,1)S(1)}, bf16[16,1024]{1,0:T(8,128)(2,1)S(1)}, bf16[16,1024]{1,0:T(8...) fusion(bf16[4,16,1024]{2,1,0:T(8,128)(2,1)S(1)} %collective-per, ...), kind=kLoop, calls=%fused_computation.10 | loop fusion | bytes 524288 | tf_op jit(solution)/shard_map/squeeze | solution.py:457
  10.4 4.7 %collective-permute-start.4 = (bf16[32,1024]{1,0:T(8,128)(2,1)S(1)}, bf16[32,1024]{1,0:T(8,128)(2,1)S(1)}, u32[]{:S(2)}, u32[]{:S(2)}) collective-permute-start(bf16[32,1024]{1,0:T(8,128)(2,1)S(1)} %pad_maximum_fusion.1), channel_id=1, source_target_pairs={{0,10},{1,15},{2,8},{3,13},{4,14},{5,11},{6,12},{7,9},{8,2},{9,7},... | collective-permute-start | bytes 196616 | tf_op jit(solution)/shard_map/ppermute | solution.py:431
  15.1 0.7 collective-permute-start.5
  15.8 1.6 %collective-permute-start.6 = (bf16[32,1024]{1,0:T(8,128)(2,1)S(1)}, bf16[32,1024]{1,0:T(8,128)(2,1)S(1)}, u32[]{:S(2)}, u32[]{:S(2)}) collective-permute-start(bf16[32,1024]{1,0:T(8,128)(2,1)S(1)} %pad_maximum_fusion.2), channel_id=1, source_target_pairs={{0,6},{1,5},{2,4},{3,7},{4,2},{5,1},{6,0},{7,3},{8,14},{9,13},{10,... | collective-permute-start | bytes 196616 | tf_op jit(solution)/shard_map/ppermute | solution.py:431
  17.4 0.1 collective-permute-start.7
  17.5 1.8 %collective-permute-done.4.refs_0_ = bf16[32,1024]{1,0:T(8,128)(2,1)S(1)} collective-permute-done((bf16[32,1024]{1,0:T(8,128)(2,1)S(1)}, bf16[32,1024]{1,0:T(8,128)(2,1)S(1)}, u32[]{:S(2)}, u32[]{:S(2)}) %collective-permute-start.4) | collective-permute-done | bytes 65568 | tf_op jit(solution)/shard_map/ppermute | solution.py:431
  19.3 1.8 %collective-permute-done.6.refs_2_ = bf16[32,1024]{1,0:T(8,128)(2,1)S(1)} collective-permute-done((bf16[32,1024]{1,0:T(8,128)(2,1)S(1)}, bf16[32,1024]{1,0:T(8,128)(2,1)S(1)}, u32[]{:S(2)}, u32[]{:S(2)}) %collective-permute-start.6) | collective-permute-done | bytes 65568 | tf_op jit(solution)/shard_map/ppermute | solution.py:431
  21.1 2.9 %collective-permute-done.7.refs_3_ = bf16[32,1024]{1,0:T(8,128)(2,1)S(1)} collective-permute-done((bf16[32,1024]{1,0:T(8,128)(2,1)S(1)}, bf16[32,1024]{1,0:T(8,128)(2,1)S(1)}, u32[]{:S(2)}, u32[]{:S(2)}) %collective-permute-start.7) | collective-permute-done | bytes 65568 | tf_op jit(solution)/shard_map/ppermute | solution.py:431
  24.0 0.7 shard_map.137
  24.7 1.5 %collective-permute-start.11 = (bf16[32,2048]{1,0:T(8,128)(2,1)S(1)}, bf16[32,2048]{1,0:T(8,128)(2,1)S(1)}, u32[]{:S(2)}, u32[]{:S(2)}) collective-permute-start(bf16[32,2048]{1,0:T(8,128)(2,1)S(1)} %get-tuple-element.71), channel_id=1, source_target_pairs={{0,10},{1,15},{2,8},{3,13},{4,14},{5,11},{6,12},{7,9},{8,2},{9,7},... | collective-permute-start | bytes 393224 | tf_op jit(solution)/shard_map/ppermute | solution.py:431
  26.2 2.4 %collective-permute-start.10 = (bf16[32,2048]{1,0:T(8,128)(2,1)S(1)}, bf16[32,2048]{1,0:T(8,128)(2,1)S(1)}, u32[]{:S(2)}, u32[]{:S(2)}) collective-permute-start(bf16[32,2048]{1,0:T(8,128)(2,1)S(1)} %get-tuple-element.70), channel_id=1, source_target_pairs={{0,12},{1,9},{2,14},{3,11},{4,8},{5,13},{6,10},{7,15},{8,4},{9,1},... | collective-permute-start | bytes 393224 | tf_op jit(solution)/shard_map/ppermute | solution.py:431
  28.6 0.6 collective-permute-start.9
  29.2 0.7 collective-permute-start.12
  29.9 8.6 %collective-permute-done.11 = bf16[32,2048]{1,0:T(8,128)(2,1)S(1)} collective-permute-done((bf16[32,2048]{1,0:T(8,128)(2,1)S(1)}, bf16[32,2048]{1,0:T(8,128)(2,1)S(1)}, u32[]{:S(2)}, u32[]{:S(2)}) %collective-permute-start.11) | collective-permute-done | bytes 131104 | tf_op jit(solution)/shard_map/ppermute | solution.py:431
  38.5 0.6 collective-permute-done.9
  39.1 0.1 convert_add_fusion.1.refs_0_
  39.2 0.1 collective-permute-start.14
  39.3 1.5 %collective-permute-done.14.refs_1_ = f32[32,2048]{1,0:T(8,128)S(1)} collective-permute-done((f32[32,2048]{1,0:T(8,128)S(1)}, f32[32,2048]{1,0:T(8,128)S(1)}, u32[]{:S(2)}, u32[]{:S(2)}) %collective-permute-start.14) | collective-permute-done | bytes 262176 | tf_op jit(solution)/shard_map/ppermute | solution.py:419
  40.8 0.2 shard_map.138
  41.0 0.2 collective-permute-start.19
  41.2 1.4 %collective-permute-start.15 = (bf16[32,2176]{1,0:T(8,128)(2,1)S(1)}, bf16[32,2176]{1,0:T(8,128)(2,1)S(1)}, u32[]{:S(2)}, u32[]{:S(2)}) collective-permute-start(bf16[32,2176]{1,0:T(8,128)(2,1)S(1)} %get-tuple-element.87.own_ref), channel_id=1, source_target_pairs={{0,10},{1,15},{2,8},{3,13},{4,14},{5,11},{6,12},{7,9},{8,2},{9,7},... | collective-permute-start | bytes 417800 | tf_op jit(solution)/shard_map/ppermute | solution.py:431
  42.6 0.7 collective-permute-start.16
  43.2 1.6 %collective-permute-start.17 = (bf16[32,2176]{1,0:T(8,128)(2,1)S(1)}, bf16[32,2176]{1,0:T(8,128)(2,1)S(1)}, u32[]{:S(2)}, u32[]{:S(2)}) collective-permute-start(bf16[32,2176]{1,0:T(8,128)(2,1)S(1)} %get-tuple-element.87.own_ref), channel_id=1, source_target_pairs={{0,6},{1,5},{2,4},{3,7},{4,2},{5,1},{6,0},{7,3},{8,14},{9,13},{10,... | collective-permute-start | bytes 417800 | tf_op jit(solution)/shard_map/ppermute | solution.py:431
  44.8 2.4 %collective-permute-start.18 = (bf16[32,2176]{1,0:T(8,128)(2,1)S(1)}, bf16[32,2176]{1,0:T(8,128)(2,1)S(1)}, u32[]{:S(2)}, u32[]{:S(2)}) collective-permute-start(bf16[32,2176]{1,0:T(8,128)(2,1)S(1)} %get-tuple-element.87.own_ref), channel_id=1, source_target_pairs={{0,12},{1,9},{2,14},{3,11},{4,8},{5,13},{6,10},{7,15},{8,4},{9,1},... | collective-permute-start | bytes 417800 | tf_op jit(solution)/shard_map/ppermute | solution.py:431
  47.2 1.7 %copy-done.5 = bf16[2,768,1024]{2,1,0:T(8,128)(2,1)} copy-done((bf16[2,768,1024]{2,1,0:T(8,128)(2,1)}, bf16[2,768,1024]{2,1,0:T(8,128)(2,1)S(1)}, u32[]{:S(2)}) %copy-start.5) | copy-done | bytes 3145752
  48.9 3.8 %shard_map.139 = (bf16[1024,768]{1,0:T(8,128)(2,1)S(1)}, bf16[1024,768]{1,0:T(8,128)(2,1)S(1)}, bf16[1024,768]{1,0:T(8,128)(2,1)S(1)}, bf16[1024,768]{1,0:T(8,12...) custom-call(bf16[2,1024,768]{2,1,0:T(8,128)(2,1)} %refs_10_, ...), custom_call_target="tpu_custom_call" | custom-call | tf_op jit(solution)/shard_map/pallas_call | solution.py:303
  52.7 2.6 %collective-permute-done.18.refs_3_ = bf16[32,2176]{1,0:T(8,128)(2,1)S(1)} collective-permute-done((bf16[32,2176]{1,0:T(8,128)(2,1)S(1)}, bf16[32,2176]{1,0:T(8,128)(2,1)S(1)}, u32[]{:S(2)}, u32[]{:S(2)}) %collective-permute-start.18) | collective-permute-done | bytes 139296 | tf_op jit(solution)/shard_map/ppermute | solution.py:431
  55.4 5.7 %shard_map.140 = (bf16[32,2048]{1,0:T(8,128)(2,1)S(1)}, bf16[32,2048]{1,0:T(8,128)(2,1)S(1)}, bf16[32,2048]{1,0:T(8,128)(2,1)S(1)}, bf16[32,2048]{1,0:T(8,128)(2,1)S(1)}) custom-call(s32[1]{0:T(128)} %bitcast.1.me_ref, s32[1]{0:T(128)} %bitcast.core_ref, bf16[32,2176]{1,0:T(8,128)(2,1)S(1)} %get-tuple-element.87.own_ref, ...), custom_call_target="tpu_custom_call" | custom-call | tf_op jit(solution)/shard_map/pallas_call | solution.py:375
  61.1 3.2 %collective-permute-start.22 = (bf16[32,2048]{1,0:T(8,128)(2,1)S(1)}, bf16[32,2048]{1,0:T(8,128)(2,1)S(1)}, u32[]{:S(2)}, u32[]{:S(2)}) collective-permute-start(bf16[32,2048]{1,0:T(8,128)(2,1)S(1)} %get-tuple-element.101), channel_id=1, source_target_pairs={{0,10},{1,15},{2,8},{3,13},{4,14},{5,11},{6,12},{7,9},{8,2},{9,7},... | collective-permute-start | bytes 393224 | tf_op jit(solution)/shard_map/ppermute | solution.py:431
  64.2 2.4 %collective-permute-start.21 = (bf16[32,2048]{1,0:T(8,128)(2,1)S(1)}, bf16[32,2048]{1,0:T(8,128)(2,1)S(1)}, u32[]{:S(2)}, u32[]{:S(2)}) collective-permute-start(bf16[32,2048]{1,0:T(8,128)(2,1)S(1)} %get-tuple-element.100), channel_id=1, source_target_pairs={{0,12},{1,9},{2,14},{3,11},{4,8},{5,13},{6,10},{7,15},{8,4},{9,1},... | collective-permute-start | bytes 393224 | tf_op jit(solution)/shard_map/ppermute | solution.py:431
  66.6 0.7 collective-permute-start.23
  67.3 7.0 %collective-permute-done.22 = bf16[32,2048]{1,0:T(8,128)(2,1)S(1)} collective-permute-done((bf16[32,2048]{1,0:T(8,128)(2,1)S(1)}, bf16[32,2048]{1,0:T(8,128)(2,1)S(1)}, u32[]{:S(2)}, u32[]{:S(2)}) %collective-permute-start.22) | collective-permute-done | bytes 131104 | tf_op jit(solution)/shard_map/ppermute | solution.py:431
  74.3 1.7 %collective-permute-done.20 = bf16[32,2048]{1,0:T(8,128)(2,1)S(1)} collective-permute-done((bf16[32,2048]{1,0:T(8,128)(2,1)S(1)}, bf16[32,2048]{1,0:T(8,128)(2,1)S(1)}, u32[]{:S(2)}, u32[]{:S(2)}) %collective-permute-start.20) | collective-permute-done | bytes 131104 | tf_op jit(solution)/shard_map/ppermute | solution.py:431
  76.0 0.1 convert_add_fusion
  76.1 0.1 collective-permute-start.24
  76.2 1.3 %collective-permute-done.24 = f32[32,1024]{1,0:T(8,128)S(1)} collective-permute-done((f32[32,1024]{1,0:T(8,128)S(1)}, f32[32,1024]{1,0:T(8,128)S(1)}, u32[]{:S(2)}, u32[]{:S(2)}) %collective-permute-start.24) | collective-permute-done | bytes 131104 | tf_op jit(solution)/shard_map/ppermute | solution.py:419
  77.6 0.6 fusion.1
  (31 shorter events, 0.1 us)
Async XLA Ops:
  0.0 7.7 %collective-permute-start = (bf16[2,1024,768]{2,1,0:T(8,128)(2,1)}, bf16[2,1024,768]{2,1,0:T(8,128)(2,1)}, u32[]{:S(2)}, u32[]{:S(2)}) collective-permute-start(bf16[2,1024,768]{2,1,0:T(8,128)(2,1)} %refs_10_), channel_id=1, source_target_pairs={{0,1},{1,0},{2,3},{3,2},{4,5},{5,4},{6,7},{7,6},{8,9},{9,8},{10,11... | collective-permute-start | bytes 9437192 | tf_op jit(solution)/shard_map/ppermute | solution.py:419
  0.5 7.2 %collective-permute-start.1 = (bf16[32,1024]{1,0:T(8,128)(2,1)}, bf16[32,1024]{1,0:T(8,128)(2,1)S(1)}, u32[]{:S(2)}, u32[]{:S(2)}) collective-permute-start(bf16[32,1024]{1,0:T(8,128)(2,1)} %refs_2_), channel_id=1, source_target_pairs={{0,1},{1,0},{2,3},{3,2},{4,5},{5,4},{6,7},{7,6},{8,9},{9,8},{10,11... | collective-permute-start | bytes 196616 | tf_op jit(solution)/shard_map/ppermute | solution.py:419
  0.5 7.2 %collective-permute-start.2 = (f32[1,1024]{1,0:T(1,128)}, f32[1,1024]{1,0:T(1,128)S(1)}, u32[]{:S(2)}, u32[]{:S(2)}) collective-permute-start(f32[1,1024]{1,0:T(1,128)} %bitcast.23), channel_id=1, source_target_pairs={{0,1},{1,0},{2,3},{3,2},{4,5},{5,4},{6,7},{7,6},{8,9},{9,8},{10,11... | collective-permute-start | bytes 12296 | tf_op jit(solution)/shard_map/ppermute | solution.py:419
  1.0 8.4 %copy-start = (bf16[1024,1024]{1,0:T(8,128)(2,1)S(1)}, bf16[1024,1024]{1,0:T(8,128)(2,1)}, u32[]{:S(2)}) copy-start(bf16[1024,1024]{1,0:T(8,128)(2,1)} %refs_4_) | copy-start | bytes 6291460
  7.7 33.1 %copy-start.1 = (bf16[32,1024]{1,0:T(8,128)(2,1)S(1)}, bf16[32,1024]{1,0:T(8,128)(2,1)}, u32[]{:S(2)}) copy-start(bf16[32,1024]{1,0:T(8,128)(2,1)} %refs_2_) | copy-start | bytes 196612
  7.7 33.1 %copy-start.2 = (f32[1024]{0:T(1024)S(1)}, f32[1024]{0:T(1024)}, u32[]{:S(2)}) copy-start(f32[1024]{0:T(1024)} %param.22) | copy-start | bytes 12292
  7.7 33.1 %copy-start.3 = (s32[32,8]{0,1:T(8,128)S(1)}, s32[32,8]{0,1:T(8,128)}, u32[]{:S(2)}) copy-start(s32[32,8]{0,1:T(8,128)} %param.23) | copy-start | bytes 3076
  7.7 33.1 %copy-start.4 = (f32[32,8]{0,1:T(8,128)S(1)}, f32[32,8]{0,1:T(8,128)}, u32[]{:S(2)}) copy-start(f32[32,8]{0,1:T(8,128)} %param.24) | copy-start | bytes 3076
  7.8 1.6 %collective-permute-start.3 = (bf16[4,16,1024]{2,1,0:T(8,128)(2,1)}, bf16[4,16,1024]{2,1,0:T(8,128)(2,1)S(1)}, u32[]{:S(2)}, u32[]{:S(2)}) collective-permute-start(bf16[4,16,1024]{2,1,0:T(8,128)(2,1)} %get-tuple-element.57), channel_id=1, source_target_pairs={{0,1},{1,0},{2,3},{3,2},{4,5},{5,4},{6,7},{7,6},{8,9},{9,8},{10,11... | collective-permute-start | bytes 393224 | tf_op jit(solution)/shard_map/ppermute | solution.py:419
  9.4 14.6 %collective-permute-start.8 = (bf16[1024,1024]{1,0:T(8,128)(2,1)S(1)}, bf16[1024,1024]{1,0:T(8,128)(2,1)S(1)}, u32[]{:S(2)}, u32[]{:S(2)}) collective-permute-start(bf16[1024,1024]{1,0:T(8,128)(2,1)S(1)} %copy-done), channel_id=1, source_target_pairs={{0,1},{1,0},{2,3},{3,2},{4,5},{5,4},{6,7},{7,6},{8,9},{9,8},{10,11... | collective-permute-start | bytes 6291464 | tf_op jit(solution)/shard_map/ppermute | solution.py:419
  10.4 8.9 %collective-permute-start.4 = (bf16[32,1024]{1,0:T(8,128)(2,1)S(1)}, bf16[32,1024]{1,0:T(8,128)(2,1)S(1)}, u32[]{:S(2)}, u32[]{:S(2)}) collective-permute-start(bf16[32,1024]{1,0:T(8,128)(2,1)S(1)} %pad_maximum_fusion.1), channel_id=1, source_target_pairs={{0,10},{1,15},{2,8},{3,13},{4,14},{5,11},{6,12},{7,9},{8,2},{9,7},... | collective-permute-start | bytes 196616 | tf_op jit(solution)/shard_map/ppermute | solution.py:431
  15.1 4.2 %collective-permute-start.5 = (bf16[32,1024]{1,0:T(8,128)(2,1)S(1)}, bf16[32,1024]{1,0:T(8,128)(2,1)S(1)}, u32[]{:S(2)}, u32[]{:S(2)}) collective-permute-start(bf16[32,1024]{1,0:T(8,128)(2,1)S(1)} %pad_maximum_fusion.own_ref), channel_id=1, source_target_pairs={{1,3},{3,1},{5,7},{7,5},{9,11},{11,9},{13,15},{15,13},{17,19},{19,... | collective-permute-start | bytes 196616 | tf_op jit(solution)/shard_map/ppermute | solution.py:431
  15.8 5.3 %collective-permute-start.6 = (bf16[32,1024]{1,0:T(8,128)(2,1)S(1)}, bf16[32,1024]{1,0:T(8,128)(2,1)S(1)}, u32[]{:S(2)}, u32[]{:S(2)}) collective-permute-start(bf16[32,1024]{1,0:T(8,128)(2,1)S(1)} %pad_maximum_fusion.2), channel_id=1, source_target_pairs={{0,6},{1,5},{2,4},{3,7},{4,2},{5,1},{6,0},{7,3},{8,14},{9,13},{10,... | collective-permute-start | bytes 196616 | tf_op jit(solution)/shard_map/ppermute | solution.py:431
  17.4 6.6 %collective-permute-start.7 = (bf16[32,1024]{1,0:T(8,128)(2,1)S(1)}, bf16[32,1024]{1,0:T(8,128)(2,1)S(1)}, u32[]{:S(2)}, u32[]{:S(2)}) collective-permute-start(bf16[32,1024]{1,0:T(8,128)(2,1)S(1)} %pad_maximum_fusion.3), channel_id=1, source_target_pairs={{0,12},{1,9},{2,14},{3,11},{4,8},{5,13},{6,10},{7,15},{8,4},{9,1},... | collective-permute-start | bytes 196616 | tf_op jit(solution)/shard_map/ppermute | solution.py:431
  24.0 15.2 %collective-permute-start.13 = (bf16[2,1024,768]{2,1,0:T(8,128)(2,1)}, bf16[2,1024,768]{2,1,0:T(8,128)(2,1)}, u32[]{:S(2)}, u32[]{:S(2)}) collective-permute-start(bf16[2,1024,768]{2,1,0:T(8,128)(2,1)} %refs_12_), channel_id=1, source_target_pairs={{0,1},{1,0},{2,3},{3,2},{4,5},{5,4},{6,7},{7,6},{8,9},{9,8},{10,11... | collective-permute-start | bytes 9437192 | tf_op jit(solution)/shard_map/ppermute | solution.py:419
  24.7 13.8 %collective-permute-start.11 = (bf16[32,2048]{1,0:T(8,128)(2,1)S(1)}, bf16[32,2048]{1,0:T(8,128)(2,1)S(1)}, u32[]{:S(2)}, u32[]{:S(2)}) collective-permute-start(bf16[32,2048]{1,0:T(8,128)(2,1)S(1)} %get-tuple-element.71), channel_id=1, source_target_pairs={{0,10},{1,15},{2,8},{3,13},{4,14},{5,11},{6,12},{7,9},{8,2},{9,7},... | collective-permute-start | bytes 393224 | tf_op jit(solution)/shard_map/ppermute | solution.py:431
  26.2 12.3 %collective-permute-start.10 = (bf16[32,2048]{1,0:T(8,128)(2,1)S(1)}, bf16[32,2048]{1,0:T(8,128)(2,1)S(1)}, u32[]{:S(2)}, u32[]{:S(2)}) collective-permute-start(bf16[32,2048]{1,0:T(8,128)(2,1)S(1)} %get-tuple-element.70), channel_id=1, source_target_pairs={{0,12},{1,9},{2,14},{3,11},{4,8},{5,13},{6,10},{7,15},{8,4},{9,1},... | collective-permute-start | bytes 393224 | tf_op jit(solution)/shard_map/ppermute | solution.py:431
  28.6 10.5 %collective-permute-start.9 = (bf16[32,2048]{1,0:T(8,128)(2,1)S(1)}, bf16[32,2048]{1,0:T(8,128)(2,1)S(1)}, u32[]{:S(2)}, u32[]{:S(2)}) collective-permute-start(bf16[32,2048]{1,0:T(8,128)(2,1)S(1)} %get-tuple-element.69), channel_id=1, source_target_pairs={{0,6},{1,5},{2,4},{3,7},{4,2},{5,1},{6,0},{7,3},{8,14},{9,13},{10,... | collective-permute-start | bytes 393224 | tf_op jit(solution)/shard_map/ppermute | solution.py:431
  29.2 9.9 %collective-permute-start.12 = (bf16[32,2048]{1,0:T(8,128)(2,1)S(1)}, bf16[32,2048]{1,0:T(8,128)(2,1)S(1)}, u32[]{:S(2)}, u32[]{:S(2)}) collective-permute-start(bf16[32,2048]{1,0:T(8,128)(2,1)S(1)} %get-tuple-element.72), channel_id=1, source_target_pairs={{1,3},{3,1},{5,7},{7,5},{9,11},{11,9},{13,15},{15,13},{17,19},{19,... | collective-permute-start | bytes 393224 | tf_op jit(solution)/shard_map/ppermute | solution.py:431
  39.2 1.6 %collective-permute-start.14 = (f32[32,2048]{1,0:T(8,128)S(1)}, f32[32,2048]{1,0:T(8,128)S(1)}, u32[]{:S(2)}, u32[]{:S(2)}) collective-permute-start(f32[32,2048]{1,0:T(8,128)S(1)} %convert_add_fusion.1.refs_0_), channel_id=1, source_target_pairs={{0,1},{1,0},{2,3},{3,2},{4,5},{5,4},{6,7},{7,6},{8,9},{9,8},{10,11... | collective-permute-start | bytes 786440 | tf_op jit(solution)/shard_map/ppermute | solution.py:419
  41.0 6.2 %collective-permute-start.19 = (bf16[2,768,1024]{2,1,0:T(8,128)(2,1)}, bf16[2,768,1024]{2,1,0:T(8,128)(2,1)S(1)}, u32[]{:S(2)}, u32[]{:S(2)}) collective-permute-start(bf16[2,768,1024]{2,1,0:T(8,128)(2,1)} %refs_14_), channel_id=1, source_target_pairs={{0,1},{1,0},{2,3},{3,2},{4,5},{5,4},{6,7},{7,6},{8,9},{9,8},{10,11... | collective-permute-start | bytes 9437192 | tf_op jit(solution)/shard_map/ppermute | solution.py:419
  41.2 11.5 %collective-permute-start.15 = (bf16[32,2176]{1,0:T(8,128)(2,1)S(1)}, bf16[32,2176]{1,0:T(8,128)(2,1)S(1)}, u32[]{:S(2)}, u32[]{:S(2)}) collective-permute-start(bf16[32,2176]{1,0:T(8,128)(2,1)S(1)} %get-tuple-element.87.own_ref), channel_id=1, source_target_pairs={{0,10},{1,15},{2,8},{3,13},{4,14},{5,11},{6,12},{7,9},{8,2},{9,7},... | collective-permute-start | bytes 417800 | tf_op jit(solution)/shard_map/ppermute | solution.py:431
  42.6 10.2 %collective-permute-start.16 = (bf16[32,2176]{1,0:T(8,128)(2,1)S(1)}, bf16[32,2176]{1,0:T(8,128)(2,1)S(1)}, u32[]{:S(2)}, u32[]{:S(2)}) collective-permute-start(bf16[32,2176]{1,0:T(8,128)(2,1)S(1)} %get-tuple-element.87.own_ref), channel_id=1, source_target_pairs={{1,3},{3,1},{5,7},{7,5},{9,11},{11,9},{13,15},{15,13},{17,19},{19,... | collective-permute-start | bytes 417800 | tf_op jit(solution)/shard_map/ppermute | solution.py:431
  43.2 9.5 %collective-permute-start.17 = (bf16[32,2176]{1,0:T(8,128)(2,1)S(1)}, bf16[32,2176]{1,0:T(8,128)(2,1)S(1)}, u32[]{:S(2)}, u32[]{:S(2)}) collective-permute-start(bf16[32,2176]{1,0:T(8,128)(2,1)S(1)} %get-tuple-element.87.own_ref), channel_id=1, source_target_pairs={{0,6},{1,5},{2,4},{3,7},{4,2},{5,1},{6,0},{7,3},{8,14},{9,13},{10,... | collective-permute-start | bytes 417800 | tf_op jit(solution)/shard_map/ppermute | solution.py:431
  44.8 10.5 %collective-permute-start.18 = (bf16[32,2176]{1,0:T(8,128)(2,1)S(1)}, bf16[32,2176]{1,0:T(8,128)(2,1)S(1)}, u32[]{:S(2)}, u32[]{:S(2)}) collective-permute-start(bf16[32,2176]{1,0:T(8,128)(2,1)S(1)} %get-tuple-element.87.own_ref), channel_id=1, source_target_pairs={{0,12},{1,9},{2,14},{3,11},{4,8},{5,13},{6,10},{7,15},{8,4},{9,1},... | collective-permute-start | bytes 417800 | tf_op jit(solution)/shard_map/ppermute | solution.py:431
  47.2 1.7 %copy-start.5 = (bf16[2,768,1024]{2,1,0:T(8,128)(2,1)}, bf16[2,768,1024]{2,1,0:T(8,128)(2,1)S(1)}, u32[]{:S(2)}) copy-start(bf16[2,768,1024]{2,1,0:T(8,128)(2,1)S(1)} %collective-permute-done.19.refs_5_.refs_15_) | copy-start | bytes 9437188
  61.1 13.2 %collective-permute-start.22 = (bf16[32,2048]{1,0:T(8,128)(2,1)S(1)}, bf16[32,2048]{1,0:T(8,128)(2,1)S(1)}, u32[]{:S(2)}, u32[]{:S(2)}) collective-permute-start(bf16[32,2048]{1,0:T(8,128)(2,1)S(1)} %get-tuple-element.101), channel_id=1, source_target_pairs={{0,10},{1,15},{2,8},{3,13},{4,14},{5,11},{6,12},{7,9},{8,2},{9,7},... | collective-permute-start | bytes 393224 | tf_op jit(solution)/shard_map/ppermute | solution.py:431
  64.2 10.1 %collective-permute-start.21 = (bf16[32,2048]{1,0:T(8,128)(2,1)S(1)}, bf16[32,2048]{1,0:T(8,128)(2,1)S(1)}, u32[]{:S(2)}, u32[]{:S(2)}) collective-permute-start(bf16[32,2048]{1,0:T(8,128)(2,1)S(1)} %get-tuple-element.100), channel_id=1, source_target_pairs={{0,12},{1,9},{2,14},{3,11},{4,8},{5,13},{6,10},{7,15},{8,4},{9,1},... | collective-permute-start | bytes 393224 | tf_op jit(solution)/shard_map/ppermute | solution.py:431
  66.6 9.4 %collective-permute-start.20 = (bf16[32,2048]{1,0:T(8,128)(2,1)S(1)}, bf16[32,2048]{1,0:T(8,128)(2,1)S(1)}, u32[]{:S(2)}, u32[]{:S(2)}) collective-permute-start(bf16[32,2048]{1,0:T(8,128)(2,1)S(1)} %get-tuple-element.99), channel_id=1, source_target_pairs={{0,6},{1,5},{2,4},{3,7},{4,2},{5,1},{6,0},{7,3},{8,14},{9,13},{10,... | collective-permute-start | bytes 393224 | tf_op jit(solution)/shard_map/ppermute | solution.py:431
  66.6 9.4 %collective-permute-start.23 = (bf16[32,2048]{1,0:T(8,128)(2,1)S(1)}, bf16[32,2048]{1,0:T(8,128)(2,1)S(1)}, u32[]{:S(2)}, u32[]{:S(2)}) collective-permute-start(bf16[32,2048]{1,0:T(8,128)(2,1)S(1)} %get-tuple-element.102), channel_id=1, source_target_pairs={{1,3},{3,1},{5,7},{7,5},{9,11},{11,9},{13,15},{15,13},{17,19},{19,... | collective-permute-start | bytes 393224 | tf_op jit(solution)/shard_map/ppermute | solution.py:431
  76.1 1.4 %collective-permute-start.24 = (f32[32,1024]{1,0:T(8,128)S(1)}, f32[32,1024]{1,0:T(8,128)S(1)}, u32[]{:S(2)}, u32[]{:S(2)}) collective-permute-start(f32[32,1024]{1,0:T(8,128)S(1)} %slice.57), channel_id=1, source_target_pairs={{0,1},{1,0},{2,3},{3,2},{4,5},{5,4},{6,7},{7,6},{8,9},{9,8},{10,11... | collective-permute-start | bytes 393224 | tf_op jit(solution)/shard_map/ppermute | solution.py:419

commit v5 on v4

--- a/solution.py
+++ b/solution.py
@@ -451,10 +451,13 @@
         query, stored_keys, stored_values, incoming_key, incoming_value, lengths, place, offset
     )
     attended, wg, stream, gain = barrier((attended, wg, stream, gain))
-    held = [attended[0]] + [from_core(attended[m], m) for m in range(1, cores)]
-    held, out_weight, w_up, w_down = barrier((held, out_weight, w_up, w_down))
+    mine = barrier([attended[0][s] for s in range(slots)])
+    theirs = [from_core(attended[m], m) for m in range(1, cores)]
+    outgoing = [
+        jnp.concatenate([mine[s]] + [block[s] for block in theirs], axis=0) for s in range(slots)
+    ]
+    outgoing, out_weight, w_up, w_down = barrier((outgoing, out_weight, w_up, w_down))
     wo = gathered(out_weight)
-    outgoing = [jnp.concatenate([h[s] for h in held], axis=0) for s in range(slots)]
     arrived = [swap(outgoing[s], s) for s in range(slots)]
     arrived, wo, w_up, w_down = barrier((arrived, wo, w_up, w_down))
     wu = gathered(w_up)

time: 78.3 us -> 77.5 us (0.990)
    ppermute x9, waiting for transfers between devices: 4.42 us -> 3.41 us  [from_core(): return lax.ppermute(value, 'pair', [(c, c ^ m) for c in range(cores)])]
  transfers between devices with their start and end apart: 25 -> 25, of which waited for: 11 -> 12; matrix products, arithmetic and copies ran while one was open for 1% -> 1% of each run, Pallas kernels for 14% -> 14%
where the time goes in v5:
time: 77.5 us; the launch traced here: 77.7 us
  waiting for transfers between devices  31.2 us (40%)
  starting transfers between devices  25.9 us (33%)
  Pallas kernels  16.8 us (22%)
  local copies, waits for them, and re-layouts  2.57 us (3%)
  other arithmetic  0.86 us (1%)
    ppermute x16, waiting for transfers between devices, swap(): return lax.ppermute(value, ('dev', 'pair'), pairs)  27.8 us
    ppermute x16, starting transfers between devices, swap(): return lax.ppermute(value, ('dev', 'pair'), pairs)  24.2 us
    pallas_call x1, Pallas kernels, attend(): pl.pallas_call(functools.partial(attend_kernel, kv_heads, offset), out_sh...  6.47 us
    pallas_call x1, Pallas kernels, apply_experts(): pl.pallas_call(functools.partial(expert_kernel, offset, devs), out_shape=...  5.7 us
    pallas_call x1, Pallas kernels, fetch(): pl.pallas_call(functools.partial(fetch_kernel, count), out_shape=[jax.Sha...  3.79 us
    ppermute x9, waiting for transfers between devices, from_core(): return lax.ppermute(value, 'pair', [(c, c ^ m) for c in range(cores)])  3.41 us
    ppermute x9, starting transfers between devices, from_core(): return lax.ppermute(value, 'pair', [(c, c ^ m) for c in range(cores)])  1.74 us
    unnamed x12, local copies, waits for them, and re-layouts  1.72 us
  transfers between devices with their start and end apart: 25, of which 12 were waited for; matrix products, arithmetic and copies ran while one was open for 1% of the time, Pallas kernels for 14%

profile of v5, /device:TPU:0, one launch (start us, length us, event | category | flops | bytes accessed | tf_op | source)
XLA Modules:
  0.0 77.7 jit_solution(3716871447865646215)
XLA Ops:
  0.0 0.5 collective-permute-start
  0.5 0.1 collective-permute-start.1
  0.5 0.5 collective-permute-start.2
  1.0 6.5 %shard_map.136 = (bf16[4,16,1024]{2,1,0:T(8,128)(2,1)}, bf16[4,16,1024]{2,1,0:T(8,128)(2,1)}) custom-call(s32[16]{0:T(128)} %len_ref.1, s32[1]{0:T(128)} %bitcast.1.me_ref, s32[1]{0:T(128)} %bitcast.core_ref, bf16[16,64,128]{2,1,0:T(8,128)(2,1)} %q_hbm.1, bf16[16,1024,128]{2,1,0:T(8,128)(2,1)} %bitcast.27, bf16[16,1024,128]{2,1,0:T(8,128)(2,1)} %bitcast.28, ...), custom_call_target="tpu_custom_call" | custom-call | tf_op jit(solution)/shard_map/pallas_call | solution.py:172
  7.5 0.2 collective-permute-start.3
  7.7 0.8 %slice_bitcast_fusion.4 = (bf16[16,1024]{1,0:T(8,128)(2,1)S(1)}, bf16[16,1024]{1,0:T(8,128)(2,1)S(1)}, bf16[16,1024]{1,0:T(8,128)(2,1)S(1)}, bf16[16,1024]{1,0:T(8,128)(2,1)S(1)}) fusion(bf16[4,16,1024]{2,1,0:T(8,128)(2,1)} %get-tuple-element.62), kind=kLoop, calls=%fused_computation.14 | loop fusion | bytes 262144 | tf_op jit(solution)/shard_map/squeeze | solution.py:454
  8.5 0.0 copy-start.1
  8.5 0.0 copy-start.3
  8.6 0.0 copy-start.4
  8.6 0.5 collective-permute-done.3
  9.2 0.2 collective-permute-start.8
  9.4 4.7 %collective-permute-start.4 = (bf16[32,1024]{1,0:T(8,128)(2,1)S(1)}, bf16[32,1024]{1,0:T(8,128)(2,1)S(1)}, u32[]{:S(2)}, u32[]{:S(2)}) collective-permute-start(bf16[32,1024]{1,0:T(8,128)(2,1)S(1)} %get-tuple-element.69), channel_id=1, source_target_pairs={{0,10},{1,15},{2,8},{3,13},{4,14},{5,11},{6,12},{7,9},{8,2},{9,7},... | collective-permute-start | bytes 196616 | tf_op jit(solution)/shard_map/ppermute | solution.py:431
  14.1 0.7 collective-permute-start.5
  14.8 1.9 %collective-permute-start.6 = (bf16[32,1024]{1,0:T(8,128)(2,1)S(1)}, bf16[32,1024]{1,0:T(8,128)(2,1)S(1)}, u32[]{:S(2)}, u32[]{:S(2)}) collective-permute-start(bf16[32,1024]{1,0:T(8,128)(2,1)S(1)} %get-tuple-element.70), channel_id=1, source_target_pairs={{0,6},{1,5},{2,4},{3,7},{4,2},{5,1},{6,0},{7,3},{8,14},{9,13},{10,... | collective-permute-start | bytes 196616 | tf_op jit(solution)/shard_map/ppermute | solution.py:431
  16.6 0.1 collective-permute-start.7
  16.8 1.3 %collective-permute-done.4.refs_0_ = bf16[32,1024]{1,0:T(8,128)(2,1)S(1)} collective-permute-done((bf16[32,1024]{1,0:T(8,128)(2,1)S(1)}, bf16[32,1024]{1,0:T(8,128)(2,1)S(1)}, u32[]{:S(2)}, u32[]{:S(2)}) %collective-permute-start.4) | collective-permute-done | bytes 65568 | tf_op jit(solution)/shard_map/ppermute | solution.py:431
  18.1 2.0 %collective-permute-done.6.refs_2_ = bf16[32,1024]{1,0:T(8,128)(2,1)S(1)} collective-permute-done((bf16[32,1024]{1,0:T(8,128)(2,1)S(1)}, bf16[32,1024]{1,0:T(8,128)(2,1)S(1)}, u32[]{:S(2)}, u32[]{:S(2)}) %collective-permute-start.6) | collective-permute-done | bytes 65568 | tf_op jit(solution)/shard_map/ppermute | solution.py:431
  20.0 3.2 %collective-permute-done.7.refs_3_ = bf16[32,1024]{1,0:T(8,128)(2,1)S(1)} collective-permute-done((bf16[32,1024]{1,0:T(8,128)(2,1)S(1)}, bf16[32,1024]{1,0:T(8,128)(2,1)S(1)}, u32[]{:S(2)}, u32[]{:S(2)}) %collective-permute-start.7) | collective-permute-done | bytes 65568 | tf_op jit(solution)/shard_map/ppermute | solution.py:431
  23.3 0.7 shard_map.137
  24.0 1.2 %collective-permute-start.11 = (bf16[32,2048]{1,0:T(8,128)(2,1)S(1)}, bf16[32,2048]{1,0:T(8,128)(2,1)S(1)}, u32[]{:S(2)}, u32[]{:S(2)}) collective-permute-start(bf16[32,2048]{1,0:T(8,128)(2,1)S(1)} %get-tuple-element.83), channel_id=1, source_target_pairs={{0,10},{1,15},{2,8},{3,13},{4,14},{5,11},{6,12},{7,9},{8,2},{9,7},... | collective-permute-start | bytes 393224 | tf_op jit(solution)/shard_map/ppermute | solution.py:431
  25.2 2.4 %collective-permute-start.10 = (bf16[32,2048]{1,0:T(8,128)(2,1)S(1)}, bf16[32,2048]{1,0:T(8,128)(2,1)S(1)}, u32[]{:S(2)}, u32[]{:S(2)}) collective-permute-start(bf16[32,2048]{1,0:T(8,128)(2,1)S(1)} %get-tuple-element.82), channel_id=1, source_target_pairs={{0,12},{1,9},{2,14},{3,11},{4,8},{5,13},{6,10},{7,15},{8,4},{9,1},... | collective-permute-start | bytes 393224 | tf_op jit(solution)/shard_map/ppermute | solution.py:431
  27.6 0.8 %collective-permute-start.9 = (bf16[32,2048]{1,0:T(8,128)(2,1)S(1)}, bf16[32,2048]{1,0:T(8,128)(2,1)S(1)}, u32[]{:S(2)}, u32[]{:S(2)}) collective-permute-start(bf16[32,2048]{1,0:T(8,128)(2,1)S(1)} %get-tuple-element.81), channel_id=1, source_target_pairs={{0,6},{1,5},{2,4},{3,7},{4,2},{5,1},{6,0},{7,3},{8,14},{9,13},{10,... | collective-permute-start | bytes 393224 | tf_op jit(solution)/shard_map/ppermute | solution.py:431
  28.4 0.7 collective-permute-start.12
  29.1 8.6 %collective-permute-done.11 = bf16[32,2048]{1,0:T(8,128)(2,1)S(1)} collective-permute-done((bf16[32,2048]{1,0:T(8,128)(2,1)S(1)}, bf16[32,2048]{1,0:T(8,128)(2,1)S(1)}, u32[]{:S(2)}, u32[]{:S(2)}) %collective-permute-start.11) | collective-permute-done | bytes 131104 | tf_op jit(solution)/shard_map/ppermute | solution.py:431
  37.7 0.6 collective-permute-done.9
  38.3 0.1 convert_add_fusion.1.refs_0_
  38.4 0.1 collective-permute-start.14
  38.5 1.5 %collective-permute-done.14.refs_1_ = f32[32,2048]{1,0:T(8,128)S(1)} collective-permute-done((f32[32,2048]{1,0:T(8,128)S(1)}, f32[32,2048]{1,0:T(8,128)S(1)}, u32[]{:S(2)}, u32[]{:S(2)}) %collective-permute-start.14) | collective-permute-done | bytes 262176 | tf_op jit(solution)/shard_map/ppermute | solution.py:419
  40.1 0.2 shard_map.138
  40.2 0.2 collective-permute-start.19
  40.4 1.4 %collective-permute-start.15 = (bf16[32,2176]{1,0:T(8,128)(2,1)S(1)}, bf16[32,2176]{1,0:T(8,128)(2,1)S(1)}, u32[]{:S(2)}, u32[]{:S(2)}) collective-permute-start(bf16[32,2176]{1,0:T(8,128)(2,1)S(1)} %get-tuple-element.99.own_ref), channel_id=1, source_target_pairs={{0,10},{1,15},{2,8},{3,13},{4,14},{5,11},{6,12},{7,9},{8,2},{9,7},... | collective-permute-start | bytes 417800 | tf_op jit(solution)/shard_map/ppermute | solution.py:431
  41.8 0.7 collective-permute-start.16
  42.5 1.6 %collective-permute-start.17 = (bf16[32,2176]{1,0:T(8,128)(2,1)S(1)}, bf16[32,2176]{1,0:T(8,128)(2,1)S(1)}, u32[]{:S(2)}, u32[]{:S(2)}) collective-permute-start(bf16[32,2176]{1,0:T(8,128)(2,1)S(1)} %get-tuple-element.99.own_ref), channel_id=1, source_target_pairs={{0,6},{1,5},{2,4},{3,7},{4,2},{5,1},{6,0},{7,3},{8,14},{9,13},{10,... | collective-permute-start | bytes 417800 | tf_op jit(solution)/shard_map/ppermute | solution.py:431
  44.1 2.4 %collective-permute-start.18 = (bf16[32,2176]{1,0:T(8,128)(2,1)S(1)}, bf16[32,2176]{1,0:T(8,128)(2,1)S(1)}, u32[]{:S(2)}, u32[]{:S(2)}) collective-permute-start(bf16[32,2176]{1,0:T(8,128)(2,1)S(1)} %get-tuple-element.99.own_ref), channel_id=1, source_target_pairs={{0,12},{1,9},{2,14},{3,11},{4,8},{5,13},{6,10},{7,15},{8,4},{9,1},... | collective-permute-start | bytes 417800 | tf_op jit(solution)/shard_map/ppermute | solution.py:431
  46.5 1.7 %copy-done.5 = bf16[2,768,1024]{2,1,0:T(8,128)(2,1)} copy-done((bf16[2,768,1024]{2,1,0:T(8,128)(2,1)}, bf16[2,768,1024]{2,1,0:T(8,128)(2,1)S(1)}, u32[]{:S(2)}) %copy-start.5) | copy-done | bytes 3145752
  48.1 3.8 %shard_map.139 = (bf16[1024,768]{1,0:T(8,128)(2,1)S(1)}, bf16[1024,768]{1,0:T(8,128)(2,1)S(1)}, bf16[1024,768]{1,0:T(8,128)(2,1)S(1)}, bf16[1024,768]{1,0:T(8,12...) custom-call(bf16[2,1024,768]{2,1,0:T(8,128)(2,1)} %refs_10_, ...), custom_call_target="tpu_custom_call" | custom-call | tf_op jit(solution)/shard_map/pallas_call | solution.py:303
  52.0 1.1 %collective-permute-done.17.refs_2_ = bf16[32,2176]{1,0:T(8,128)(2,1)S(1)} collective-permute-done((bf16[32,2176]{1,0:T(8,128)(2,1)S(1)}, bf16[32,2176]{1,0:T(8,128)(2,1)S(1)}, u32[]{:S(2)}, u32[]{:S(2)}) %collective-permute-start.17) | collective-permute-done | bytes 139296 | tf_op jit(solution)/shard_map/ppermute | solution.py:431
  53.1 1.7 %collective-permute-done.18.refs_3_ = bf16[32,2176]{1,0:T(8,128)(2,1)S(1)} collective-permute-done((bf16[32,2176]{1,0:T(8,128)(2,1)S(1)}, bf16[32,2176]{1,0:T(8,128)(2,1)S(1)}, u32[]{:S(2)}, u32[]{:S(2)}) %collective-permute-start.18) | collective-permute-done | bytes 139296 | tf_op jit(solution)/shard_map/ppermute | solution.py:431
  54.8 5.7 %shard_map.140 = (bf16[32,2048]{1,0:T(8,128)(2,1)S(1)}, bf16[32,2048]{1,0:T(8,128)(2,1)S(1)}, bf16[32,2048]{1,0:T(8,128)(2,1)S(1)}, bf16[32,2048]{1,0:T(8,128)(2,1)S(1)}) custom-call(s32[1]{0:T(128)} %bitcast.1.me_ref, s32[1]{0:T(128)} %bitcast.core_ref, bf16[32,2176]{1,0:T(8,128)(2,1)S(1)} %get-tuple-element.99.own_ref, ...), custom_call_target="tpu_custom_call" | custom-call | tf_op jit(solution)/shard_map/pallas_call | solution.py:375
  60.5 2.6 %collective-permute-start.22 = (bf16[32,2048]{1,0:T(8,128)(2,1)S(1)}, bf16[32,2048]{1,0:T(8,128)(2,1)S(1)}, u32[]{:S(2)}, u32[]{:S(2)}) collective-permute-start(bf16[32,2048]{1,0:T(8,128)(2,1)S(1)} %get-tuple-element.113), channel_id=1, source_target_pairs={{0,10},{1,15},{2,8},{3,13},{4,14},{5,11},{6,12},{7,9},{8,2},{9,7},... | collective-permute-start | bytes 393224 | tf_op jit(solution)/shard_map/ppermute | solution.py:431
  63.1 2.4 %collective-permute-start.21 = (bf16[32,2048]{1,0:T(8,128)(2,1)S(1)}, bf16[32,2048]{1,0:T(8,128)(2,1)S(1)}, u32[]{:S(2)}, u32[]{:S(2)}) collective-permute-start(bf16[32,2048]{1,0:T(8,128)(2,1)S(1)} %get-tuple-element.112), channel_id=1, source_target_pairs={{0,12},{1,9},{2,14},{3,11},{4,8},{5,13},{6,10},{7,15},{8,4},{9,1},... | collective-permute-start | bytes 393224 | tf_op jit(solution)/shard_map/ppermute | solution.py:431
  65.5 0.7 collective-permute-start.23
  66.2 8.1 %collective-permute-done.22 = bf16[32,2048]{1,0:T(8,128)(2,1)S(1)} collective-permute-done((bf16[32,2048]{1,0:T(8,128)(2,1)S(1)}, bf16[32,2048]{1,0:T(8,128)(2,1)S(1)}, u32[]{:S(2)}, u32[]{:S(2)}) %collective-permute-start.22) | collective-permute-done | bytes 131104 | tf_op jit(solution)/shard_map/ppermute | solution.py:431
  74.3 1.1 %collective-permute-done.20 = bf16[32,2048]{1,0:T(8,128)(2,1)S(1)} collective-permute-done((bf16[32,2048]{1,0:T(8,128)(2,1)S(1)}, bf16[32,2048]{1,0:T(8,128)(2,1)S(1)}, u32[]{:S(2)}, u32[]{:S(2)}) %collective-permute-start.20) | collective-permute-done | bytes 131104 | tf_op jit(solution)/shard_map/ppermute | solution.py:431
  75.4 0.1 convert_add_fusion
  75.5 0.1 collective-permute-start.24
  75.6 1.3 %collective-permute-done.24 = f32[32,1024]{1,0:T(8,128)S(1)} collective-permute-done((f32[32,1024]{1,0:T(8,128)S(1)}, f32[32,1024]{1,0:T(8,128)S(1)}, u32[]{:S(2)}, u32[]{:S(2)}) %collective-permute-start.24) | collective-permute-done | bytes 131104 | tf_op jit(solution)/shard_map/ppermute | solution.py:419
  77.0 0.7 fusion.1
  (30 shorter events, 0.1 us)
Async XLA Ops:
  0.0 7.5 %collective-permute-start = (bf16[2,1024,768]{2,1,0:T(8,128)(2,1)}, bf16[2,1024,768]{2,1,0:T(8,128)(2,1)}, u32[]{:S(2)}, u32[]{:S(2)}) collective-permute-start(bf16[2,1024,768]{2,1,0:T(8,128)(2,1)} %refs_10_), channel_id=1, source_target_pairs={{0,1},{1,0},{2,3},{3,2},{4,5},{5,4},{6,7},{7,6},{8,9},{9,8},{10,11... | collective-permute-start | bytes 9437192 | tf_op jit(solution)/shard_map/ppermute | solution.py:419
  0.5 7.0 %collective-permute-start.1 = (bf16[32,1024]{1,0:T(8,128)(2,1)}, bf16[32,1024]{1,0:T(8,128)(2,1)S(1)}, u32[]{:S(2)}, u32[]{:S(2)}) collective-permute-start(bf16[32,1024]{1,0:T(8,128)(2,1)} %refs_2_), channel_id=1, source_target_pairs={{0,1},{1,0},{2,3},{3,2},{4,5},{5,4},{6,7},{7,6},{8,9},{9,8},{10,11... | collective-permute-start | bytes 196616 | tf_op jit(solution)/shard_map/ppermute | solution.py:419
  0.5 6.9 %collective-permute-start.2 = (f32[1,1024]{1,0:T(1,128)}, f32[1,1024]{1,0:T(1,128)S(1)}, u32[]{:S(2)}, u32[]{:S(2)}) collective-permute-start(f32[1,1024]{1,0:T(1,128)} %bitcast.23), channel_id=1, source_target_pairs={{0,1},{1,0},{2,3},{3,2},{4,5},{5,4},{6,7},{7,6},{8,9},{9,8},{10,11... | collective-permute-start | bytes 12296 | tf_op jit(solution)/shard_map/ppermute | solution.py:419
  1.0 8.2 %copy-start = (bf16[1024,1024]{1,0:T(8,128)(2,1)S(1)}, bf16[1024,1024]{1,0:T(8,128)(2,1)}, u32[]{:S(2)}) copy-start(bf16[1024,1024]{1,0:T(8,128)(2,1)} %refs_4_) | copy-start | bytes 6291460
  7.5 1.6 %collective-permute-start.3 = (bf16[4,16,1024]{2,1,0:T(8,128)(2,1)}, bf16[4,16,1024]{2,1,0:T(8,128)(2,1)S(1)}, u32[]{:S(2)}, u32[]{:S(2)}) collective-permute-start(bf16[4,16,1024]{2,1,0:T(8,128)(2,1)} %get-tuple-element.64), channel_id=1, source_target_pairs={{0,1},{1,0},{2,3},{3,2},{4,5},{5,4},{6,7},{7,6},{8,9},{9,8},{10,11... | collective-permute-start | bytes 393224 | tf_op jit(solution)/shard_map/ppermute | solution.py:419
  8.5 31.5 %copy-start.1 = (bf16[32,1024]{1,0:T(8,128)(2,1)S(1)}, bf16[32,1024]{1,0:T(8,128)(2,1)}, u32[]{:S(2)}) copy-start(bf16[32,1024]{1,0:T(8,128)(2,1)} %refs_2_) | copy-start | bytes 196612
  8.5 31.5 %copy-start.2 = (f32[1024]{0:T(1024)S(1)}, f32[1024]{0:T(1024)}, u32[]{:S(2)}) copy-start(f32[1024]{0:T(1024)} %param.22) | copy-start | bytes 12292
  8.5 31.5 %copy-start.3 = (s32[32,8]{0,1:T(8,128)S(1)}, s32[32,8]{0,1:T(8,128)}, u32[]{:S(2)}) copy-start(s32[32,8]{0,1:T(8,128)} %param.23) | copy-start | bytes 3076
  8.6 31.5 %copy-start.4 = (f32[32,8]{0,1:T(8,128)S(1)}, f32[32,8]{0,1:T(8,128)}, u32[]{:S(2)}) copy-start(f32[32,8]{0,1:T(8,128)} %param.24) | copy-start | bytes 3076
  9.2 14.1 %collective-permute-start.8 = (bf16[1024,1024]{1,0:T(8,128)(2,1)S(1)}, bf16[1024,1024]{1,0:T(8,128)(2,1)S(1)}, u32[]{:S(2)}, u32[]{:S(2)}) collective-permute-start(bf16[1024,1024]{1,0:T(8,128)(2,1)S(1)} %copy-done), channel_id=1, source_target_pairs={{0,1},{1,0},{2,3},{3,2},{4,5},{5,4},{6,7},{7,6},{8,9},{9,8},{10,11... | collective-permute-start | bytes 6291464 | tf_op jit(solution)/shard_map/ppermute | solution.py:419
  9.4 8.7 %collective-permute-start.4 = (bf16[32,1024]{1,0:T(8,128)(2,1)S(1)}, bf16[32,1024]{1,0:T(8,128)(2,1)S(1)}, u32[]{:S(2)}, u32[]{:S(2)}) collective-permute-start(bf16[32,1024]{1,0:T(8,128)(2,1)S(1)} %get-tuple-element.69), channel_id=1, source_target_pairs={{0,10},{1,15},{2,8},{3,13},{4,14},{5,11},{6,12},{7,9},{8,2},{9,7},... | collective-permute-start | bytes 196616 | tf_op jit(solution)/shard_map/ppermute | solution.py:431
  14.1 3.9 %collective-permute-start.5 = (bf16[32,1024]{1,0:T(8,128)(2,1)S(1)}, bf16[32,1024]{1,0:T(8,128)(2,1)S(1)}, u32[]{:S(2)}, u32[]{:S(2)}) collective-permute-start(bf16[32,1024]{1,0:T(8,128)(2,1)S(1)} %get-tuple-element.68.own_ref), channel_id=1, source_target_pairs={{1,3},{3,1},{5,7},{7,5},{9,11},{11,9},{13,15},{15,13},{17,19},{19,... | collective-permute-start | bytes 196616 | tf_op jit(solution)/shard_map/ppermute | solution.py:431
  14.8 5.3 %collective-permute-start.6 = (bf16[32,1024]{1,0:T(8,128)(2,1)S(1)}, bf16[32,1024]{1,0:T(8,128)(2,1)S(1)}, u32[]{:S(2)}, u32[]{:S(2)}) collective-permute-start(bf16[32,1024]{1,0:T(8,128)(2,1)S(1)} %get-tuple-element.70), channel_id=1, source_target_pairs={{0,6},{1,5},{2,4},{3,7},{4,2},{5,1},{6,0},{7,3},{8,14},{9,13},{10,... | collective-permute-start | bytes 196616 | tf_op jit(solution)/shard_map/ppermute | solution.py:431
  16.6 6.6 %collective-permute-start.7 = (bf16[32,1024]{1,0:T(8,128)(2,1)S(1)}, bf16[32,1024]{1,0:T(8,128)(2,1)S(1)}, u32[]{:S(2)}, u32[]{:S(2)}) collective-permute-start(bf16[32,1024]{1,0:T(8,128)(2,1)S(1)} %get-tuple-element.71), channel_id=1, source_target_pairs={{0,12},{1,9},{2,14},{3,11},{4,8},{5,13},{6,10},{7,15},{8,4},{9,1},... | collective-permute-start | bytes 196616 | tf_op jit(solution)/shard_map/ppermute | solution.py:431
  23.2 15.2 %collective-permute-start.13 = (bf16[2,1024,768]{2,1,0:T(8,128)(2,1)}, bf16[2,1024,768]{2,1,0:T(8,128)(2,1)}, u32[]{:S(2)}, u32[]{:S(2)}) collective-permute-start(bf16[2,1024,768]{2,1,0:T(8,128)(2,1)} %refs_12_), channel_id=1, source_target_pairs={{0,1},{1,0},{2,3},{3,2},{4,5},{5,4},{6,7},{7,6},{8,9},{9,8},{10,11... | collective-permute-start | bytes 9437192 | tf_op jit(solution)/shard_map/ppermute | solution.py:419
  24.0 13.8 %collective-permute-start.11 = (bf16[32,2048]{1,0:T(8,128)(2,1)S(1)}, bf16[32,2048]{1,0:T(8,128)(2,1)S(1)}, u32[]{:S(2)}, u32[]{:S(2)}) collective-permute-start(bf16[32,2048]{1,0:T(8,128)(2,1)S(1)} %get-tuple-element.83), channel_id=1, source_target_pairs={{0,10},{1,15},{2,8},{3,13},{4,14},{5,11},{6,12},{7,9},{8,2},{9,7},... | collective-permute-start | bytes 393224 | tf_op jit(solution)/shard_map/ppermute | solution.py:431
  25.2 12.5 %collective-permute-start.10 = (bf16[32,2048]{1,0:T(8,128)(2,1)S(1)}, bf16[32,2048]{1,0:T(8,128)(2,1)S(1)}, u32[]{:S(2)}, u32[]{:S(2)}) collective-permute-start(bf16[32,2048]{1,0:T(8,128)(2,1)S(1)} %get-tuple-element.82), channel_id=1, source_target_pairs={{0,12},{1,9},{2,14},{3,11},{4,8},{5,13},{6,10},{7,15},{8,4},{9,1},... | collective-permute-start | bytes 393224 | tf_op jit(solution)/shard_map/ppermute | solution.py:431
  27.6 10.7 %collective-permute-start.9 = (bf16[32,2048]{1,0:T(8,128)(2,1)S(1)}, bf16[32,2048]{1,0:T(8,128)(2,1)S(1)}, u32[]{:S(2)}, u32[]{:S(2)}) collective-permute-start(bf16[32,2048]{1,0:T(8,128)(2,1)S(1)} %get-tuple-element.81), channel_id=1, source_target_pairs={{0,6},{1,5},{2,4},{3,7},{4,2},{5,1},{6,0},{7,3},{8,14},{9,13},{10,... | collective-permute-start | bytes 393224 | tf_op jit(solution)/shard_map/ppermute | solution.py:431
  28.4 9.9 %collective-permute-start.12 = (bf16[32,2048]{1,0:T(8,128)(2,1)S(1)}, bf16[32,2048]{1,0:T(8,128)(2,1)S(1)}, u32[]{:S(2)}, u32[]{:S(2)}) collective-permute-start(bf16[32,2048]{1,0:T(8,128)(2,1)S(1)} %get-tuple-element.84), channel_id=1, source_target_pairs={{1,3},{3,1},{5,7},{7,5},{9,11},{11,9},{13,15},{15,13},{17,19},{19,... | collective-permute-start | bytes 393224 | tf_op jit(solution)/shard_map/ppermute | solution.py:431
  38.4 1.6 %collective-permute-start.14 = (f32[32,2048]{1,0:T(8,128)S(1)}, f32[32,2048]{1,0:T(8,128)S(1)}, u32[]{:S(2)}, u32[]{:S(2)}) collective-permute-start(f32[32,2048]{1,0:T(8,128)S(1)} %convert_add_fusion.1.refs_0_), channel_id=1, source_target_pairs={{0,1},{1,0},{2,3},{3,2},{4,5},{5,4},{6,7},{7,6},{8,9},{9,8},{10,11... | collective-permute-start | bytes 786440 | tf_op jit(solution)/shard_map/ppermute | solution.py:419
  40.2 6.2 %collective-permute-start.19 = (bf16[2,768,1024]{2,1,0:T(8,128)(2,1)}, bf16[2,768,1024]{2,1,0:T(8,128)(2,1)S(1)}, u32[]{:S(2)}, u32[]{:S(2)}) collective-permute-start(bf16[2,768,1024]{2,1,0:T(8,128)(2,1)} %refs_14_), channel_id=1, source_target_pairs={{0,1},{1,0},{2,3},{3,2},{4,5},{5,4},{6,7},{7,6},{8,9},{9,8},{10,11... | collective-permute-start | bytes 9437192 | tf_op jit(solution)/shard_map/ppermute | solution.py:419
  40.4 11.5 %collective-permute-start.15 = (bf16[32,2176]{1,0:T(8,128)(2,1)S(1)}, bf16[32,2176]{1,0:T(8,128)(2,1)S(1)}, u32[]{:S(2)}, u32[]{:S(2)}) collective-permute-start(bf16[32,2176]{1,0:T(8,128)(2,1)S(1)} %get-tuple-element.99.own_ref), channel_id=1, source_target_pairs={{0,10},{1,15},{2,8},{3,13},{4,14},{5,11},{6,12},{7,9},{8,2},{9,7},... | collective-permute-start | bytes 417800 | tf_op jit(solution)/shard_map/ppermute | solution.py:431
  41.8 10.1 %collective-permute-start.16 = (bf16[32,2176]{1,0:T(8,128)(2,1)S(1)}, bf16[32,2176]{1,0:T(8,128)(2,1)S(1)}, u32[]{:S(2)}, u32[]{:S(2)}) collective-permute-start(bf16[32,2176]{1,0:T(8,128)(2,1)S(1)} %get-tuple-element.99.own_ref), channel_id=1, source_target_pairs={{1,3},{3,1},{5,7},{7,5},{9,11},{11,9},{13,15},{15,13},{17,19},{19,... | collective-permute-start | bytes 417800 | tf_op jit(solution)/shard_map/ppermute | solution.py:431
  42.5 10.6 %collective-permute-start.17 = (bf16[32,2176]{1,0:T(8,128)(2,1)S(1)}, bf16[32,2176]{1,0:T(8,128)(2,1)S(1)}, u32[]{:S(2)}, u32[]{:S(2)}) collective-permute-start(bf16[32,2176]{1,0:T(8,128)(2,1)S(1)} %get-tuple-element.99.own_ref), channel_id=1, source_target_pairs={{0,6},{1,5},{2,4},{3,7},{4,2},{5,1},{6,0},{7,3},{8,14},{9,13},{10,... | collective-permute-start | bytes 417800 | tf_op jit(solution)/shard_map/ppermute | solution.py:431
  44.1 10.7 %collective-permute-start.18 = (bf16[32,2176]{1,0:T(8,128)(2,1)S(1)}, bf16[32,2176]{1,0:T(8,128)(2,1)S(1)}, u32[]{:S(2)}, u32[]{:S(2)}) collective-permute-start(bf16[32,2176]{1,0:T(8,128)(2,1)S(1)} %get-tuple-element.99.own_ref), channel_id=1, source_target_pairs={{0,12},{1,9},{2,14},{3,11},{4,8},{5,13},{6,10},{7,15},{8,4},{9,1},... | collective-permute-start | bytes 417800 | tf_op jit(solution)/shard_map/ppermute | solution.py:431
  46.5 1.7 %copy-start.5 = (bf16[2,768,1024]{2,1,0:T(8,128)(2,1)}, bf16[2,768,1024]{2,1,0:T(8,128)(2,1)S(1)}, u32[]{:S(2)}) copy-start(bf16[2,768,1024]{2,1,0:T(8,128)(2,1)S(1)} %collective-permute-done.19.refs_5_.refs_15_) | copy-start | bytes 9437188
  60.5 13.8 %collective-permute-start.22 = (bf16[32,2048]{1,0:T(8,128)(2,1)S(1)}, bf16[32,2048]{1,0:T(8,128)(2,1)S(1)}, u32[]{:S(2)}, u32[]{:S(2)}) collective-permute-start(bf16[32,2048]{1,0:T(8,128)(2,1)S(1)} %get-tuple-element.113), channel_id=1, source_target_pairs={{0,10},{1,15},{2,8},{3,13},{4,14},{5,11},{6,12},{7,9},{8,2},{9,7},... | collective-permute-start | bytes 393224 | tf_op jit(solution)/shard_map/ppermute | solution.py:431
  63.1 11.2 %collective-permute-start.21 = (bf16[32,2048]{1,0:T(8,128)(2,1)S(1)}, bf16[32,2048]{1,0:T(8,128)(2,1)S(1)}, u32[]{:S(2)}, u32[]{:S(2)}) collective-permute-start(bf16[32,2048]{1,0:T(8,128)(2,1)S(1)} %get-tuple-element.112), channel_id=1, source_target_pairs={{0,12},{1,9},{2,14},{3,11},{4,8},{5,13},{6,10},{7,15},{8,4},{9,1},... | collective-permute-start | bytes 393224 | tf_op jit(solution)/shard_map/ppermute | solution.py:431
  65.5 9.9 %collective-permute-start.20 = (bf16[32,2048]{1,0:T(8,128)(2,1)S(1)}, bf16[32,2048]{1,0:T(8,128)(2,1)S(1)}, u32[]{:S(2)}, u32[]{:S(2)}) collective-permute-start(bf16[32,2048]{1,0:T(8,128)(2,1)S(1)} %get-tuple-element.111), channel_id=1, source_target_pairs={{0,6},{1,5},{2,4},{3,7},{4,2},{5,1},{6,0},{7,3},{8,14},{9,13},{10,... | collective-permute-start | bytes 393224 | tf_op jit(solution)/shard_map/ppermute | solution.py:431
  65.5 9.9 %collective-permute-start.23 = (bf16[32,2048]{1,0:T(8,128)(2,1)S(1)}, bf16[32,2048]{1,0:T(8,128)(2,1)S(1)}, u32[]{:S(2)}, u32[]{:S(2)}) collective-permute-start(bf16[32,2048]{1,0:T(8,128)(2,1)S(1)} %get-tuple-element.114), channel_id=1, source_target_pairs={{1,3},{3,1},{5,7},{7,5},{9,11},{11,9},{13,15},{15,13},{17,19},{19,... | collective-permute-start | bytes 393224 | tf_op jit(solution)/shard_map/ppermute | solution.py:431
  75.5 1.4 %collective-permute-start.24 = (f32[32,1024]{1,0:T(8,128)S(1)}, f32[32,1024]{1,0:T(8,128)S(1)}, u32[]{:S(2)}, u32[]{:S(2)}) collective-permute-start(f32[32,1024]{1,0:T(8,128)S(1)} %slice.61), channel_id=1, source_target_pairs={{0,1},{1,0},{2,3},{3,2},{4,5},{5,4},{6,7},{7,6},{8,9},{9,8},{10,11... | collective-permute-start | bytes 393224 | tf_op jit(solution)/shard_map/ppermute | solution.py:419

commit v6 on v5

--- a/solution.py
+++ b/solution.py
@@ -14,7 +14,7 @@
 SMEM = pl.BlockSpec(memory_space=pltpu.SMEM)
 ANY = pl.BlockSpec(memory_space=pl.ANY)
 MIB = 1024 * 1024
-TUNED = {(8, 2): ((5, 0, 3, 6), (7, 1, 2, 4))}
+TUNED = {(8, 2): ((5, 0, 3, 6), (7, 1, 4, 2))}
 
 
 def choose(core, values):

time: 77.5 us -> 76.1 us (0.982); the launches traced: 77.7 us -> 75.4 us
  waiting for transfers between devices: 31.2 us -> 28.9 us
    ppermute x16, waiting for transfers between devices: 27.8 us -> 25.7 us  [swap(): return lax.ppermute(value, ('dev', 'pair'), pairs)]
  transfers between devices with their start and end apart: 25 -> 25, of which waited for: 12 -> 12; matrix products, arithmetic and copies ran while one was open for 1% -> 1% of each run, Pallas kernels for 14% -> 15%
where the time goes in v6:
time: 76.1 us; the launch traced here: 75.4 us
  waiting for transfers between devices  28.9 us (38%)
  starting transfers between devices  25.8 us (34%)
  Pallas kernels  17 us (22%)
  local copies, waits for them, and re-layouts  2.58 us (3%)
  other arithmetic  0.86 us (1%)
    ppermute x16, waiting for transfers between devices, swap(): return lax.ppermute(value, ('dev', 'pair'), pairs)  25.7 us
    ppermute x16, starting transfers between devices, swap(): return lax.ppermute(value, ('dev', 'pair'), pairs)  23.9 us
    pallas_call x1, Pallas kernels, attend(): pl.pallas_call(functools.partial(attend_kernel, kv_heads, offset), out_sh...  6.6 us
    pallas_call x1, Pallas kernels, apply_experts(): pl.pallas_call(functools.partial(expert_kernel, offset, devs), out_shape=...  5.7 us
    pallas_call x1, Pallas kernels, fetch(): pl.pallas_call(functools.partial(fetch_kernel, count), out_shape=[jax.Sha...  3.79 us
    ppermute x9, waiting for transfers between devices, from_core(): return lax.ppermute(value, 'pair', [(c, c ^ m) for c in range(cores)])  3.2 us
    ppermute x9, starting transfers between devices, from_core(): return lax.ppermute(value, 'pair', [(c, c ^ m) for c in range(cores)])  1.99 us
    unnamed x12, local copies, waits for them, and re-layouts  1.72 us
  transfers between devices with their start and end apart: 25, of which 12 were waited for; matrix products, arithmetic and copies ran while one was open for 1% of the time, Pallas kernels for 15%

profile of v6, /device:TPU:0, one launch (start us, length us, event | category | flops | bytes accessed | tf_op | source)
XLA Modules:
  0.0 75.4 jit_solution(9832923284541958837)
XLA Ops:
  0.0 0.5 collective-permute-start
  0.5 0.1 collective-permute-start.1
  0.5 0.5 collective-permute-start.2
  1.0 6.6 %shard_map.136 = (bf16[4,16,1024]{2,1,0:T(8,128)(2,1)}, bf16[4,16,1024]{2,1,0:T(8,128)(2,1)}) custom-call(s32[16]{0:T(128)} %len_ref.1, s32[1]{0:T(128)} %bitcast.1.me_ref, s32[1]{0:T(128)} %bitcast.core_ref, bf16[16,64,128]{2,1,0:T(8,128)(2,1)} %q_hbm.1, bf16[16,1024,128]{2,1,0:T(8,128)(2,1)} %bitcast.27, bf16[16,1024,128]{2,1,0:T(8,128)(2,1)} %bitcast.28, ...), custom_call_target="tpu_custom_call" | custom-call | tf_op jit(solution)/shard_map/pallas_call | solution.py:172
  7.6 0.1 collective-permute-start.3
  7.7 0.8 %slice_bitcast_fusion.4 = (bf16[16,1024]{1,0:T(8,128)(2,1)S(1)}, bf16[16,1024]{1,0:T(8,128)(2,1)S(1)}, bf16[16,1024]{1,0:T(8,128)(2,1)S(1)}, bf16[16,1024]{1,0:T(8,128)(2,1)S(1)}) fusion(bf16[4,16,1024]{2,1,0:T(8,128)(2,1)} %get-tuple-element.62), kind=kLoop, calls=%fused_computation.14 | loop fusion | bytes 262144 | tf_op jit(solution)/shard_map/squeeze | solution.py:454
  8.5 0.0 copy-start.1
  8.5 0.0 copy-start.2
  8.5 0.0 copy-start.3
  8.5 0.0 copy-start.4
  8.6 0.7 collective-permute-done.3
  9.3 0.2 collective-permute-start.8
  9.5 4.7 %collective-permute-start.4 = (bf16[32,1024]{1,0:T(8,128)(2,1)S(1)}, bf16[32,1024]{1,0:T(8,128)(2,1)S(1)}, u32[]{:S(2)}, u32[]{:S(2)}) collective-permute-start(bf16[32,1024]{1,0:T(8,128)(2,1)S(1)} %get-tuple-element.69), channel_id=1, source_target_pairs={{0,10},{1,15},{2,8},{3,13},{4,14},{5,11},{6,12},{7,9},{8,2},{9,7},... | collective-permute-start | bytes 196616 | tf_op jit(solution)/shard_map/ppermute | solution.py:431
  14.2 0.7 collective-permute-start.5
  14.9 1.9 %collective-permute-start.6 = (bf16[32,1024]{1,0:T(8,128)(2,1)S(1)}, bf16[32,1024]{1,0:T(8,128)(2,1)S(1)}, u32[]{:S(2)}, u32[]{:S(2)}) collective-permute-start(bf16[32,1024]{1,0:T(8,128)(2,1)S(1)} %get-tuple-element.70), channel_id=1, source_target_pairs={{0,6},{1,9},{2,4},{3,11},{4,2},{5,13},{6,0},{7,15},{8,14},{9,1},{1... | collective-permute-start | bytes 196616 | tf_op jit(solution)/shard_map/ppermute | solution.py:431
  16.8 1.3 %collective-permute-done.4.refs_0_ = bf16[32,1024]{1,0:T(8,128)(2,1)S(1)} collective-permute-done((bf16[32,1024]{1,0:T(8,128)(2,1)S(1)}, bf16[32,1024]{1,0:T(8,128)(2,1)S(1)}, u32[]{:S(2)}, u32[]{:S(2)}) %collective-permute-start.4) | collective-permute-done | bytes 65568 | tf_op jit(solution)/shard_map/ppermute | solution.py:431
  18.1 2.1 %collective-permute-done.6.refs_2_ = bf16[32,1024]{1,0:T(8,128)(2,1)S(1)} collective-permute-done((bf16[32,1024]{1,0:T(8,128)(2,1)S(1)}, bf16[32,1024]{1,0:T(8,128)(2,1)S(1)}, u32[]{:S(2)}, u32[]{:S(2)}) %collective-permute-start.6) | collective-permute-done | bytes 65568 | tf_op jit(solution)/shard_map/ppermute | solution.py:431
  20.1 3.2 %collective-permute-done.7.refs_3_ = bf16[32,1024]{1,0:T(8,128)(2,1)S(1)} collective-permute-done((bf16[32,1024]{1,0:T(8,128)(2,1)S(1)}, bf16[32,1024]{1,0:T(8,128)(2,1)S(1)}, u32[]{:S(2)}, u32[]{:S(2)}) %collective-permute-start.7) | collective-permute-done | bytes 65568 | tf_op jit(solution)/shard_map/ppermute | solution.py:431
  23.4 0.7 shard_map.137
  24.1 1.2 %collective-permute-start.11 = (bf16[32,2048]{1,0:T(8,128)(2,1)S(1)}, bf16[32,2048]{1,0:T(8,128)(2,1)S(1)}, u32[]{:S(2)}, u32[]{:S(2)}) collective-permute-start(bf16[32,2048]{1,0:T(8,128)(2,1)S(1)} %get-tuple-element.83), channel_id=1, source_target_pairs={{0,10},{1,15},{2,8},{3,13},{4,14},{5,11},{6,12},{7,9},{8,2},{9,7},... | collective-permute-start | bytes 393224 | tf_op jit(solution)/shard_map/ppermute | solution.py:431
  25.3 1.4 %collective-permute-start.10 = (bf16[32,2048]{1,0:T(8,128)(2,1)S(1)}, bf16[32,2048]{1,0:T(8,128)(2,1)S(1)}, u32[]{:S(2)}, u32[]{:S(2)}) collective-permute-start(bf16[32,2048]{1,0:T(8,128)(2,1)S(1)} %get-tuple-element.82), channel_id=1, source_target_pairs={{0,12},{1,5},{2,14},{3,7},{4,8},{5,1},{6,10},{7,3},{8,4},{9,13},{1... | collective-permute-start | bytes 393224 | tf_op jit(solution)/shard_map/ppermute | solution.py:431
  26.7 1.9 %collective-permute-start.9 = (bf16[32,2048]{1,0:T(8,128)(2,1)S(1)}, bf16[32,2048]{1,0:T(8,128)(2,1)S(1)}, u32[]{:S(2)}, u32[]{:S(2)}) collective-permute-start(bf16[32,2048]{1,0:T(8,128)(2,1)S(1)} %get-tuple-element.81), channel_id=1, source_target_pairs={{0,6},{1,9},{2,4},{3,11},{4,2},{5,13},{6,0},{7,15},{8,14},{9,1},{1... | collective-permute-start | bytes 393224 | tf_op jit(solution)/shard_map/ppermute | solution.py:431
  28.6 0.7 collective-permute-start.12
  29.2 7.2 %collective-permute-done.11 = bf16[32,2048]{1,0:T(8,128)(2,1)S(1)} collective-permute-done((bf16[32,2048]{1,0:T(8,128)(2,1)S(1)}, bf16[32,2048]{1,0:T(8,128)(2,1)S(1)}, u32[]{:S(2)}, u32[]{:S(2)}) %collective-permute-start.11) | collective-permute-done | bytes 131104 | tf_op jit(solution)/shard_map/ppermute | solution.py:431
  36.5 1.3 %collective-permute-done.9 = bf16[32,2048]{1,0:T(8,128)(2,1)S(1)} collective-permute-done((bf16[32,2048]{1,0:T(8,128)(2,1)S(1)}, bf16[32,2048]{1,0:T(8,128)(2,1)S(1)}, u32[]{:S(2)}, u32[]{:S(2)}) %collective-permute-start.9) | collective-permute-done | bytes 131104 | tf_op jit(solution)/shard_map/ppermute | solution.py:431
  37.7 0.1 convert_add_fusion.1.refs_0_
  37.8 0.1 collective-permute-start.14
  37.9 1.5 %collective-permute-done.14.refs_1_ = f32[32,2048]{1,0:T(8,128)S(1)} collective-permute-done((f32[32,2048]{1,0:T(8,128)S(1)}, f32[32,2048]{1,0:T(8,128)S(1)}, u32[]{:S(2)}, u32[]{:S(2)}) %collective-permute-start.14) | collective-permute-done | bytes 262176 | tf_op jit(solution)/shard_map/ppermute | solution.py:419
  39.4 0.2 shard_map.138
  39.6 0.2 collective-permute-start.19
  39.8 2.2 %collective-permute-start.15 = (bf16[32,2176]{1,0:T(8,128)(2,1)S(1)}, bf16[32,2176]{1,0:T(8,128)(2,1)S(1)}, u32[]{:S(2)}, u32[]{:S(2)}) collective-permute-start(bf16[32,2176]{1,0:T(8,128)(2,1)S(1)} %get-tuple-element.99.own_ref), channel_id=1, source_target_pairs={{0,10},{1,15},{2,8},{3,13},{4,14},{5,11},{6,12},{7,9},{8,2},{9,7},... | collective-permute-start | bytes 417800 | tf_op jit(solution)/shard_map/ppermute | solution.py:431
  42.0 0.7 collective-permute-start.16
  42.7 1.5 %collective-permute-start.17 = (bf16[32,2176]{1,0:T(8,128)(2,1)S(1)}, bf16[32,2176]{1,0:T(8,128)(2,1)S(1)}, u32[]{:S(2)}, u32[]{:S(2)}) collective-permute-start(bf16[32,2176]{1,0:T(8,128)(2,1)S(1)} %get-tuple-element.99.own_ref), channel_id=1, source_target_pairs={{0,6},{1,9},{2,4},{3,11},{4,2},{5,13},{6,0},{7,15},{8,14},{9,1},{1... | collective-permute-start | bytes 417800 | tf_op jit(solution)/shard_map/ppermute | solution.py:431
  44.1 1.7 %collective-permute-start.18 = (bf16[32,2176]{1,0:T(8,128)(2,1)S(1)}, bf16[32,2176]{1,0:T(8,128)(2,1)S(1)}, u32[]{:S(2)}, u32[]{:S(2)}) collective-permute-start(bf16[32,2176]{1,0:T(8,128)(2,1)S(1)} %get-tuple-element.99.own_ref), channel_id=1, source_target_pairs={{0,12},{1,5},{2,14},{3,7},{4,8},{5,1},{6,10},{7,3},{8,4},{9,13},{1... | collective-permute-start | bytes 417800 | tf_op jit(solution)/shard_map/ppermute | solution.py:431
  45.8 1.7 %copy-done.5 = bf16[2,768,1024]{2,1,0:T(8,128)(2,1)} copy-done((bf16[2,768,1024]{2,1,0:T(8,128)(2,1)}, bf16[2,768,1024]{2,1,0:T(8,128)(2,1)S(1)}, u32[]{:S(2)}) %copy-start.5) | copy-done | bytes 3145752
  47.5 3.8 %shard_map.139 = (bf16[1024,768]{1,0:T(8,128)(2,1)S(1)}, bf16[1024,768]{1,0:T(8,128)(2,1)S(1)}, bf16[1024,768]{1,0:T(8,128)(2,1)S(1)}, bf16[1024,768]{1,0:T(8,12...) custom-call(bf16[2,1024,768]{2,1,0:T(8,128)(2,1)} %refs_10_, ...), custom_call_target="tpu_custom_call" | custom-call | tf_op jit(solution)/shard_map/pallas_call | solution.py:303
  51.3 2.4 %collective-permute-done.15.refs_0_ = bf16[32,2176]{1,0:T(8,128)(2,1)S(1)} collective-permute-done((bf16[32,2176]{1,0:T(8,128)(2,1)S(1)}, bf16[32,2176]{1,0:T(8,128)(2,1)S(1)}, u32[]{:S(2)}, u32[]{:S(2)}) %collective-permute-start.15) | collective-permute-done | bytes 139296 | tf_op jit(solution)/shard_map/ppermute | solution.py:431
  53.7 0.4 collective-permute-done.17.refs_2_
  54.1 5.7 %shard_map.140 = (bf16[32,2048]{1,0:T(8,128)(2,1)S(1)}, bf16[32,2048]{1,0:T(8,128)(2,1)S(1)}, bf16[32,2048]{1,0:T(8,128)(2,1)S(1)}, bf16[32,2048]{1,0:T(8,128)(2,1)S(1)}) custom-call(s32[1]{0:T(128)} %bitcast.1.me_ref, s32[1]{0:T(128)} %bitcast.core_ref, bf16[32,2176]{1,0:T(8,128)(2,1)S(1)} %get-tuple-element.99.own_ref, ...), custom_call_target="tpu_custom_call" | custom-call | tf_op jit(solution)/shard_map/pallas_call | solution.py:375
  59.8 3.4 %collective-permute-start.22 = (bf16[32,2048]{1,0:T(8,128)(2,1)S(1)}, bf16[32,2048]{1,0:T(8,128)(2,1)S(1)}, u32[]{:S(2)}, u32[]{:S(2)}) collective-permute-start(bf16[32,2048]{1,0:T(8,128)(2,1)S(1)} %get-tuple-element.113), channel_id=1, source_target_pairs={{0,10},{1,15},{2,8},{3,13},{4,14},{5,11},{6,12},{7,9},{8,2},{9,7},... | collective-permute-start | bytes 393224 | tf_op jit(solution)/shard_map/ppermute | solution.py:431
  63.2 1.5 %collective-permute-start.21 = (bf16[32,2048]{1,0:T(8,128)(2,1)S(1)}, bf16[32,2048]{1,0:T(8,128)(2,1)S(1)}, u32[]{:S(2)}, u32[]{:S(2)}) collective-permute-start(bf16[32,2048]{1,0:T(8,128)(2,1)S(1)} %get-tuple-element.112), channel_id=1, source_target_pairs={{0,12},{1,5},{2,14},{3,7},{4,8},{5,1},{6,10},{7,3},{8,4},{9,13},{1... | collective-permute-start | bytes 393224 | tf_op jit(solution)/shard_map/ppermute | solution.py:431
  64.7 0.7 collective-permute-start.23
  65.3 7.6 %collective-permute-done.22 = bf16[32,2048]{1,0:T(8,128)(2,1)S(1)} collective-permute-done((bf16[32,2048]{1,0:T(8,128)(2,1)S(1)}, bf16[32,2048]{1,0:T(8,128)(2,1)S(1)}, u32[]{:S(2)}, u32[]{:S(2)}) %collective-permute-start.22) | collective-permute-done | bytes 131104 | tf_op jit(solution)/shard_map/ppermute | solution.py:431
  72.9 0.2 collective-permute-done.20
  73.1 0.1 convert_add_fusion
  73.2 0.5 collective-permute-start.24
  73.7 1.0 %collective-permute-done.24 = f32[32,1024]{1,0:T(8,128)S(1)} collective-permute-done((f32[32,1024]{1,0:T(8,128)S(1)}, f32[32,1024]{1,0:T(8,128)S(1)}, u32[]{:S(2)}, u32[]{:S(2)}) %collective-permute-start.24) | collective-permute-done | bytes 131104 | tf_op jit(solution)/shard_map/ppermute | solution.py:419
  74.8 0.7 fusion.1
  (30 shorter events, 0.1 us)
Async XLA Ops:
  0.0 7.6 %collective-permute-start = (bf16[2,1024,768]{2,1,0:T(8,128)(2,1)}, bf16[2,1024,768]{2,1,0:T(8,128)(2,1)}, u32[]{:S(2)}, u32[]{:S(2)}) collective-permute-start(bf16[2,1024,768]{2,1,0:T(8,128)(2,1)} %refs_10_), channel_id=1, source_target_pairs={{0,1},{1,0},{2,3},{3,2},{4,5},{5,4},{6,7},{7,6},{8,9},{9,8},{10,11... | collective-permute-start | bytes 9437192 | tf_op jit(solution)/shard_map/ppermute | solution.py:419
  0.5 7.1 %collective-permute-start.1 = (bf16[32,1024]{1,0:T(8,128)(2,1)}, bf16[32,1024]{1,0:T(8,128)(2,1)S(1)}, u32[]{:S(2)}, u32[]{:S(2)}) collective-permute-start(bf16[32,1024]{1,0:T(8,128)(2,1)} %refs_2_), channel_id=1, source_target_pairs={{0,1},{1,0},{2,3},{3,2},{4,5},{5,4},{6,7},{7,6},{8,9},{9,8},{10,11... | collective-permute-start | bytes 196616 | tf_op jit(solution)/shard_map/ppermute | solution.py:419
  0.5 7.1 %collective-permute-start.2 = (f32[1,1024]{1,0:T(1,128)}, f32[1,1024]{1,0:T(1,128)S(1)}, u32[]{:S(2)}, u32[]{:S(2)}) collective-permute-start(f32[1,1024]{1,0:T(1,128)} %bitcast.23), channel_id=1, source_target_pairs={{0,1},{1,0},{2,3},{3,2},{4,5},{5,4},{6,7},{7,6},{8,9},{9,8},{10,11... | collective-permute-start | bytes 12296 | tf_op jit(solution)/shard_map/ppermute | solution.py:419
  1.0 8.3 %copy-start = (bf16[1024,1024]{1,0:T(8,128)(2,1)S(1)}, bf16[1024,1024]{1,0:T(8,128)(2,1)}, u32[]{:S(2)}) copy-start(bf16[1024,1024]{1,0:T(8,128)(2,1)} %refs_4_) | copy-start | bytes 6291460
  7.6 1.6 %collective-permute-start.3 = (bf16[4,16,1024]{2,1,0:T(8,128)(2,1)}, bf16[4,16,1024]{2,1,0:T(8,128)(2,1)S(1)}, u32[]{:S(2)}, u32[]{:S(2)}) collective-permute-start(bf16[4,16,1024]{2,1,0:T(8,128)(2,1)} %get-tuple-element.64), channel_id=1, source_target_pairs={{0,1},{1,0},{2,3},{3,2},{4,5},{5,4},{6,7},{7,6},{8,9},{9,8},{10,11... | collective-permute-start | bytes 393224 | tf_op jit(solution)/shard_map/ppermute | solution.py:419
  8.5 30.9 %copy-start.1 = (bf16[32,1024]{1,0:T(8,128)(2,1)S(1)}, bf16[32,1024]{1,0:T(8,128)(2,1)}, u32[]{:S(2)}) copy-start(bf16[32,1024]{1,0:T(8,128)(2,1)} %refs_2_) | copy-start | bytes 196612
  8.5 30.9 %copy-start.2 = (f32[1024]{0:T(1024)S(1)}, f32[1024]{0:T(1024)}, u32[]{:S(2)}) copy-start(f32[1024]{0:T(1024)} %param.22) | copy-start | bytes 12292
  8.5 30.9 %copy-start.3 = (s32[32,8]{0,1:T(8,128)S(1)}, s32[32,8]{0,1:T(8,128)}, u32[]{:S(2)}) copy-start(s32[32,8]{0,1:T(8,128)} %param.23) | copy-start | bytes 3076
  8.5 30.9 %copy-start.4 = (f32[32,8]{0,1:T(8,128)S(1)}, f32[32,8]{0,1:T(8,128)}, u32[]{:S(2)}) copy-start(f32[32,8]{0,1:T(8,128)} %param.24) | copy-start | bytes 3076
  9.3 14.1 %collective-permute-start.8 = (bf16[1024,1024]{1,0:T(8,128)(2,1)S(1)}, bf16[1024,1024]{1,0:T(8,128)(2,1)S(1)}, u32[]{:S(2)}, u32[]{:S(2)}) collective-permute-start(bf16[1024,1024]{1,0:T(8,128)(2,1)S(1)} %copy-done), channel_id=1, source_target_pairs={{0,1},{1,0},{2,3},{3,2},{4,5},{5,4},{6,7},{7,6},{8,9},{9,8},{10,11... | collective-permute-start | bytes 6291464 | tf_op jit(solution)/shard_map/ppermute | solution.py:419
  9.5 8.5 %collective-permute-start.4 = (bf16[32,1024]{1,0:T(8,128)(2,1)S(1)}, bf16[32,1024]{1,0:T(8,128)(2,1)S(1)}, u32[]{:S(2)}, u32[]{:S(2)}) collective-permute-start(bf16[32,1024]{1,0:T(8,128)(2,1)S(1)} %get-tuple-element.69), channel_id=1, source_target_pairs={{0,10},{1,15},{2,8},{3,13},{4,14},{5,11},{6,12},{7,9},{8,2},{9,7},... | collective-permute-start | bytes 196616 | tf_op jit(solution)/shard_map/ppermute | solution.py:431
  14.2 3.8 %collective-permute-start.5 = (bf16[32,1024]{1,0:T(8,128)(2,1)S(1)}, bf16[32,1024]{1,0:T(8,128)(2,1)S(1)}, u32[]{:S(2)}, u32[]{:S(2)}) collective-permute-start(bf16[32,1024]{1,0:T(8,128)(2,1)S(1)} %get-tuple-element.68.own_ref), channel_id=1, source_target_pairs={{1,3},{3,1},{5,7},{7,5},{9,11},{11,9},{13,15},{15,13},{17,19},{19,... | collective-permute-start | bytes 196616 | tf_op jit(solution)/shard_map/ppermute | solution.py:431
  14.9 5.3 %collective-permute-start.6 = (bf16[32,1024]{1,0:T(8,128)(2,1)S(1)}, bf16[32,1024]{1,0:T(8,128)(2,1)S(1)}, u32[]{:S(2)}, u32[]{:S(2)}) collective-permute-start(bf16[32,1024]{1,0:T(8,128)(2,1)S(1)} %get-tuple-element.70), channel_id=1, source_target_pairs={{0,6},{1,9},{2,4},{3,11},{4,2},{5,13},{6,0},{7,15},{8,14},{9,1},{1... | collective-permute-start | bytes 196616 | tf_op jit(solution)/shard_map/ppermute | solution.py:431
  16.8 6.6 %collective-permute-start.7 = (bf16[32,1024]{1,0:T(8,128)(2,1)S(1)}, bf16[32,1024]{1,0:T(8,128)(2,1)S(1)}, u32[]{:S(2)}, u32[]{:S(2)}) collective-permute-start(bf16[32,1024]{1,0:T(8,128)(2,1)S(1)} %get-tuple-element.71), channel_id=1, source_target_pairs={{0,12},{1,5},{2,14},{3,7},{4,8},{5,1},{6,10},{7,3},{8,4},{9,13},{1... | collective-permute-start | bytes 196616 | tf_op jit(solution)/shard_map/ppermute | solution.py:431
  23.4 14.4 %collective-permute-start.13 = (bf16[2,1024,768]{2,1,0:T(8,128)(2,1)}, bf16[2,1024,768]{2,1,0:T(8,128)(2,1)}, u32[]{:S(2)}, u32[]{:S(2)}) collective-permute-start(bf16[2,1024,768]{2,1,0:T(8,128)(2,1)} %refs_12_), channel_id=1, source_target_pairs={{0,1},{1,0},{2,3},{3,2},{4,5},{5,4},{6,7},{7,6},{8,9},{9,8},{10,11... | collective-permute-start | bytes 9437192 | tf_op jit(solution)/shard_map/ppermute | solution.py:419
  24.1 12.3 %collective-permute-start.11 = (bf16[32,2048]{1,0:T(8,128)(2,1)S(1)}, bf16[32,2048]{1,0:T(8,128)(2,1)S(1)}, u32[]{:S(2)}, u32[]{:S(2)}) collective-permute-start(bf16[32,2048]{1,0:T(8,128)(2,1)S(1)} %get-tuple-element.83), channel_id=1, source_target_pairs={{0,10},{1,15},{2,8},{3,13},{4,14},{5,11},{6,12},{7,9},{8,2},{9,7},... | collective-permute-start | bytes 393224 | tf_op jit(solution)/shard_map/ppermute | solution.py:431
  25.3 11.2 %collective-permute-start.10 = (bf16[32,2048]{1,0:T(8,128)(2,1)S(1)}, bf16[32,2048]{1,0:T(8,128)(2,1)S(1)}, u32[]{:S(2)}, u32[]{:S(2)}) collective-permute-start(bf16[32,2048]{1,0:T(8,128)(2,1)S(1)} %get-tuple-element.82), channel_id=1, source_target_pairs={{0,12},{1,5},{2,14},{3,7},{4,8},{5,1},{6,10},{7,3},{8,4},{9,13},{1... | collective-permute-start | bytes 393224 | tf_op jit(solution)/shard_map/ppermute | solution.py:431
  26.7 11.0 %collective-permute-start.9 = (bf16[32,2048]{1,0:T(8,128)(2,1)S(1)}, bf16[32,2048]{1,0:T(8,128)(2,1)S(1)}, u32[]{:S(2)}, u32[]{:S(2)}) collective-permute-start(bf16[32,2048]{1,0:T(8,128)(2,1)S(1)} %get-tuple-element.81), channel_id=1, source_target_pairs={{0,6},{1,9},{2,4},{3,11},{4,2},{5,13},{6,0},{7,15},{8,14},{9,1},{1... | collective-permute-start | bytes 393224 | tf_op jit(solution)/shard_map/ppermute | solution.py:431
  28.6 9.2 %collective-permute-start.12 = (bf16[32,2048]{1,0:T(8,128)(2,1)S(1)}, bf16[32,2048]{1,0:T(8,128)(2,1)S(1)}, u32[]{:S(2)}, u32[]{:S(2)}) collective-permute-start(bf16[32,2048]{1,0:T(8,128)(2,1)S(1)} %get-tuple-element.84), channel_id=1, source_target_pairs={{1,3},{3,1},{5,7},{7,5},{9,11},{11,9},{13,15},{15,13},{17,19},{19,... | collective-permute-start | bytes 393224 | tf_op jit(solution)/shard_map/ppermute | solution.py:431
  37.8 1.6 %collective-permute-start.14 = (f32[32,2048]{1,0:T(8,128)S(1)}, f32[32,2048]{1,0:T(8,128)S(1)}, u32[]{:S(2)}, u32[]{:S(2)}) collective-permute-start(f32[32,2048]{1,0:T(8,128)S(1)} %convert_add_fusion.1.refs_0_), channel_id=1, source_target_pairs={{0,1},{1,0},{2,3},{3,2},{4,5},{5,4},{6,7},{7,6},{8,9},{9,8},{10,11... | collective-permute-start | bytes 786440 | tf_op jit(solution)/shard_map/ppermute | solution.py:419
  39.6 6.2 %collective-permute-start.19 = (bf16[2,768,1024]{2,1,0:T(8,128)(2,1)}, bf16[2,768,1024]{2,1,0:T(8,128)(2,1)S(1)}, u32[]{:S(2)}, u32[]{:S(2)}) collective-permute-start(bf16[2,768,1024]{2,1,0:T(8,128)(2,1)} %refs_14_), channel_id=1, source_target_pairs={{0,1},{1,0},{2,3},{3,2},{4,5},{5,4},{6,7},{7,6},{8,9},{9,8},{10,11... | collective-permute-start | bytes 9437192 | tf_op jit(solution)/shard_map/ppermute | solution.py:419
  39.8 13.9 %collective-permute-start.15 = (bf16[32,2176]{1,0:T(8,128)(2,1)S(1)}, bf16[32,2176]{1,0:T(8,128)(2,1)S(1)}, u32[]{:S(2)}, u32[]{:S(2)}) collective-permute-start(bf16[32,2176]{1,0:T(8,128)(2,1)S(1)} %get-tuple-element.99.own_ref), channel_id=1, source_target_pairs={{0,10},{1,15},{2,8},{3,13},{4,14},{5,11},{6,12},{7,9},{8,2},{9,7},... | collective-permute-start | bytes 417800 | tf_op jit(solution)/shard_map/ppermute | solution.py:431
  42.0 11.7 %collective-permute-start.16 = (bf16[32,2176]{1,0:T(8,128)(2,1)S(1)}, bf16[32,2176]{1,0:T(8,128)(2,1)S(1)}, u32[]{:S(2)}, u32[]{:S(2)}) collective-permute-start(bf16[32,2176]{1,0:T(8,128)(2,1)S(1)} %get-tuple-element.99.own_ref), channel_id=1, source_target_pairs={{1,3},{3,1},{5,7},{7,5},{9,11},{11,9},{13,15},{15,13},{17,19},{19,... | collective-permute-start | bytes 417800 | tf_op jit(solution)/shard_map/ppermute | solution.py:431
  42.7 11.4 %collective-permute-start.17 = (bf16[32,2176]{1,0:T(8,128)(2,1)S(1)}, bf16[32,2176]{1,0:T(8,128)(2,1)S(1)}, u32[]{:S(2)}, u32[]{:S(2)}) collective-permute-start(bf16[32,2176]{1,0:T(8,128)(2,1)S(1)} %get-tuple-element.99.own_ref), channel_id=1, source_target_pairs={{0,6},{1,9},{2,4},{3,11},{4,2},{5,13},{6,0},{7,15},{8,14},{9,1},{1... | collective-permute-start | bytes 417800 | tf_op jit(solution)/shard_map/ppermute | solution.py:431
  44.1 10.0 %collective-permute-start.18 = (bf16[32,2176]{1,0:T(8,128)(2,1)S(1)}, bf16[32,2176]{1,0:T(8,128)(2,1)S(1)}, u32[]{:S(2)}, u32[]{:S(2)}) collective-permute-start(bf16[32,2176]{1,0:T(8,128)(2,1)S(1)} %get-tuple-element.99.own_ref), channel_id=1, source_target_pairs={{0,12},{1,5},{2,14},{3,7},{4,8},{5,1},{6,10},{7,3},{8,4},{9,13},{1... | collective-permute-start | bytes 417800 | tf_op jit(solution)/shard_map/ppermute | solution.py:431
  45.8 1.7 %copy-start.5 = (bf16[2,768,1024]{2,1,0:T(8,128)(2,1)}, bf16[2,768,1024]{2,1,0:T(8,128)(2,1)S(1)}, u32[]{:S(2)}) copy-start(bf16[2,768,1024]{2,1,0:T(8,128)(2,1)S(1)} %collective-permute-done.19.refs_5_.refs_15_) | copy-start | bytes 9437188
  59.8 13.1 %collective-permute-start.22 = (bf16[32,2048]{1,0:T(8,128)(2,1)S(1)}, bf16[32,2048]{1,0:T(8,128)(2,1)S(1)}, u32[]{:S(2)}, u32[]{:S(2)}) collective-permute-start(bf16[32,2048]{1,0:T(8,128)(2,1)S(1)} %get-tuple-element.113), channel_id=1, source_target_pairs={{0,10},{1,15},{2,8},{3,13},{4,14},{5,11},{6,12},{7,9},{8,2},{9,7},... | collective-permute-start | bytes 393224 | tf_op jit(solution)/shard_map/ppermute | solution.py:431
  63.2 9.8 %collective-permute-start.21 = (bf16[32,2048]{1,0:T(8,128)(2,1)S(1)}, bf16[32,2048]{1,0:T(8,128)(2,1)S(1)}, u32[]{:S(2)}, u32[]{:S(2)}) collective-permute-start(bf16[32,2048]{1,0:T(8,128)(2,1)S(1)} %get-tuple-element.112), channel_id=1, source_target_pairs={{0,12},{1,5},{2,14},{3,7},{4,8},{5,1},{6,10},{7,3},{8,4},{9,13},{1... | collective-permute-start | bytes 393224 | tf_op jit(solution)/shard_map/ppermute | solution.py:431
  64.6 8.5 %collective-permute-start.20 = (bf16[32,2048]{1,0:T(8,128)(2,1)S(1)}, bf16[32,2048]{1,0:T(8,128)(2,1)S(1)}, u32[]{:S(2)}, u32[]{:S(2)}) collective-permute-start(bf16[32,2048]{1,0:T(8,128)(2,1)S(1)} %get-tuple-element.111), channel_id=1, source_target_pairs={{0,6},{1,9},{2,4},{3,11},{4,2},{5,13},{6,0},{7,15},{8,14},{9,1},{1... | collective-permute-start | bytes 393224 | tf_op jit(solution)/shard_map/ppermute | solution.py:431
  64.7 8.5 %collective-permute-start.23 = (bf16[32,2048]{1,0:T(8,128)(2,1)S(1)}, bf16[32,2048]{1,0:T(8,128)(2,1)S(1)}, u32[]{:S(2)}, u32[]{:S(2)}) collective-permute-start(bf16[32,2048]{1,0:T(8,128)(2,1)S(1)} %get-tuple-element.114), channel_id=1, source_target_pairs={{1,3},{3,1},{5,7},{7,5},{9,11},{11,9},{13,15},{15,13},{17,19},{19,... | collective-permute-start | bytes 393224 | tf_op jit(solution)/shard_map/ppermute | solution.py:431
  73.2 1.5 %collective-permute-start.24 = (f32[32,1024]{1,0:T(8,128)S(1)}, f32[32,1024]{1,0:T(8,128)S(1)}, u32[]{:S(2)}, u32[]{:S(2)}) collective-permute-start(f32[32,1024]{1,0:T(8,128)S(1)} %slice.61), channel_id=1, source_target_pairs={{0,1},{1,0},{2,3},{3,2},{4,5},{5,4},{6,7},{7,6},{8,9},{9,8},{10,11... | collective-permute-start | bytes 393224 | tf_op jit(solution)/shard_map/ppermute | solution.py:419

commit v7 on v6

--- a/solution.py
+++ b/solution.py
@@ -434,7 +434,7 @@
 
     def total_of(own, moved):
         result = 0.0
-        for s in (2, 3, 0, 1):
+        for s in sorted(range(slots), key=lambda s: (s + slots // 2) % slots):
             block = moved[s]
             for c in own_slot[s]:
                 block = jnp.where(core == c, own[s], block)

time: 76.1 us -> 76.2 us (level)
  starting transfers between devices: 25.8 us -> 27.4 us
    ppermute x9, starting transfers between devices: 1.99 us -> 3.04 us  [from_core(): return lax.ppermute(value, 'pair', [(c, c ^ m) for c in range(cores)])]
  transfers between devices with their start and end apart: 25 -> 25, of which waited for: 12 -> 12; matrix products, arithmetic and copies ran while one was open for 1% -> 1% of each run, Pallas kernels for 15% -> 14%
where the time goes in v7:
time: 76.2 us; the launch traced here: 76 us
  waiting for transfers between devices  28.2 us (37%)
  starting transfers between devices  27.4 us (36%)
  Pallas kernels  16.7 us (22%)
  local copies, waits for them, and re-layouts  2.57 us (3%)
  other arithmetic  0.86 us (1%)
    ppermute x16, waiting for transfers between devices, swap(): return lax.ppermute(value, ('dev', 'pair'), pairs)  25.1 us
    ppermute x16, starting transfers between devices, swap(): return lax.ppermute(value, ('dev', 'pair'), pairs)  24.4 us
    pallas_call x1, Pallas kernels, attend(): pl.pallas_call(functools.partial(attend_kernel, kv_heads, offset), out_sh...  6.33 us
    pallas_call x1, Pallas kernels, apply_experts(): pl.pallas_call(functools.partial(expert_kernel, offset, devs), out_shape=...  5.7 us
    pallas_call x1, Pallas kernels, fetch(): pl.pallas_call(functools.partial(fetch_kernel, count), out_shape=[jax.Sha...  3.79 us
    ppermute x9, waiting for transfers between devices, from_core(): return lax.ppermute(value, 'pair', [(c, c ^ m) for c in range(cores)])  3.16 us
    ppermute x9, starting transfers between devices, from_core(): return lax.ppermute(value, 'pair', [(c, c ^ m) for c in range(cores)])  3.04 us
    unnamed x12, local copies, waits for them, and re-layouts  1.72 us
  transfers between devices with their start and end apart: 25, of which 12 were waited for; matrix products, arithmetic and copies ran while one was open for 1% of the time, Pallas kernels for 14%

profile of v7, /device:TPU:0, one launch (start us, length us, event | category | flops | bytes accessed | tf_op | source)
XLA Modules:
  0.0 76.0 jit_solution(9832923284541958837)
XLA Ops:
  0.0 0.5 collective-permute-start
  0.5 0.1 collective-permute-start.1
  0.5 0.5 collective-permute-start.2
  1.0 6.3 %shard_map.136 = (bf16[4,16,1024]{2,1,0:T(8,128)(2,1)}, bf16[4,16,1024]{2,1,0:T(8,128)(2,1)}) custom-call(s32[16]{0:T(128)} %len_ref.1, s32[1]{0:T(128)} %bitcast.1.me_ref, s32[1]{0:T(128)} %bitcast.core_ref, bf16[16,64,128]{2,1,0:T(8,128)(2,1)} %q_hbm.1, bf16[16,1024,128]{2,1,0:T(8,128)(2,1)} %bitcast.27, bf16[16,1024,128]{2,1,0:T(8,128)(2,1)} %bitcast.28, ...), custom_call_target="tpu_custom_call" | custom-call | tf_op jit(solution)/shard_map/pallas_call | solution.py:172
  7.3 0.1 collective-permute-start.3
  7.5 0.8 %slice_bitcast_fusion.4 = (bf16[16,1024]{1,0:T(8,128)(2,1)S(1)}, bf16[16,1024]{1,0:T(8,128)(2,1)S(1)}, bf16[16,1024]{1,0:T(8,128)(2,1)S(1)}, bf16[16,1024]{1,0:T(8,128)(2,1)S(1)}) fusion(bf16[4,16,1024]{2,1,0:T(8,128)(2,1)} %get-tuple-element.62), kind=kLoop, calls=%fused_computation.14 | loop fusion | bytes 262144 | tf_op jit(solution)/shard_map/squeeze | solution.py:454
  8.3 0.0 copy-start.1
  8.3 0.0 copy-start.3
  8.3 0.0 copy-start.4
  8.3 0.6 collective-permute-done.3
  9.0 0.2 collective-permute-start.8
  9.2 5.0 %collective-permute-start.4 = (bf16[32,1024]{1,0:T(8,128)(2,1)S(1)}, bf16[32,1024]{1,0:T(8,128)(2,1)S(1)}, u32[]{:S(2)}, u32[]{:S(2)}) collective-permute-start(bf16[32,1024]{1,0:T(8,128)(2,1)S(1)} %get-tuple-element.69), channel_id=1, source_target_pairs={{0,10},{1,15},{2,8},{3,13},{4,14},{5,11},{6,12},{7,9},{8,2},{9,7},... | collective-permute-start | bytes 196616 | tf_op jit(solution)/shard_map/ppermute | solution.py:431
  14.2 0.7 collective-permute-start.5
  14.9 1.5 %collective-permute-start.6 = (bf16[32,1024]{1,0:T(8,128)(2,1)S(1)}, bf16[32,1024]{1,0:T(8,128)(2,1)S(1)}, u32[]{:S(2)}, u32[]{:S(2)}) collective-permute-start(bf16[32,1024]{1,0:T(8,128)(2,1)S(1)} %get-tuple-element.70), channel_id=1, source_target_pairs={{0,6},{1,9},{2,4},{3,11},{4,2},{5,13},{6,0},{7,15},{8,14},{9,1},{1... | collective-permute-start | bytes 196616 | tf_op jit(solution)/shard_map/ppermute | solution.py:431
  16.4 0.1 collective-permute-start.7
  16.4 1.6 %collective-permute-done.4.refs_0_ = bf16[32,1024]{1,0:T(8,128)(2,1)S(1)} collective-permute-done((bf16[32,1024]{1,0:T(8,128)(2,1)S(1)}, bf16[32,1024]{1,0:T(8,128)(2,1)S(1)}, u32[]{:S(2)}, u32[]{:S(2)}) %collective-permute-start.4) | collective-permute-done | bytes 65568 | tf_op jit(solution)/shard_map/ppermute | solution.py:431
  18.1 2.1 %collective-permute-done.6.refs_2_ = bf16[32,1024]{1,0:T(8,128)(2,1)S(1)} collective-permute-done((bf16[32,1024]{1,0:T(8,128)(2,1)S(1)}, bf16[32,1024]{1,0:T(8,128)(2,1)S(1)}, u32[]{:S(2)}, u32[]{:S(2)}) %collective-permute-start.6) | collective-permute-done | bytes 65568 | tf_op jit(solution)/shard_map/ppermute | solution.py:431
  20.2 2.8 %collective-permute-done.7.refs_3_ = bf16[32,1024]{1,0:T(8,128)(2,1)S(1)} collective-permute-done((bf16[32,1024]{1,0:T(8,128)(2,1)S(1)}, bf16[32,1024]{1,0:T(8,128)(2,1)S(1)}, u32[]{:S(2)}, u32[]{:S(2)}) %collective-permute-start.7) | collective-permute-done | bytes 65568 | tf_op jit(solution)/shard_map/ppermute | solution.py:431
  23.0 0.7 shard_map.137
  23.7 1.7 %collective-permute-start.11 = (bf16[32,2048]{1,0:T(8,128)(2,1)S(1)}, bf16[32,2048]{1,0:T(8,128)(2,1)S(1)}, u32[]{:S(2)}, u32[]{:S(2)}) collective-permute-start(bf16[32,2048]{1,0:T(8,128)(2,1)S(1)} %get-tuple-element.83), channel_id=1, source_target_pairs={{0,10},{1,15},{2,8},{3,13},{4,14},{5,11},{6,12},{7,9},{8,2},{9,7},... | collective-permute-start | bytes 393224 | tf_op jit(solution)/shard_map/ppermute | solution.py:431
  25.4 1.4 %collective-permute-start.10 = (bf16[32,2048]{1,0:T(8,128)(2,1)S(1)}, bf16[32,2048]{1,0:T(8,128)(2,1)S(1)}, u32[]{:S(2)}, u32[]{:S(2)}) collective-permute-start(bf16[32,2048]{1,0:T(8,128)(2,1)S(1)} %get-tuple-element.82), channel_id=1, source_target_pairs={{0,12},{1,5},{2,14},{3,7},{4,8},{5,1},{6,10},{7,3},{8,4},{9,13},{1... | collective-permute-start | bytes 393224 | tf_op jit(solution)/shard_map/ppermute | solution.py:431
  26.8 1.4 %collective-permute-start.9 = (bf16[32,2048]{1,0:T(8,128)(2,1)S(1)}, bf16[32,2048]{1,0:T(8,128)(2,1)S(1)}, u32[]{:S(2)}, u32[]{:S(2)}) collective-permute-start(bf16[32,2048]{1,0:T(8,128)(2,1)S(1)} %get-tuple-element.81), channel_id=1, source_target_pairs={{0,6},{1,9},{2,4},{3,11},{4,2},{5,13},{6,0},{7,15},{8,14},{9,1},{1... | collective-permute-start | bytes 393224 | tf_op jit(solution)/shard_map/ppermute | solution.py:431
  28.2 0.7 collective-permute-start.12
  28.9 7.5 %collective-permute-done.11 = bf16[32,2048]{1,0:T(8,128)(2,1)S(1)} collective-permute-done((bf16[32,2048]{1,0:T(8,128)(2,1)S(1)}, bf16[32,2048]{1,0:T(8,128)(2,1)S(1)}, u32[]{:S(2)}, u32[]{:S(2)}) %collective-permute-start.11) | collective-permute-done | bytes 131104 | tf_op jit(solution)/shard_map/ppermute | solution.py:431
  36.3 1.0 %collective-permute-done.9 = bf16[32,2048]{1,0:T(8,128)(2,1)S(1)} collective-permute-done((bf16[32,2048]{1,0:T(8,128)(2,1)S(1)}, bf16[32,2048]{1,0:T(8,128)(2,1)S(1)}, u32[]{:S(2)}, u32[]{:S(2)}) %collective-permute-start.9) | collective-permute-done | bytes 131104 | tf_op jit(solution)/shard_map/ppermute | solution.py:431
  37.4 0.1 convert_add_fusion.1.refs_0_
  37.5 0.1 collective-permute-start.14
  37.5 1.5 %collective-permute-done.14.refs_1_ = f32[32,2048]{1,0:T(8,128)S(1)} collective-permute-done((f32[32,2048]{1,0:T(8,128)S(1)}, f32[32,2048]{1,0:T(8,128)S(1)}, u32[]{:S(2)}, u32[]{:S(2)}) %collective-permute-start.14) | collective-permute-done | bytes 262176 | tf_op jit(solution)/shard_map/ppermute | solution.py:419
  39.1 0.2 shard_map.138
  39.3 0.2 collective-permute-start.19
  39.5 2.3 %collective-permute-start.15 = (bf16[32,2176]{1,0:T(8,128)(2,1)S(1)}, bf16[32,2176]{1,0:T(8,128)(2,1)S(1)}, u32[]{:S(2)}, u32[]{:S(2)}) collective-permute-start(bf16[32,2176]{1,0:T(8,128)(2,1)S(1)} %get-tuple-element.99.own_ref), channel_id=1, source_target_pairs={{0,10},{1,15},{2,8},{3,13},{4,14},{5,11},{6,12},{7,9},{8,2},{9,7},... | collective-permute-start | bytes 417800 | tf_op jit(solution)/shard_map/ppermute | solution.py:431
  41.8 0.7 collective-permute-start.16
  42.5 1.3 %collective-permute-start.17 = (bf16[32,2176]{1,0:T(8,128)(2,1)S(1)}, bf16[32,2176]{1,0:T(8,128)(2,1)S(1)}, u32[]{:S(2)}, u32[]{:S(2)}) collective-permute-start(bf16[32,2176]{1,0:T(8,128)(2,1)S(1)} %get-tuple-element.99.own_ref), channel_id=1, source_target_pairs={{0,6},{1,9},{2,4},{3,11},{4,2},{5,13},{6,0},{7,15},{8,14},{9,1},{1... | collective-permute-start | bytes 417800 | tf_op jit(solution)/shard_map/ppermute | solution.py:431
  43.8 1.7 %collective-permute-start.18 = (bf16[32,2176]{1,0:T(8,128)(2,1)S(1)}, bf16[32,2176]{1,0:T(8,128)(2,1)S(1)}, u32[]{:S(2)}, u32[]{:S(2)}) collective-permute-start(bf16[32,2176]{1,0:T(8,128)(2,1)S(1)} %get-tuple-element.99.own_ref), channel_id=1, source_target_pairs={{0,12},{1,5},{2,14},{3,7},{4,8},{5,1},{6,10},{7,3},{8,4},{9,13},{1... | collective-permute-start | bytes 417800 | tf_op jit(solution)/shard_map/ppermute | solution.py:431
  45.5 1.7 %copy-done.5 = bf16[2,768,1024]{2,1,0:T(8,128)(2,1)} copy-done((bf16[2,768,1024]{2,1,0:T(8,128)(2,1)}, bf16[2,768,1024]{2,1,0:T(8,128)(2,1)S(1)}, u32[]{:S(2)}) %copy-start.5) | copy-done | bytes 3145752
  47.2 3.8 %shard_map.139 = (bf16[1024,768]{1,0:T(8,128)(2,1)S(1)}, bf16[1024,768]{1,0:T(8,128)(2,1)S(1)}, bf16[1024,768]{1,0:T(8,128)(2,1)S(1)}, bf16[1024,768]{1,0:T(8,12...) custom-call(bf16[2,1024,768]{2,1,0:T(8,128)(2,1)} %refs_10_, ...), custom_call_target="tpu_custom_call" | custom-call | tf_op jit(solution)/shard_map/pallas_call | solution.py:303
  51.0 2.7 %collective-permute-done.15.refs_0_ = bf16[32,2176]{1,0:T(8,128)(2,1)S(1)} collective-permute-done((bf16[32,2176]{1,0:T(8,128)(2,1)S(1)}, bf16[32,2176]{1,0:T(8,128)(2,1)S(1)}, u32[]{:S(2)}, u32[]{:S(2)}) %collective-permute-start.15) | collective-permute-done | bytes 139296 | tf_op jit(solution)/shard_map/ppermute | solution.py:431
  53.7 5.7 %shard_map.140 = (bf16[32,2048]{1,0:T(8,128)(2,1)S(1)}, bf16[32,2048]{1,0:T(8,128)(2,1)S(1)}, bf16[32,2048]{1,0:T(8,128)(2,1)S(1)}, bf16[32,2048]{1,0:T(8,128)(2,1)S(1)}) custom-call(s32[1]{0:T(128)} %bitcast.1.me_ref, s32[1]{0:T(128)} %bitcast.core_ref, bf16[32,2176]{1,0:T(8,128)(2,1)S(1)} %get-tuple-element.99.own_ref, ...), custom_call_target="tpu_custom_call" | custom-call | tf_op jit(solution)/shard_map/pallas_call | solution.py:375
  59.4 3.9 %collective-permute-start.22 = (bf16[32,2048]{1,0:T(8,128)(2,1)S(1)}, bf16[32,2048]{1,0:T(8,128)(2,1)S(1)}, u32[]{:S(2)}, u32[]{:S(2)}) collective-permute-start(bf16[32,2048]{1,0:T(8,128)(2,1)S(1)} %get-tuple-element.113), channel_id=1, source_target_pairs={{0,10},{1,15},{2,8},{3,13},{4,14},{5,11},{6,12},{7,9},{8,2},{9,7},... | collective-permute-start | bytes 393224 | tf_op jit(solution)/shard_map/ppermute | solution.py:431
  63.3 1.5 %collective-permute-start.21 = (bf16[32,2048]{1,0:T(8,128)(2,1)S(1)}, bf16[32,2048]{1,0:T(8,128)(2,1)S(1)}, u32[]{:S(2)}, u32[]{:S(2)}) collective-permute-start(bf16[32,2048]{1,0:T(8,128)(2,1)S(1)} %get-tuple-element.112), channel_id=1, source_target_pairs={{0,12},{1,5},{2,14},{3,7},{4,8},{5,1},{6,10},{7,3},{8,4},{9,13},{1... | collective-permute-start | bytes 393224 | tf_op jit(solution)/shard_map/ppermute | solution.py:431
  64.8 0.7 collective-permute-start.23
  65.5 4.1 %collective-permute-done.22 = bf16[32,2048]{1,0:T(8,128)(2,1)S(1)} collective-permute-done((bf16[32,2048]{1,0:T(8,128)(2,1)S(1)}, bf16[32,2048]{1,0:T(8,128)(2,1)S(1)}, u32[]{:S(2)}, u32[]{:S(2)}) %collective-permute-start.22) | collective-permute-done | bytes 131104 | tf_op jit(solution)/shard_map/ppermute | solution.py:431
  69.6 2.3 %collective-permute-done.21 = bf16[32,2048]{1,0:T(8,128)(2,1)S(1)} collective-permute-done((bf16[32,2048]{1,0:T(8,128)(2,1)S(1)}, bf16[32,2048]{1,0:T(8,128)(2,1)S(1)}, u32[]{:S(2)}, u32[]{:S(2)}) %collective-permute-start.21) | collective-permute-done | bytes 131104 | tf_op jit(solution)/shard_map/ppermute | solution.py:431
  72.0 0.8 %collective-permute-done.20 = bf16[32,2048]{1,0:T(8,128)(2,1)S(1)} collective-permute-done((bf16[32,2048]{1,0:T(8,128)(2,1)S(1)}, bf16[32,2048]{1,0:T(8,128)(2,1)S(1)}, u32[]{:S(2)}, u32[]{:S(2)}) %collective-permute-start.20) | collective-permute-done | bytes 131104 | tf_op jit(solution)/shard_map/ppermute | solution.py:431
  72.8 0.1 convert_add_fusion
  72.9 1.5 %collective-permute-start.24 = (f32[32,1024]{1,0:T(8,128)S(1)}, f32[32,1024]{1,0:T(8,128)S(1)}, u32[]{:S(2)}, u32[]{:S(2)}) collective-permute-start(f32[32,1024]{1,0:T(8,128)S(1)} %slice.61), channel_id=1, source_target_pairs={{0,1},{1,0},{2,3},{3,2},{4,5},{5,4},{6,7},{7,6},{8,9},{9,8},{10,11... | collective-permute-start | bytes 393224 | tf_op jit(solution)/shard_map/ppermute | solution.py:419
  74.3 1.0 %collective-permute-done.24 = f32[32,1024]{1,0:T(8,128)S(1)} collective-permute-done((f32[32,1024]{1,0:T(8,128)S(1)}, f32[32,1024]{1,0:T(8,128)S(1)}, u32[]{:S(2)}, u32[]{:S(2)}) %collective-permute-start.24) | collective-permute-done | bytes 131104 | tf_op jit(solution)/shard_map/ppermute | solution.py:419
  75.4 0.7 fusion.1
  (30 shorter events, 0.1 us)
Async XLA Ops:
  0.0 7.3 %collective-permute-start = (bf16[2,1024,768]{2,1,0:T(8,128)(2,1)}, bf16[2,1024,768]{2,1,0:T(8,128)(2,1)}, u32[]{:S(2)}, u32[]{:S(2)}) collective-permute-start(bf16[2,1024,768]{2,1,0:T(8,128)(2,1)} %refs_10_), channel_id=1, source_target_pairs={{0,1},{1,0},{2,3},{3,2},{4,5},{5,4},{6,7},{7,6},{8,9},{9,8},{10,11... | collective-permute-start | bytes 9437192 | tf_op jit(solution)/shard_map/ppermute | solution.py:419
  0.5 6.9 %collective-permute-start.1 = (bf16[32,1024]{1,0:T(8,128)(2,1)}, bf16[32,1024]{1,0:T(8,128)(2,1)S(1)}, u32[]{:S(2)}, u32[]{:S(2)}) collective-permute-start(bf16[32,1024]{1,0:T(8,128)(2,1)} %refs_2_), channel_id=1, source_target_pairs={{0,1},{1,0},{2,3},{3,2},{4,5},{5,4},{6,7},{7,6},{8,9},{9,8},{10,11... | collective-permute-start | bytes 196616 | tf_op jit(solution)/shard_map/ppermute | solution.py:419
  0.5 6.8 %collective-permute-start.2 = (f32[1,1024]{1,0:T(1,128)}, f32[1,1024]{1,0:T(1,128)S(1)}, u32[]{:S(2)}, u32[]{:S(2)}) collective-permute-start(f32[1,1024]{1,0:T(1,128)} %bitcast.23), channel_id=1, source_target_pairs={{0,1},{1,0},{2,3},{3,2},{4,5},{5,4},{6,7},{7,6},{8,9},{9,8},{10,11... | collective-permute-start | bytes 12296 | tf_op jit(solution)/shard_map/ppermute | solution.py:419
  1.0 8.1 %copy-start = (bf16[1024,1024]{1,0:T(8,128)(2,1)S(1)}, bf16[1024,1024]{1,0:T(8,128)(2,1)}, u32[]{:S(2)}) copy-start(bf16[1024,1024]{1,0:T(8,128)(2,1)} %refs_4_) | copy-start | bytes 6291460
  7.3 1.6 %collective-permute-start.3 = (bf16[4,16,1024]{2,1,0:T(8,128)(2,1)}, bf16[4,16,1024]{2,1,0:T(8,128)(2,1)S(1)}, u32[]{:S(2)}, u32[]{:S(2)}) collective-permute-start(bf16[4,16,1024]{2,1,0:T(8,128)(2,1)} %get-tuple-element.64), channel_id=1, source_target_pairs={{0,1},{1,0},{2,3},{3,2},{4,5},{5,4},{6,7},{7,6},{8,9},{9,8},{10,11... | collective-permute-start | bytes 393224 | tf_op jit(solution)/shard_map/ppermute | solution.py:419
  8.3 30.8 %copy-start.1 = (bf16[32,1024]{1,0:T(8,128)(2,1)S(1)}, bf16[32,1024]{1,0:T(8,128)(2,1)}, u32[]{:S(2)}) copy-start(bf16[32,1024]{1,0:T(8,128)(2,1)} %refs_2_) | copy-start | bytes 196612
  8.3 30.8 %copy-start.2 = (f32[1024]{0:T(1024)S(1)}, f32[1024]{0:T(1024)}, u32[]{:S(2)}) copy-start(f32[1024]{0:T(1024)} %param.22) | copy-start | bytes 12292
  8.3 30.8 %copy-start.3 = (s32[32,8]{0,1:T(8,128)S(1)}, s32[32,8]{0,1:T(8,128)}, u32[]{:S(2)}) copy-start(s32[32,8]{0,1:T(8,128)} %param.23) | copy-start | bytes 3076
  8.3 30.8 %copy-start.4 = (f32[32,8]{0,1:T(8,128)S(1)}, f32[32,8]{0,1:T(8,128)}, u32[]{:S(2)}) copy-start(f32[32,8]{0,1:T(8,128)} %param.24) | copy-start | bytes 3076
  9.0 14.0 %collective-permute-start.8 = (bf16[1024,1024]{1,0:T(8,128)(2,1)S(1)}, bf16[1024,1024]{1,0:T(8,128)(2,1)S(1)}, u32[]{:S(2)}, u32[]{:S(2)}) collective-permute-start(bf16[1024,1024]{1,0:T(8,128)(2,1)S(1)} %copy-done), channel_id=1, source_target_pairs={{0,1},{1,0},{2,3},{3,2},{4,5},{5,4},{6,7},{7,6},{8,9},{9,8},{10,11... | collective-permute-start | bytes 6291464 | tf_op jit(solution)/shard_map/ppermute | solution.py:419
  9.2 8.8 %collective-permute-start.4 = (bf16[32,1024]{1,0:T(8,128)(2,1)S(1)}, bf16[32,1024]{1,0:T(8,128)(2,1)S(1)}, u32[]{:S(2)}, u32[]{:S(2)}) collective-permute-start(bf16[32,1024]{1,0:T(8,128)(2,1)S(1)} %get-tuple-element.69), channel_id=1, source_target_pairs={{0,10},{1,15},{2,8},{3,13},{4,14},{5,11},{6,12},{7,9},{8,2},{9,7},... | collective-permute-start | bytes 196616 | tf_op jit(solution)/shard_map/ppermute | solution.py:431
  14.2 3.8 %collective-permute-start.5 = (bf16[32,1024]{1,0:T(8,128)(2,1)S(1)}, bf16[32,1024]{1,0:T(8,128)(2,1)S(1)}, u32[]{:S(2)}, u32[]{:S(2)}) collective-permute-start(bf16[32,1024]{1,0:T(8,128)(2,1)S(1)} %get-tuple-element.68.own_ref), channel_id=1, source_target_pairs={{1,3},{3,1},{5,7},{7,5},{9,11},{11,9},{13,15},{15,13},{17,19},{19,... | collective-permute-start | bytes 196616 | tf_op jit(solution)/shard_map/ppermute | solution.py:431
  14.9 5.3 %collective-permute-start.6 = (bf16[32,1024]{1,0:T(8,128)(2,1)S(1)}, bf16[32,1024]{1,0:T(8,128)(2,1)S(1)}, u32[]{:S(2)}, u32[]{:S(2)}) collective-permute-start(bf16[32,1024]{1,0:T(8,128)(2,1)S(1)} %get-tuple-element.70), channel_id=1, source_target_pairs={{0,6},{1,9},{2,4},{3,11},{4,2},{5,13},{6,0},{7,15},{8,14},{9,1},{1... | collective-permute-start | bytes 196616 | tf_op jit(solution)/shard_map/ppermute | solution.py:431
  16.4 6.6 %collective-permute-start.7 = (bf16[32,1024]{1,0:T(8,128)(2,1)S(1)}, bf16[32,1024]{1,0:T(8,128)(2,1)S(1)}, u32[]{:S(2)}, u32[]{:S(2)}) collective-permute-start(bf16[32,1024]{1,0:T(8,128)(2,1)S(1)} %get-tuple-element.71), channel_id=1, source_target_pairs={{0,12},{1,5},{2,14},{3,7},{4,8},{5,1},{6,10},{7,3},{8,4},{9,13},{1... | collective-permute-start | bytes 196616 | tf_op jit(solution)/shard_map/ppermute | solution.py:431
  23.0 14.4 %collective-permute-start.13 = (bf16[2,1024,768]{2,1,0:T(8,128)(2,1)}, bf16[2,1024,768]{2,1,0:T(8,128)(2,1)}, u32[]{:S(2)}, u32[]{:S(2)}) collective-permute-start(bf16[2,1024,768]{2,1,0:T(8,128)(2,1)} %refs_12_), channel_id=1, source_target_pairs={{0,1},{1,0},{2,3},{3,2},{4,5},{5,4},{6,7},{7,6},{8,9},{9,8},{10,11... | collective-permute-start | bytes 9437192 | tf_op jit(solution)/shard_map/ppermute | solution.py:419
  23.7 12.6 %collective-permute-start.11 = (bf16[32,2048]{1,0:T(8,128)(2,1)S(1)}, bf16[32,2048]{1,0:T(8,128)(2,1)S(1)}, u32[]{:S(2)}, u32[]{:S(2)}) collective-permute-start(bf16[32,2048]{1,0:T(8,128)(2,1)S(1)} %get-tuple-element.83), channel_id=1, source_target_pairs={{0,10},{1,15},{2,8},{3,13},{4,14},{5,11},{6,12},{7,9},{8,2},{9,7},... | collective-permute-start | bytes 393224 | tf_op jit(solution)/shard_map/ppermute | solution.py:431
  25.4 10.9 %collective-permute-start.10 = (bf16[32,2048]{1,0:T(8,128)(2,1)S(1)}, bf16[32,2048]{1,0:T(8,128)(2,1)S(1)}, u32[]{:S(2)}, u32[]{:S(2)}) collective-permute-start(bf16[32,2048]{1,0:T(8,128)(2,1)S(1)} %get-tuple-element.82), channel_id=1, source_target_pairs={{0,12},{1,5},{2,14},{3,7},{4,8},{5,1},{6,10},{7,3},{8,4},{9,13},{1... | collective-permute-start | bytes 393224 | tf_op jit(solution)/shard_map/ppermute | solution.py:431
  26.8 10.6 %collective-permute-start.9 = (bf16[32,2048]{1,0:T(8,128)(2,1)S(1)}, bf16[32,2048]{1,0:T(8,128)(2,1)S(1)}, u32[]{:S(2)}, u32[]{:S(2)}) collective-permute-start(bf16[32,2048]{1,0:T(8,128)(2,1)S(1)} %get-tuple-element.81), channel_id=1, source_target_pairs={{0,6},{1,9},{2,4},{3,11},{4,2},{5,13},{6,0},{7,15},{8,14},{9,1},{1... | collective-permute-start | bytes 393224 | tf_op jit(solution)/shard_map/ppermute | solution.py:431
  28.2 9.2 %collective-permute-start.12 = (bf16[32,2048]{1,0:T(8,128)(2,1)S(1)}, bf16[32,2048]{1,0:T(8,128)(2,1)S(1)}, u32[]{:S(2)}, u32[]{:S(2)}) collective-permute-start(bf16[32,2048]{1,0:T(8,128)(2,1)S(1)} %get-tuple-element.84), channel_id=1, source_target_pairs={{1,3},{3,1},{5,7},{7,5},{9,11},{11,9},{13,15},{15,13},{17,19},{19,... | collective-permute-start | bytes 393224 | tf_op jit(solution)/shard_map/ppermute | solution.py:431
  37.5 1.6 %collective-permute-start.14 = (f32[32,2048]{1,0:T(8,128)S(1)}, f32[32,2048]{1,0:T(8,128)S(1)}, u32[]{:S(2)}, u32[]{:S(2)}) collective-permute-start(f32[32,2048]{1,0:T(8,128)S(1)} %convert_add_fusion.1.refs_0_), channel_id=1, source_target_pairs={{0,1},{1,0},{2,3},{3,2},{4,5},{5,4},{6,7},{7,6},{8,9},{9,8},{10,11... | collective-permute-start | bytes 786440 | tf_op jit(solution)/shard_map/ppermute | solution.py:419
  39.3 6.2 %collective-permute-start.19 = (bf16[2,768,1024]{2,1,0:T(8,128)(2,1)}, bf16[2,768,1024]{2,1,0:T(8,128)(2,1)S(1)}, u32[]{:S(2)}, u32[]{:S(2)}) collective-permute-start(bf16[2,768,1024]{2,1,0:T(8,128)(2,1)} %refs_14_), channel_id=1, source_target_pairs={{0,1},{1,0},{2,3},{3,2},{4,5},{5,4},{6,7},{7,6},{8,9},{9,8},{10,11... | collective-permute-start | bytes 9437192 | tf_op jit(solution)/shard_map/ppermute | solution.py:419
  39.5 14.3 %collective-permute-start.15 = (bf16[32,2176]{1,0:T(8,128)(2,1)S(1)}, bf16[32,2176]{1,0:T(8,128)(2,1)S(1)}, u32[]{:S(2)}, u32[]{:S(2)}) collective-permute-start(bf16[32,2176]{1,0:T(8,128)(2,1)S(1)} %get-tuple-element.99.own_ref), channel_id=1, source_target_pairs={{0,10},{1,15},{2,8},{3,13},{4,14},{5,11},{6,12},{7,9},{8,2},{9,7},... | collective-permute-start | bytes 417800 | tf_op jit(solution)/shard_map/ppermute | solution.py:431
  41.8 11.9 %collective-permute-start.16 = (bf16[32,2176]{1,0:T(8,128)(2,1)S(1)}, bf16[32,2176]{1,0:T(8,128)(2,1)S(1)}, u32[]{:S(2)}, u32[]{:S(2)}) collective-permute-start(bf16[32,2176]{1,0:T(8,128)(2,1)S(1)} %get-tuple-element.99.own_ref), channel_id=1, source_target_pairs={{1,3},{3,1},{5,7},{7,5},{9,11},{11,9},{13,15},{15,13},{17,19},{19,... | collective-permute-start | bytes 417800 | tf_op jit(solution)/shard_map/ppermute | solution.py:431
  42.5 11.3 %collective-permute-start.17 = (bf16[32,2176]{1,0:T(8,128)(2,1)S(1)}, bf16[32,2176]{1,0:T(8,128)(2,1)S(1)}, u32[]{:S(2)}, u32[]{:S(2)}) collective-permute-start(bf16[32,2176]{1,0:T(8,128)(2,1)S(1)} %get-tuple-element.99.own_ref), channel_id=1, source_target_pairs={{0,6},{1,9},{2,4},{3,11},{4,2},{5,13},{6,0},{7,15},{8,14},{9,1},{1... | collective-permute-start | bytes 417800 | tf_op jit(solution)/shard_map/ppermute | solution.py:431
  43.8 9.9 %collective-permute-start.18 = (bf16[32,2176]{1,0:T(8,128)(2,1)S(1)}, bf16[32,2176]{1,0:T(8,128)(2,1)S(1)}, u32[]{:S(2)}, u32[]{:S(2)}) collective-permute-start(bf16[32,2176]{1,0:T(8,128)(2,1)S(1)} %get-tuple-element.99.own_ref), channel_id=1, source_target_pairs={{0,12},{1,5},{2,14},{3,7},{4,8},{5,1},{6,10},{7,3},{8,4},{9,13},{1... | collective-permute-start | bytes 417800 | tf_op jit(solution)/shard_map/ppermute | solution.py:431
  45.5 1.7 %copy-start.5 = (bf16[2,768,1024]{2,1,0:T(8,128)(2,1)}, bf16[2,768,1024]{2,1,0:T(8,128)(2,1)S(1)}, u32[]{:S(2)}) copy-start(bf16[2,768,1024]{2,1,0:T(8,128)(2,1)S(1)} %collective-permute-done.19.refs_5_.refs_15_) | copy-start | bytes 9437188
  59.4 10.2 %collective-permute-start.22 = (bf16[32,2048]{1,0:T(8,128)(2,1)S(1)}, bf16[32,2048]{1,0:T(8,128)(2,1)S(1)}, u32[]{:S(2)}, u32[]{:S(2)}) collective-permute-start(bf16[32,2048]{1,0:T(8,128)(2,1)S(1)} %get-tuple-element.113), channel_id=1, source_target_pairs={{0,10},{1,15},{2,8},{3,13},{4,14},{5,11},{6,12},{7,9},{8,2},{9,7},... | collective-permute-start | bytes 393224 | tf_op jit(solution)/shard_map/ppermute | solution.py:431
  63.3 8.7 %collective-permute-start.21 = (bf16[32,2048]{1,0:T(8,128)(2,1)S(1)}, bf16[32,2048]{1,0:T(8,128)(2,1)S(1)}, u32[]{:S(2)}, u32[]{:S(2)}) collective-permute-start(bf16[32,2048]{1,0:T(8,128)(2,1)S(1)} %get-tuple-element.112), channel_id=1, source_target_pairs={{0,12},{1,5},{2,14},{3,7},{4,8},{5,1},{6,10},{7,3},{8,4},{9,13},{1... | collective-permute-start | bytes 393224 | tf_op jit(solution)/shard_map/ppermute | solution.py:431
  64.8 7.9 %collective-permute-start.20 = (bf16[32,2048]{1,0:T(8,128)(2,1)S(1)}, bf16[32,2048]{1,0:T(8,128)(2,1)S(1)}, u32[]{:S(2)}, u32[]{:S(2)}) collective-permute-start(bf16[32,2048]{1,0:T(8,128)(2,1)S(1)} %get-tuple-element.111), channel_id=1, source_target_pairs={{0,6},{1,9},{2,4},{3,11},{4,2},{5,13},{6,0},{7,15},{8,14},{9,1},{1... | collective-permute-start | bytes 393224 | tf_op jit(solution)/shard_map/ppermute | solution.py:431
  64.8 7.9 %collective-permute-start.23 = (bf16[32,2048]{1,0:T(8,128)(2,1)S(1)}, bf16[32,2048]{1,0:T(8,128)(2,1)S(1)}, u32[]{:S(2)}, u32[]{:S(2)}) collective-permute-start(bf16[32,2048]{1,0:T(8,128)(2,1)S(1)} %get-tuple-element.114), channel_id=1, source_target_pairs={{1,3},{3,1},{5,7},{7,5},{9,11},{11,9},{13,15},{15,13},{17,19},{19,... | collective-permute-start | bytes 393224 | tf_op jit(solution)/shard_map/ppermute | solution.py:431
  72.9 2.5 %collective-permute-start.24 = (f32[32,1024]{1,0:T(8,128)S(1)}, f32[32,1024]{1,0:T(8,128)S(1)}, u32[]{:S(2)}, u32[]{:S(2)}) collective-permute-start(f32[32,1024]{1,0:T(8,128)S(1)} %slice.61), channel_id=1, source_target_pairs={{0,1},{1,0},{2,3},{3,2},{4,5},{5,4},{6,7},{7,6},{8,9},{9,8},{10,11... | collective-permute-start | bytes 393224 | tf_op jit(solution)/shard_map/ppermute | solution.py:419

commit v8 on v7

--- a/solution.py
+++ b/solution.py
@@ -434,7 +434,7 @@
 
     def total_of(own, moved):
         result = 0.0
-        for s in sorted(range(slots), key=lambda s: (s + slots // 2) % slots):
+        for s in reversed(range(slots)):
             block = moved[s]
             for c in own_slot[s]:
                 block = jnp.where(core == c, own[s], block)

time: 76.2 us -> 76.3 us (level)
    ppermute x9, starting transfers between devices: 3.04 us -> 1.76 us  [from_core(): return lax.ppermute(value, 'pair', [(c, c ^ m) for c in range(cores)])]
  transfers between devices with their start and end apart: 25 -> 25, of which waited for: 12 -> 12; matrix products, arithmetic and copies ran while one was open for 1% -> 1% of each run, Pallas kernels for 14% -> 15%
where the time goes in v8:
time: 76.3 us; the launch traced here: 76.2 us
  waiting for transfers between devices  28.7 us (38%)
  starting transfers between devices  26.8 us (35%)
  Pallas kernels  17 us (22%)
  local copies, waits for them, and re-layouts  2.57 us (3%)
  other arithmetic  0.86 us (1%)
    ppermute x16, waiting for transfers between devices, swap(): return lax.ppermute(value, ('dev', 'pair'), pairs)  25.3 us
    ppermute x16, starting transfers between devices, swap(): return lax.ppermute(value, ('dev', 'pair'), pairs)  25 us
    pallas_call x1, Pallas kernels, attend(): pl.pallas_call(functools.partial(attend_kernel, kv_heads, offset), out_sh...  6.6 us
    pallas_call x1, Pallas kernels, apply_experts(): pl.pallas_call(functools.partial(expert_kernel, offset, devs), out_shape=...  5.69 us
    pallas_call x1, Pallas kernels, fetch(): pl.pallas_call(functools.partial(fetch_kernel, count), out_shape=[jax.Sha...  3.79 us
    ppermute x9, waiting for transfers between devices, from_core(): return lax.ppermute(value, 'pair', [(c, c ^ m) for c in range(cores)])  3.4 us
    ppermute x9, starting transfers between devices, from_core(): return lax.ppermute(value, 'pair', [(c, c ^ m) for c in range(cores)])  1.76 us
    unnamed x12, local copies, waits for them, and re-layouts  1.72 us
  transfers between devices with their start and end apart: 25, of which 12 were waited for; matrix products, arithmetic and copies ran while one was open for 1% of the time, Pallas kernels for 15%

profile of v8, /device:TPU:0, one launch (start us, length us, event | category | flops | bytes accessed | tf_op | source)
XLA Modules:
  0.0 76.2 jit_solution(8117463526689506732)
XLA Ops:
  0.0 0.5 collective-permute-start
  0.5 0.1 collective-permute-start.1
  0.5 0.5 collective-permute-start.2
  1.0 6.6 %shard_map.136 = (bf16[4,16,1024]{2,1,0:T(8,128)(2,1)}, bf16[4,16,1024]{2,1,0:T(8,128)(2,1)}) custom-call(s32[16]{0:T(128)} %len_ref.1, s32[1]{0:T(128)} %bitcast.1.me_ref, s32[1]{0:T(128)} %bitcast.core_ref, bf16[16,64,128]{2,1,0:T(8,128)(2,1)} %q_hbm.1, bf16[16,1024,128]{2,1,0:T(8,128)(2,1)} %bitcast.27, bf16[16,1024,128]{2,1,0:T(8,128)(2,1)} %bitcast.28, ...), custom_call_target="tpu_custom_call" | custom-call | tf_op jit(solution)/shard_map/pallas_call | solution.py:172
  7.6 0.2 collective-permute-start.3
  7.8 0.8 %slice_bitcast_fusion.4 = (bf16[16,1024]{1,0:T(8,128)(2,1)S(1)}, bf16[16,1024]{1,0:T(8,128)(2,1)S(1)}, bf16[16,1024]{1,0:T(8,128)(2,1)S(1)}, bf16[16,1024]{1,0:T(8,128)(2,1)S(1)}) fusion(bf16[4,16,1024]{2,1,0:T(8,128)(2,1)} %get-tuple-element.62), kind=kLoop, calls=%fused_computation.14 | loop fusion | bytes 262144 | tf_op jit(solution)/shard_map/squeeze | solution.py:454
  8.6 0.0 copy-start.1
  8.7 0.0 copy-start.3
  8.7 0.0 copy-start.4
  8.7 0.5 collective-permute-done.3
  9.3 0.2 collective-permute-start.8
  9.5 4.8 %collective-permute-start.4 = (bf16[32,1024]{1,0:T(8,128)(2,1)S(1)}, bf16[32,1024]{1,0:T(8,128)(2,1)S(1)}, u32[]{:S(2)}, u32[]{:S(2)}) collective-permute-start(bf16[32,1024]{1,0:T(8,128)(2,1)S(1)} %get-tuple-element.69), channel_id=1, source_target_pairs={{0,10},{1,15},{2,8},{3,13},{4,14},{5,11},{6,12},{7,9},{8,2},{9,7},... | collective-permute-start | bytes 196616 | tf_op jit(solution)/shard_map/ppermute | solution.py:431
  14.3 0.7 collective-permute-start.5
  15.0 1.5 %collective-permute-start.6 = (bf16[32,1024]{1,0:T(8,128)(2,1)S(1)}, bf16[32,1024]{1,0:T(8,128)(2,1)S(1)}, u32[]{:S(2)}, u32[]{:S(2)}) collective-permute-start(bf16[32,1024]{1,0:T(8,128)(2,1)S(1)} %get-tuple-element.70), channel_id=1, source_target_pairs={{0,6},{1,9},{2,4},{3,11},{4,2},{5,13},{6,0},{7,15},{8,14},{9,1},{1... | collective-permute-start | bytes 196616 | tf_op jit(solution)/shard_map/ppermute | solution.py:431
  16.5 0.1 collective-permute-start.7
  16.5 1.6 %collective-permute-done.4.refs_0_ = bf16[32,1024]{1,0:T(8,128)(2,1)S(1)} collective-permute-done((bf16[32,1024]{1,0:T(8,128)(2,1)S(1)}, bf16[32,1024]{1,0:T(8,128)(2,1)S(1)}, u32[]{:S(2)}, u32[]{:S(2)}) %collective-permute-start.4) | collective-permute-done | bytes 65568 | tf_op jit(solution)/shard_map/ppermute | solution.py:431
  18.2 2.1 %collective-permute-done.6.refs_2_ = bf16[32,1024]{1,0:T(8,128)(2,1)S(1)} collective-permute-done((bf16[32,1024]{1,0:T(8,128)(2,1)S(1)}, bf16[32,1024]{1,0:T(8,128)(2,1)S(1)}, u32[]{:S(2)}, u32[]{:S(2)}) %collective-permute-start.6) | collective-permute-done | bytes 65568 | tf_op jit(solution)/shard_map/ppermute | solution.py:431
  20.3 2.8 %collective-permute-done.7.refs_3_ = bf16[32,1024]{1,0:T(8,128)(2,1)S(1)} collective-permute-done((bf16[32,1024]{1,0:T(8,128)(2,1)S(1)}, bf16[32,1024]{1,0:T(8,128)(2,1)S(1)}, u32[]{:S(2)}, u32[]{:S(2)}) %collective-permute-start.7) | collective-permute-done | bytes 65568 | tf_op jit(solution)/shard_map/ppermute | solution.py:431
  23.1 0.7 shard_map.137
  23.8 1.5 %collective-permute-start.12 = (bf16[32,2048]{1,0:T(8,128)(2,1)S(1)}, bf16[32,2048]{1,0:T(8,128)(2,1)S(1)}, u32[]{:S(2)}, u32[]{:S(2)}) collective-permute-start(bf16[32,2048]{1,0:T(8,128)(2,1)S(1)} %get-tuple-element.84), channel_id=1, source_target_pairs={{0,10},{1,15},{2,8},{3,13},{4,14},{5,11},{6,12},{7,9},{8,2},{9,7},... | collective-permute-start | bytes 393224 | tf_op jit(solution)/shard_map/ppermute | solution.py:431
  25.4 1.4 %collective-permute-start.10 = (bf16[32,2048]{1,0:T(8,128)(2,1)S(1)}, bf16[32,2048]{1,0:T(8,128)(2,1)S(1)}, u32[]{:S(2)}, u32[]{:S(2)}) collective-permute-start(bf16[32,2048]{1,0:T(8,128)(2,1)S(1)} %get-tuple-element.82), channel_id=1, source_target_pairs={{0,6},{1,9},{2,4},{3,11},{4,2},{5,13},{6,0},{7,15},{8,14},{9,1},{1... | collective-permute-start | bytes 393224 | tf_op jit(solution)/shard_map/ppermute | solution.py:431
  26.8 2.4 %collective-permute-start.9 = (bf16[32,2048]{1,0:T(8,128)(2,1)S(1)}, bf16[32,2048]{1,0:T(8,128)(2,1)S(1)}, u32[]{:S(2)}, u32[]{:S(2)}) collective-permute-start(bf16[32,2048]{1,0:T(8,128)(2,1)S(1)} %get-tuple-element.81), channel_id=1, source_target_pairs={{0,12},{1,5},{2,14},{3,7},{4,8},{5,1},{6,10},{7,3},{8,4},{9,13},{1... | collective-permute-start | bytes 393224 | tf_op jit(solution)/shard_map/ppermute | solution.py:431
  29.2 0.7 collective-permute-start.11
  29.9 7.0 %collective-permute-done.12 = bf16[32,2048]{1,0:T(8,128)(2,1)S(1)} collective-permute-done((bf16[32,2048]{1,0:T(8,128)(2,1)S(1)}, bf16[32,2048]{1,0:T(8,128)(2,1)S(1)}, u32[]{:S(2)}, u32[]{:S(2)}) %collective-permute-start.12) | collective-permute-done | bytes 131104 | tf_op jit(solution)/shard_map/ppermute | solution.py:431
  36.9 1.2 %collective-permute-done.10 = bf16[32,2048]{1,0:T(8,128)(2,1)S(1)} collective-permute-done((bf16[32,2048]{1,0:T(8,128)(2,1)S(1)}, bf16[32,2048]{1,0:T(8,128)(2,1)S(1)}, u32[]{:S(2)}, u32[]{:S(2)}) %collective-permute-start.10) | collective-permute-done | bytes 131104 | tf_op jit(solution)/shard_map/ppermute | solution.py:431
  38.1 0.1 convert_add_fusion.1.refs_0_
  38.2 0.1 collective-permute-start.14
  38.3 1.5 %collective-permute-done.14.refs_1_ = f32[32,2048]{1,0:T(8,128)S(1)} collective-permute-done((f32[32,2048]{1,0:T(8,128)S(1)}, f32[32,2048]{1,0:T(8,128)S(1)}, u32[]{:S(2)}, u32[]{:S(2)}) %collective-permute-start.14) | collective-permute-done | bytes 262176 | tf_op jit(solution)/shard_map/ppermute | solution.py:419
  39.8 0.2 shard_map.138
  40.0 0.2 collective-permute-start.19
  40.2 1.7 %collective-permute-start.15 = (bf16[32,2176]{1,0:T(8,128)(2,1)S(1)}, bf16[32,2176]{1,0:T(8,128)(2,1)S(1)}, u32[]{:S(2)}, u32[]{:S(2)}) collective-permute-start(bf16[32,2176]{1,0:T(8,128)(2,1)S(1)} %get-tuple-element.99.own_ref), channel_id=1, source_target_pairs={{0,10},{1,15},{2,8},{3,13},{4,14},{5,11},{6,12},{7,9},{8,2},{9,7},... | collective-permute-start | bytes 417800 | tf_op jit(solution)/shard_map/ppermute | solution.py:431
  41.8 0.7 collective-permute-start.16
  42.5 1.1 %collective-permute-start.17 = (bf16[32,2176]{1,0:T(8,128)(2,1)S(1)}, bf16[32,2176]{1,0:T(8,128)(2,1)S(1)}, u32[]{:S(2)}, u32[]{:S(2)}) collective-permute-start(bf16[32,2176]{1,0:T(8,128)(2,1)S(1)} %get-tuple-element.99.own_ref), channel_id=1, source_target_pairs={{0,6},{1,9},{2,4},{3,11},{4,2},{5,13},{6,0},{7,15},{8,14},{9,1},{1... | collective-permute-start | bytes 417800 | tf_op jit(solution)/shard_map/ppermute | solution.py:431
  43.6 2.6 %collective-permute-start.18 = (bf16[32,2176]{1,0:T(8,128)(2,1)S(1)}, bf16[32,2176]{1,0:T(8,128)(2,1)S(1)}, u32[]{:S(2)}, u32[]{:S(2)}) collective-permute-start(bf16[32,2176]{1,0:T(8,128)(2,1)S(1)} %get-tuple-element.99.own_ref), channel_id=1, source_target_pairs={{0,12},{1,5},{2,14},{3,7},{4,8},{5,1},{6,10},{7,3},{8,4},{9,13},{1... | collective-permute-start | bytes 417800 | tf_op jit(solution)/shard_map/ppermute | solution.py:431
  46.2 1.7 %copy-done.5 = bf16[2,768,1024]{2,1,0:T(8,128)(2,1)} copy-done((bf16[2,768,1024]{2,1,0:T(8,128)(2,1)}, bf16[2,768,1024]{2,1,0:T(8,128)(2,1)S(1)}, u32[]{:S(2)}) %copy-start.5) | copy-done | bytes 3145752
  47.9 3.8 %shard_map.139 = (bf16[1024,768]{1,0:T(8,128)(2,1)S(1)}, bf16[1024,768]{1,0:T(8,128)(2,1)S(1)}, bf16[1024,768]{1,0:T(8,128)(2,1)S(1)}, bf16[1024,768]{1,0:T(8,12...) custom-call(bf16[2,1024,768]{2,1,0:T(8,128)(2,1)} %refs_10_, ...), custom_call_target="tpu_custom_call" | custom-call | tf_op jit(solution)/shard_map/pallas_call | solution.py:303
  51.7 2.7 %collective-permute-done.15.refs_0_ = bf16[32,2176]{1,0:T(8,128)(2,1)S(1)} collective-permute-done((bf16[32,2176]{1,0:T(8,128)(2,1)S(1)}, bf16[32,2176]{1,0:T(8,128)(2,1)S(1)}, u32[]{:S(2)}, u32[]{:S(2)}) %collective-permute-start.15) | collective-permute-done | bytes 139296 | tf_op jit(solution)/shard_map/ppermute | solution.py:431
  54.4 0.4 collective-permute-done.17.refs_2_
  54.8 5.7 %shard_map.140 = (bf16[32,2048]{1,0:T(8,128)(2,1)S(1)}, bf16[32,2048]{1,0:T(8,128)(2,1)S(1)}, bf16[32,2048]{1,0:T(8,128)(2,1)S(1)}, bf16[32,2048]{1,0:T(8,128)(2,1)S(1)}) custom-call(s32[1]{0:T(128)} %bitcast.1.me_ref, s32[1]{0:T(128)} %bitcast.core_ref, bf16[32,2176]{1,0:T(8,128)(2,1)S(1)} %get-tuple-element.99.own_ref, ...), custom_call_target="tpu_custom_call" | custom-call | tf_op jit(solution)/shard_map/pallas_call | solution.py:375
  60.5 2.8 %collective-permute-start.23 = (bf16[32,2048]{1,0:T(8,128)(2,1)S(1)}, bf16[32,2048]{1,0:T(8,128)(2,1)S(1)}, u32[]{:S(2)}, u32[]{:S(2)}) collective-permute-start(bf16[32,2048]{1,0:T(8,128)(2,1)S(1)} %get-tuple-element.114), channel_id=1, source_target_pairs={{0,10},{1,15},{2,8},{3,13},{4,14},{5,11},{6,12},{7,9},{8,2},{9,7},... | collective-permute-start | bytes 393224 | tf_op jit(solution)/shard_map/ppermute | solution.py:431
  63.3 2.5 %collective-permute-start.20 = (bf16[32,2048]{1,0:T(8,128)(2,1)S(1)}, bf16[32,2048]{1,0:T(8,128)(2,1)S(1)}, u32[]{:S(2)}, u32[]{:S(2)}) collective-permute-start(bf16[32,2048]{1,0:T(8,128)(2,1)S(1)} %get-tuple-element.111), channel_id=1, source_target_pairs={{0,12},{1,5},{2,14},{3,7},{4,8},{5,1},{6,10},{7,3},{8,4},{9,13},{1... | collective-permute-start | bytes 393224 | tf_op jit(solution)/shard_map/ppermute | solution.py:431
  65.8 0.7 collective-permute-start.22
  66.5 6.7 %collective-permute-done.23 = bf16[32,2048]{1,0:T(8,128)(2,1)S(1)} collective-permute-done((bf16[32,2048]{1,0:T(8,128)(2,1)S(1)}, bf16[32,2048]{1,0:T(8,128)(2,1)S(1)}, u32[]{:S(2)}, u32[]{:S(2)}) %collective-permute-start.23) | collective-permute-done | bytes 131104 | tf_op jit(solution)/shard_map/ppermute | solution.py:431
  73.2 0.7 collective-permute-done.20
  73.9 0.1 convert_add_fusion
  74.0 0.1 collective-permute-start.24
  74.1 1.3 %collective-permute-done.24 = f32[32,1024]{1,0:T(8,128)S(1)} collective-permute-done((f32[32,1024]{1,0:T(8,128)S(1)}, f32[32,1024]{1,0:T(8,128)S(1)}, u32[]{:S(2)}, u32[]{:S(2)}) %collective-permute-start.24) | collective-permute-done | bytes 131104 | tf_op jit(solution)/shard_map/ppermute | solution.py:419
  75.5 0.7 fusion.1
  (30 shorter events, 0.1 us)
Async XLA Ops:
  0.0 7.6 %collective-permute-start = (bf16[2,1024,768]{2,1,0:T(8,128)(2,1)}, bf16[2,1024,768]{2,1,0:T(8,128)(2,1)}, u32[]{:S(2)}, u32[]{:S(2)}) collective-permute-start(bf16[2,1024,768]{2,1,0:T(8,128)(2,1)} %refs_10_), channel_id=1, source_target_pairs={{0,1},{1,0},{2,3},{3,2},{4,5},{5,4},{6,7},{7,6},{8,9},{9,8},{10,11... | collective-permute-start | bytes 9437192 | tf_op jit(solution)/shard_map/ppermute | solution.py:419
  0.5 7.1 %collective-permute-start.1 = (bf16[32,1024]{1,0:T(8,128)(2,1)}, bf16[32,1024]{1,0:T(8,128)(2,1)S(1)}, u32[]{:S(2)}, u32[]{:S(2)}) collective-permute-start(bf16[32,1024]{1,0:T(8,128)(2,1)} %refs_2_), channel_id=1, source_target_pairs={{0,1},{1,0},{2,3},{3,2},{4,5},{5,4},{6,7},{7,6},{8,9},{9,8},{10,11... | collective-permute-start | bytes 196616 | tf_op jit(solution)/shard_map/ppermute | solution.py:419
  0.5 7.1 %collective-permute-start.2 = (f32[1,1024]{1,0:T(1,128)}, f32[1,1024]{1,0:T(1,128)S(1)}, u32[]{:S(2)}, u32[]{:S(2)}) collective-permute-start(f32[1,1024]{1,0:T(1,128)} %bitcast.23), channel_id=1, source_target_pairs={{0,1},{1,0},{2,3},{3,2},{4,5},{5,4},{6,7},{7,6},{8,9},{9,8},{10,11... | collective-permute-start | bytes 12296 | tf_op jit(solution)/shard_map/ppermute | solution.py:419
  1.0 8.3 %copy-start = (bf16[1024,1024]{1,0:T(8,128)(2,1)S(1)}, bf16[1024,1024]{1,0:T(8,128)(2,1)}, u32[]{:S(2)}) copy-start(bf16[1024,1024]{1,0:T(8,128)(2,1)} %refs_4_) | copy-start | bytes 6291460
  7.6 1.6 %collective-permute-start.3 = (bf16[4,16,1024]{2,1,0:T(8,128)(2,1)}, bf16[4,16,1024]{2,1,0:T(8,128)(2,1)S(1)}, u32[]{:S(2)}, u32[]{:S(2)}) collective-permute-start(bf16[4,16,1024]{2,1,0:T(8,128)(2,1)} %get-tuple-element.64), channel_id=1, source_target_pairs={{0,1},{1,0},{2,3},{3,2},{4,5},{5,4},{6,7},{7,6},{8,9},{9,8},{10,11... | collective-permute-start | bytes 393224 | tf_op jit(solution)/shard_map/ppermute | solution.py:419
  8.6 31.1 %copy-start.1 = (bf16[32,1024]{1,0:T(8,128)(2,1)S(1)}, bf16[32,1024]{1,0:T(8,128)(2,1)}, u32[]{:S(2)}) copy-start(bf16[32,1024]{1,0:T(8,128)(2,1)} %refs_2_) | copy-start | bytes 196612
  8.7 31.1 %copy-start.2 = (f32[1024]{0:T(1024)S(1)}, f32[1024]{0:T(1024)}, u32[]{:S(2)}) copy-start(f32[1024]{0:T(1024)} %param.22) | copy-start | bytes 12292
  8.7 31.1 %copy-start.3 = (s32[32,8]{0,1:T(8,128)S(1)}, s32[32,8]{0,1:T(8,128)}, u32[]{:S(2)}) copy-start(s32[32,8]{0,1:T(8,128)} %param.23) | copy-start | bytes 3076
  8.7 31.1 %copy-start.4 = (f32[32,8]{0,1:T(8,128)S(1)}, f32[32,8]{0,1:T(8,128)}, u32[]{:S(2)}) copy-start(f32[32,8]{0,1:T(8,128)} %param.24) | copy-start | bytes 3076
  9.3 13.8 %collective-permute-start.8 = (bf16[1024,1024]{1,0:T(8,128)(2,1)S(1)}, bf16[1024,1024]{1,0:T(8,128)(2,1)S(1)}, u32[]{:S(2)}, u32[]{:S(2)}) collective-permute-start(bf16[1024,1024]{1,0:T(8,128)(2,1)S(1)} %copy-done), channel_id=1, source_target_pairs={{0,1},{1,0},{2,3},{3,2},{4,5},{5,4},{6,7},{7,6},{8,9},{9,8},{10,11... | collective-permute-start | bytes 6291464 | tf_op jit(solution)/shard_map/ppermute | solution.py:419
  9.5 8.6 %collective-permute-start.4 = (bf16[32,1024]{1,0:T(8,128)(2,1)S(1)}, bf16[32,1024]{1,0:T(8,128)(2,1)S(1)}, u32[]{:S(2)}, u32[]{:S(2)}) collective-permute-start(bf16[32,1024]{1,0:T(8,128)(2,1)S(1)} %get-tuple-element.69), channel_id=1, source_target_pairs={{0,10},{1,15},{2,8},{3,13},{4,14},{5,11},{6,12},{7,9},{8,2},{9,7},... | collective-permute-start | bytes 196616 | tf_op jit(solution)/shard_map/ppermute | solution.py:431
  14.3 3.8 %collective-permute-start.5 = (bf16[32,1024]{1,0:T(8,128)(2,1)S(1)}, bf16[32,1024]{1,0:T(8,128)(2,1)S(1)}, u32[]{:S(2)}, u32[]{:S(2)}) collective-permute-start(bf16[32,1024]{1,0:T(8,128)(2,1)S(1)} %get-tuple-element.68.own_ref), channel_id=1, source_target_pairs={{1,3},{3,1},{5,7},{7,5},{9,11},{11,9},{13,15},{15,13},{17,19},{19,... | collective-permute-start | bytes 196616 | tf_op jit(solution)/shard_map/ppermute | solution.py:431
  15.0 5.3 %collective-permute-start.6 = (bf16[32,1024]{1,0:T(8,128)(2,1)S(1)}, bf16[32,1024]{1,0:T(8,128)(2,1)S(1)}, u32[]{:S(2)}, u32[]{:S(2)}) collective-permute-start(bf16[32,1024]{1,0:T(8,128)(2,1)S(1)} %get-tuple-element.70), channel_id=1, source_target_pairs={{0,6},{1,9},{2,4},{3,11},{4,2},{5,13},{6,0},{7,15},{8,14},{9,1},{1... | collective-permute-start | bytes 196616 | tf_op jit(solution)/shard_map/ppermute | solution.py:431
  16.5 6.6 %collective-permute-start.7 = (bf16[32,1024]{1,0:T(8,128)(2,1)S(1)}, bf16[32,1024]{1,0:T(8,128)(2,1)S(1)}, u32[]{:S(2)}, u32[]{:S(2)}) collective-permute-start(bf16[32,1024]{1,0:T(8,128)(2,1)S(1)} %get-tuple-element.71), channel_id=1, source_target_pairs={{0,12},{1,5},{2,14},{3,7},{4,8},{5,1},{6,10},{7,3},{8,4},{9,13},{1... | collective-permute-start | bytes 196616 | tf_op jit(solution)/shard_map/ppermute | solution.py:431
  23.1 15.1 %collective-permute-start.13 = (bf16[2,1024,768]{2,1,0:T(8,128)(2,1)}, bf16[2,1024,768]{2,1,0:T(8,128)(2,1)}, u32[]{:S(2)}, u32[]{:S(2)}) collective-permute-start(bf16[2,1024,768]{2,1,0:T(8,128)(2,1)} %refs_12_), channel_id=1, source_target_pairs={{0,1},{1,0},{2,3},{3,2},{4,5},{5,4},{6,7},{7,6},{8,9},{9,8},{10,11... | collective-permute-start | bytes 9437192 | tf_op jit(solution)/shard_map/ppermute | solution.py:419
  23.8 13.0 %collective-permute-start.12 = (bf16[32,2048]{1,0:T(8,128)(2,1)S(1)}, bf16[32,2048]{1,0:T(8,128)(2,1)S(1)}, u32[]{:S(2)}, u32[]{:S(2)}) collective-permute-start(bf16[32,2048]{1,0:T(8,128)(2,1)S(1)} %get-tuple-element.84), channel_id=1, source_target_pairs={{0,10},{1,15},{2,8},{3,13},{4,14},{5,11},{6,12},{7,9},{8,2},{9,7},... | collective-permute-start | bytes 393224 | tf_op jit(solution)/shard_map/ppermute | solution.py:431
  25.4 12.7 %collective-permute-start.10 = (bf16[32,2048]{1,0:T(8,128)(2,1)S(1)}, bf16[32,2048]{1,0:T(8,128)(2,1)S(1)}, u32[]{:S(2)}, u32[]{:S(2)}) collective-permute-start(bf16[32,2048]{1,0:T(8,128)(2,1)S(1)} %get-tuple-element.82), channel_id=1, source_target_pairs={{0,6},{1,9},{2,4},{3,11},{4,2},{5,13},{6,0},{7,15},{8,14},{9,1},{1... | collective-permute-start | bytes 393224 | tf_op jit(solution)/shard_map/ppermute | solution.py:431
  26.8 11.3 %collective-permute-start.9 = (bf16[32,2048]{1,0:T(8,128)(2,1)S(1)}, bf16[32,2048]{1,0:T(8,128)(2,1)S(1)}, u32[]{:S(2)}, u32[]{:S(2)}) collective-permute-start(bf16[32,2048]{1,0:T(8,128)(2,1)S(1)} %get-tuple-element.81), channel_id=1, source_target_pairs={{0,12},{1,5},{2,14},{3,7},{4,8},{5,1},{6,10},{7,3},{8,4},{9,13},{1... | collective-permute-start | bytes 393224 | tf_op jit(solution)/shard_map/ppermute | solution.py:431
  29.2 8.9 %collective-permute-start.11 = (bf16[32,2048]{1,0:T(8,128)(2,1)S(1)}, bf16[32,2048]{1,0:T(8,128)(2,1)S(1)}, u32[]{:S(2)}, u32[]{:S(2)}) collective-permute-start(bf16[32,2048]{1,0:T(8,128)(2,1)S(1)} %get-tuple-element.83), channel_id=1, source_target_pairs={{1,3},{3,1},{5,7},{7,5},{9,11},{11,9},{13,15},{15,13},{17,19},{19,... | collective-permute-start | bytes 393224 | tf_op jit(solution)/shard_map/ppermute | solution.py:431
  38.2 1.6 %collective-permute-start.14 = (f32[32,2048]{1,0:T(8,128)S(1)}, f32[32,2048]{1,0:T(8,128)S(1)}, u32[]{:S(2)}, u32[]{:S(2)}) collective-permute-start(f32[32,2048]{1,0:T(8,128)S(1)} %convert_add_fusion.1.refs_0_), channel_id=1, source_target_pairs={{0,1},{1,0},{2,3},{3,2},{4,5},{5,4},{6,7},{7,6},{8,9},{9,8},{10,11... | collective-permute-start | bytes 786440 | tf_op jit(solution)/shard_map/ppermute | solution.py:419
  40.0 6.2 %collective-permute-start.19 = (bf16[2,768,1024]{2,1,0:T(8,128)(2,1)}, bf16[2,768,1024]{2,1,0:T(8,128)(2,1)S(1)}, u32[]{:S(2)}, u32[]{:S(2)}) collective-permute-start(bf16[2,768,1024]{2,1,0:T(8,128)(2,1)} %refs_14_), channel_id=1, source_target_pairs={{0,1},{1,0},{2,3},{3,2},{4,5},{5,4},{6,7},{7,6},{8,9},{9,8},{10,11... | collective-permute-start | bytes 9437192 | tf_op jit(solution)/shard_map/ppermute | solution.py:419
  40.2 14.2 %collective-permute-start.15 = (bf16[32,2176]{1,0:T(8,128)(2,1)S(1)}, bf16[32,2176]{1,0:T(8,128)(2,1)S(1)}, u32[]{:S(2)}, u32[]{:S(2)}) collective-permute-start(bf16[32,2176]{1,0:T(8,128)(2,1)S(1)} %get-tuple-element.99.own_ref), channel_id=1, source_target_pairs={{0,10},{1,15},{2,8},{3,13},{4,14},{5,11},{6,12},{7,9},{8,2},{9,7},... | collective-permute-start | bytes 417800 | tf_op jit(solution)/shard_map/ppermute | solution.py:431
  41.8 12.5 %collective-permute-start.16 = (bf16[32,2176]{1,0:T(8,128)(2,1)S(1)}, bf16[32,2176]{1,0:T(8,128)(2,1)S(1)}, u32[]{:S(2)}, u32[]{:S(2)}) collective-permute-start(bf16[32,2176]{1,0:T(8,128)(2,1)S(1)} %get-tuple-element.99.own_ref), channel_id=1, source_target_pairs={{1,3},{3,1},{5,7},{7,5},{9,11},{11,9},{13,15},{15,13},{17,19},{19,... | collective-permute-start | bytes 417800 | tf_op jit(solution)/shard_map/ppermute | solution.py:431
  42.5 12.3 %collective-permute-start.17 = (bf16[32,2176]{1,0:T(8,128)(2,1)S(1)}, bf16[32,2176]{1,0:T(8,128)(2,1)S(1)}, u32[]{:S(2)}, u32[]{:S(2)}) collective-permute-start(bf16[32,2176]{1,0:T(8,128)(2,1)S(1)} %get-tuple-element.99.own_ref), channel_id=1, source_target_pairs={{0,6},{1,9},{2,4},{3,11},{4,2},{5,13},{6,0},{7,15},{8,14},{9,1},{1... | collective-permute-start | bytes 417800 | tf_op jit(solution)/shard_map/ppermute | solution.py:431
  43.6 11.2 %collective-permute-start.18 = (bf16[32,2176]{1,0:T(8,128)(2,1)S(1)}, bf16[32,2176]{1,0:T(8,128)(2,1)S(1)}, u32[]{:S(2)}, u32[]{:S(2)}) collective-permute-start(bf16[32,2176]{1,0:T(8,128)(2,1)S(1)} %get-tuple-element.99.own_ref), channel_id=1, source_target_pairs={{0,12},{1,5},{2,14},{3,7},{4,8},{5,1},{6,10},{7,3},{8,4},{9,13},{1... | collective-permute-start | bytes 417800 | tf_op jit(solution)/shard_map/ppermute | solution.py:431
  46.2 1.7 %copy-start.5 = (bf16[2,768,1024]{2,1,0:T(8,128)(2,1)}, bf16[2,768,1024]{2,1,0:T(8,128)(2,1)S(1)}, u32[]{:S(2)}) copy-start(bf16[2,768,1024]{2,1,0:T(8,128)(2,1)S(1)} %collective-permute-done.19.refs_5_.refs_15_) | copy-start | bytes 9437188
  60.5 12.7 %collective-permute-start.23 = (bf16[32,2048]{1,0:T(8,128)(2,1)S(1)}, bf16[32,2048]{1,0:T(8,128)(2,1)S(1)}, u32[]{:S(2)}, u32[]{:S(2)}) collective-permute-start(bf16[32,2048]{1,0:T(8,128)(2,1)S(1)} %get-tuple-element.114), channel_id=1, source_target_pairs={{0,10},{1,15},{2,8},{3,13},{4,14},{5,11},{6,12},{7,9},{8,2},{9,7},... | collective-permute-start | bytes 393224 | tf_op jit(solution)/shard_map/ppermute | solution.py:431
  63.3 9.9 %collective-permute-start.21 = (bf16[32,2048]{1,0:T(8,128)(2,1)S(1)}, bf16[32,2048]{1,0:T(8,128)(2,1)S(1)}, u32[]{:S(2)}, u32[]{:S(2)}) collective-permute-start(bf16[32,2048]{1,0:T(8,128)(2,1)S(1)} %get-tuple-element.112), channel_id=1, source_target_pairs={{0,6},{1,9},{2,4},{3,11},{4,2},{5,13},{6,0},{7,15},{8,14},{9,1},{1... | collective-permute-start | bytes 393224 | tf_op jit(solution)/shard_map/ppermute | solution.py:431
  63.3 10.6 %collective-permute-start.20 = (bf16[32,2048]{1,0:T(8,128)(2,1)S(1)}, bf16[32,2048]{1,0:T(8,128)(2,1)S(1)}, u32[]{:S(2)}, u32[]{:S(2)}) collective-permute-start(bf16[32,2048]{1,0:T(8,128)(2,1)S(1)} %get-tuple-element.111), channel_id=1, source_target_pairs={{0,12},{1,5},{2,14},{3,7},{4,8},{5,1},{6,10},{7,3},{8,4},{9,13},{1... | collective-permute-start | bytes 393224 | tf_op jit(solution)/shard_map/ppermute | solution.py:431
  65.8 8.1 %collective-permute-start.22 = (bf16[32,2048]{1,0:T(8,128)(2,1)S(1)}, bf16[32,2048]{1,0:T(8,128)(2,1)S(1)}, u32[]{:S(2)}, u32[]{:S(2)}) collective-permute-start(bf16[32,2048]{1,0:T(8,128)(2,1)S(1)} %get-tuple-element.113), channel_id=1, source_target_pairs={{1,3},{3,1},{5,7},{7,5},{9,11},{11,9},{13,15},{15,13},{17,19},{19,... | collective-permute-start | bytes 393224 | tf_op jit(solution)/shard_map/ppermute | solution.py:431
  74.0 1.4 %collective-permute-start.24 = (f32[32,1024]{1,0:T(8,128)S(1)}, f32[32,1024]{1,0:T(8,128)S(1)}, u32[]{:S(2)}, u32[]{:S(2)}) collective-permute-start(f32[32,1024]{1,0:T(8,128)S(1)} %slice.61), channel_id=1, source_target_pairs={{0,1},{1,0},{2,3},{3,2},{4,5},{5,4},{6,7},{7,6},{8,9},{9,8},{10,11... | collective-permute-start | bytes 393224 | tf_op jit(solution)/shard_map/ppermute | solution.py:419
